TPU v7x, 512 devices: a whole 4x8x8 slice. The times are simulated.
512 devices in a mesh: row: 32 (over x_hi, z, core), col: 16 (over y, x_lo).
Axes of the slice: x: 4 (x_hi: 2, x_lo: 2; x = x_hi * 2 + x_lo), y: 8, z: 8, core: 2. Of those that a mesh axis runs over, the one named last changes fastest.
Arguments:
- tensor: float32 [8, 4096, 4096], P(None, 'row', 'col'), may hold values from -6 to 6
- factor_a: float32 [32, 4096], P(None, 'row'), as said below
- factor_b: float32 [32, 4096], P(None, 'col'), as said below
- factor_c: float32 [32, 8], replicated, may hold values from -2.5 to 2.5
Outputs:
- new_a: float32 [32, 4096], P(None, 'row')
- new_b: float32 [32, 4096], P(None, 'col')
- new_c: float32 [32, 8], replicated
Inputs may be any that keep to these rules, and one draw needn't show every extreme that they name: factor_a's scale differs from index to index. factor_b's scale differs from index to index.
All inputs are finite; a program needn't handle non-finite values.
Results may differ from a plain program's by a relative error of at most 0.0003.
Values sent between devices are 32-bit elements; how exact they have to be, the bound alone decides.
No kernel may reach another device: no remote copies, remote signals or barrier semaphores. Data moves between devices by JAX's collectives and lax.ppermute only.
A program may use at most 64 MiB of HBM per device.

v0:
```python
import jax
import jax.numpy as jnp
from jax import lax
from jax.sharding import PartitionSpec as P

ITERS = 6


HP = lax.Precision.HIGHEST


def gram(factor):
    return jnp.dot(factor, factor.T, precision=HP)


def inverse_norm(matrix):
    return 1.0 / jnp.sqrt(jnp.sum(matrix * matrix) + 1e-06)


def descend(factor, hessian, contraction):
    return factor - inverse_norm(hessian) * (jnp.dot(hessian, factor, precision=HP) - contraction)


def shards(tensor, factor_a, factor_b, factor_c):
    fa, fb, fc = (factor_a, factor_b, factor_c)
    for step in range(ITERS):
        gram_c = gram(fc)
        gram_a = lax.psum(gram(fa), "row")
        gram_b = lax.psum(gram(fb), "col")
        part_y = jnp.einsum("kij,rj->kri", tensor, fb, precision=HP)
        part_a = jnp.einsum("rk,kri->ri", fc, part_y, precision=HP)
        part_c = jnp.einsum("kri,ri->rk", part_y, fa, precision=HP)
        part_z = jnp.einsum("kij,ri->krj", tensor, fa, precision=HP)
        part_b = jnp.einsum("rk,krj->rj", fc, part_z, precision=HP)
        mode_c = lax.psum(part_c, ("row", "col"))
        h_a, h_b, h_c = (gram_b * gram_c, gram_a * gram_c, gram_a * gram_b)
        mode_a = lax.psum(part_a, "col")
        mode_b = lax.psum(part_b, "row")
        next_a = descend(fa, h_a, mode_a)
        next_b = descend(fb, h_b, mode_b)
        next_c = descend(fc, h_c, mode_c)
        fa, fb, fc = (next_a, next_b, next_c)
    return (fa, fb, fc)


def solution(mesh):
    in_specs = (P(None, "row", "col"), P(None, "row"), P(None, "col"), P())
    out_specs = (P(None, "row"), P(None, "col"), P())
    return jax.shard_map(shards, mesh=mesh, in_specs=in_specs, out_specs=out_specs, check_vma=False)
```

profile of v0, /device:TPU:1, one launch (start us, length us, event | category | flops | bytes accessed | tf_op | source)
XLA Modules:
  0.0 1598.6 jit_solution(16463000123059033197)
XLA Ops:
  7.2 1.0 fusion.114
  8.3 0.2 copy-done
  8.4 1.0 convolution_bitcast_fusion.5
  9.7 0.7 fusion.94
  10.4 134.9 %psum.212 = f32[32,32]{1,0:T(8,128)S(1)} all-reduce(f32[32,32]{1,0:T(8,128)S(1)} %fusion.115), channel_id=1, replica_groups=mesh['row'=32,'col'=16] {'row'}, use_global_device_ids=true, to_apply=%region_3.0 | all-reduce | flops 1024 | bytes 8192 | tf_op jit(solution)/shard_map/psum | solution.py:28
  145.3 0.4 fusion.76
  145.7 49.3 %all-reduce.13 = (f32[32,128]{1,0:T(8,128)S(1)}, f32[32,32]{1,0:T(8,128)S(1)}) all-reduce(f32[32,128]{1,0:T(8,128)S(1)} %bitcast.226, f32[32,32]{1,0:T(8,128)S(1)} %fusion.114), channel_id=1, replica_groups=mesh['row'=32,'col'=16] {'col'}, use_global_device_ids=true, to_apply=%region_2.0 | all-reduce | flops 5120 | bytes 40960 | tf_op jit(solution)/shard_map/psum | solution.py:37
  195.1 0.8 multiply_reduce_fusion.16
  196.6 0.5 fusion.46
  198.1 142.4 %all-reduce.7 = (f32[32,256]{1,0:T(8,128)S(1)}, f32[32,32]{1,0:T(8,128)S(1)}) all-reduce(f32[32,256]{1,0:T(8,128)S(1)} %bitcast.213, f32[32,32]{1,0:T(8,128)S(1)} %fusion.117), channel_id=1, replica_groups=mesh['row'=32,'col'=16] {'row'}, use_global_device_ids=true, to_apply=%region_5.0 | all-reduce | flops 9216 | bytes 73728 | tf_op jit(solution)/shard_map/psum | solution.py:38
  340.7 1.0 convolution_bitcast_fusion.4
  341.7 0.2 fusion.116
  341.9 0.6 fusion.92
  342.5 0.4 fusion.74
  343.0 0.4 fusion.70
  344.2 97.6 %all-reduce.2 = (f32[32,8]{0,1:T(8,128)S(1)}, f32[32,8]{0,1:T(8,128)S(1)}) all-reduce(f32[32,8]{0,1:T(8,128)S(1)} %bitcast.228, f32[32,8]{0,1:T(8,128)S(1)} %bitcast.231), channel_id=1, replica_groups=mesh['row'=32,'col'=16] {'row','col'}, use_global_device_ids=true, to_apply=%region_8.0 | all-reduce | flops 512 | bytes 4096 | tf_op jit(solution)/shard_map/psum | solution.py:35
  442.0 0.4 fusion.72
  442.4 50.2 %all-reduce.12 = (f32[32,128]{1,0:T(8,128)S(1)}, f32[32,32]{1,0:T(8,128)S(1)}) all-reduce(f32[32,128]{1,0:T(8,128)S(1)} %bitcast.223, f32[32,32]{1,0:T(8,128)S(1)} %fusion.116), channel_id=1, replica_groups=mesh['row'=32,'col'=16] {'col'}, use_global_device_ids=true, to_apply=%region_10.0 | all-reduce | flops 5120 | bytes 40960 | tf_op jit(solution)/shard_map/psum | solution.py:37
  492.6 0.8 multiply_reduce_fusion.13
  494.1 0.5 fusion.44
  495.6 137.1 %all-reduce.6 = (f32[32,256]{1,0:T(8,128)S(1)}, f32[32,32]{1,0:T(8,128)S(1)}) all-reduce(f32[32,256]{1,0:T(8,128)S(1)} %bitcast.212, f32[32,32]{1,0:T(8,128)S(1)} %fusion.119), channel_id=1, replica_groups=mesh['row'=32,'col'=16] {'row'}, use_global_device_ids=true, to_apply=%region_13.0 | all-reduce | flops 9216 | bytes 73728 | tf_op jit(solution)/shard_map/psum | solution.py:38
  632.9 1.0 convolution_bitcast_fusion.3
  633.9 0.2 fusion.118
  634.1 0.6 fusion.90
  635.7 0.4 fusion.68
  636.1 46.1 %all-reduce.11 = (f32[32,128]{1,0:T(8,128)S(1)}, f32[32,32]{1,0:T(8,128)S(1)}) all-reduce(f32[32,128]{1,0:T(8,128)S(1)} %bitcast.227, f32[32,32]{1,0:T(8,128)S(1)} %fusion.118), channel_id=1, replica_groups=mesh['row'=32,'col'=16] {'col'}, use_global_device_ids=true, to_apply=%region_18.0 | all-reduce | flops 5120 | bytes 40960 | tf_op jit(solution)/shard_map/psum | solution.py:37
  682.3 0.8 multiply_reduce_fusion.10
  683.8 0.5 fusion.42
  685.3 142.4 %all-reduce.5 = (f32[32,256]{1,0:T(8,128)S(1)}, f32[32,32]{1,0:T(8,128)S(1)}) all-reduce(f32[32,256]{1,0:T(8,128)S(1)} %bitcast.214, f32[32,32]{1,0:T(8,128)S(1)} %fusion.121), channel_id=1, replica_groups=mesh['row'=32,'col'=16] {'row'}, use_global_device_ids=true, to_apply=%region_21.0 | all-reduce | flops 9216 | bytes 73728 | tf_op jit(solution)/shard_map/psum | solution.py:38
  827.8 1.0 convolution_bitcast_fusion.2
  828.9 0.2 fusion.120
  829.1 0.7 fusion.88
  829.7 0.4 fusion.66
  830.2 0.4 fusion.62
  831.4 97.6 %all-reduce.1 = (f32[32,8]{0,1:T(8,128)S(1)}, f32[32,8]{0,1:T(8,128)S(1)}) all-reduce(f32[32,8]{0,1:T(8,128)S(1)} %bitcast.229, f32[32,8]{0,1:T(8,128)S(1)} %bitcast.232), channel_id=1, replica_groups=mesh['row'=32,'col'=16] {'row','col'}, use_global_device_ids=true, to_apply=%region_24.0 | all-reduce | flops 512 | bytes 4096 | tf_op jit(solution)/shard_map/psum | solution.py:35
  929.1 0.4 fusion.64
  929.6 50.2 %all-reduce.10 = (f32[32,128]{1,0:T(8,128)S(1)}, f32[32,32]{1,0:T(8,128)S(1)}) all-reduce(f32[32,128]{1,0:T(8,128)S(1)} %bitcast.224, f32[32,32]{1,0:T(8,128)S(1)} %fusion.120), channel_id=1, replica_groups=mesh['row'=32,'col'=16] {'col'}, use_global_device_ids=true, to_apply=%region_26.0 | all-reduce | flops 5120 | bytes 40960 | tf_op jit(solution)/shard_map/psum | solution.py:37
  979.8 0.8 multiply_reduce_fusion.7
  981.5 0.8 fusion.123
  982.2 0.6 fusion.86
  983.8 0.5 fusion.40
  984.3 0.6 copy.105
  984.9 0.5 fusion.38
  985.4 0.6 copy.104
  986.7 246.1 %all-reduce.16.cloned.1.call-done = (f32[32,256]{1,0:T(8,128)}, f32[32,32]{1,0:T(8,128)}, f32[32,256]{1,0:T(8,128)}) async-done(((f32[32,256]{1,0:T(8,128)}, f32[32,32]{1,0:T(8,128)}, f32[32,256]{1,0:T(8,128)}), (f32[32,256]{1,0:T(8,128)}, f32[32,32]{1,0:T(8,128)}, f32[32,256]{1,0:T(8,128)})) %all-reduce.16.cloned.1.call-update) | async-done | bytes 69648 | tf_op jit(solution)/shard_map/psum | solution.py:38
  1232.8 0.9 fusion.5
  1233.7 1.0 convolution_bitcast_fusion.1
  1234.8 0.2 fusion.122
  1234.9 0.4 fusion.60
  1235.4 48.7 %all-reduce.9 = (f32[32,128]{1,0:T(8,128)S(1)}, f32[32,32]{1,0:T(8,128)S(1)}) all-reduce(f32[32,128]{1,0:T(8,128)S(1)} %bitcast.225, f32[32,32]{1,0:T(8,128)S(1)} %fusion.122), channel_id=1, replica_groups=mesh['row'=32,'col'=16] {'col'}, use_global_device_ids=true, to_apply=%region_34.0 | all-reduce | flops 5120 | bytes 40960 | tf_op jit(solution)/shard_map/psum | solution.py:37
  1284.1 0.8 multiply_reduce_fusion.4
  1285.8 1.0 convolution_bitcast_fusion
  1288.0 0.7 fusion.84
  1288.7 0.4 fusion.58
  1289.1 0.4 fusion.54
  1290.3 107.8 %all-reduce = (f32[32,8]{0,1:T(8,128)S(1)}, f32[32,8]{0,1:T(8,128)S(1)}) all-reduce(f32[32,8]{0,1:T(8,128)S(1)} %bitcast.230, f32[32,8]{0,1:T(8,128)S(1)} %bitcast.233), channel_id=1, replica_groups=mesh['row'=32,'col'=16] {'row','col'}, use_global_device_ids=true, to_apply=%region_40.0 | all-reduce | flops 512 | bytes 4096 | tf_op jit(solution)/shard_map/psum | solution.py:35
  1398.3 0.4 fusion.56
  1398.8 0.5 fusion.36
  1399.3 50.2 %all-reduce.8 = (f32[32,128]{1,0:T(8,128)S(1)}, f32[32,32]{1,0:T(8,128)S(1)}) all-reduce(f32[32,128]{1,0:T(8,128)S(1)} %bitcast.222, f32[32,32]{1,0:T(8,128)S(1)} %fusion.124), channel_id=1, replica_groups=mesh['row'=32,'col'=16] {'col'}, use_global_device_ids=true, to_apply=%region_42.0 | all-reduce | flops 5120 | bytes 40960 | tf_op jit(solution)/shard_map/psum | solution.py:37
  1449.5 137.1 %all-reduce.3 = (f32[32,32]{1,0:T(8,128)S(1)}, f32[32,256]{1,0:T(8,128)S(1)}) all-reduce(f32[32,32]{1,0:T(8,128)S(1)} %fusion.125, f32[32,256]{1,0:T(8,128)S(1)} %bitcast.215), channel_id=1, replica_groups=mesh['row'=32,'col'=16] {'row'}, use_global_device_ids=true, to_apply=%region_43.0 | all-reduce | flops 9216 | bytes 73728 | tf_op jit(solution)/shard_map/psum | solution.py:28
  1586.6 0.8 multiply_reduce_fusion
  1589.4 0.8 fusion.13
  1590.2 0.8 fusion.1
  1591.0 0.7 fusion.25
  (49 shorter events, 3.9 us)
Async XLA Ops:
  7.2 1.3 copy-start
  7.2 1.2 copy-start.1
  7.2 1225.6 %all-reduce.16.cloned.1.call-start = ((), (), s32[]{:S(2)}) async-start(), calls=%async_computation | async-start | bytes 163840 | tf_op jit(solution)/shard_map/psum | solution.py:38
  8.4 1.1 copy-start.2
  9.6 0.7 copy-start.4
  1235.4 48.7 %copy-start.3 = (f32[32,32]{1,0:T(8,128)S(1)}, f32[32,32]{1,0:T(8,128)}, u32[]{:S(2)}) copy-start(f32[32,32]{1,0:T(8,128)} %get-tuple-element.30) | copy-start | bytes 12292
  1284.1 1.5 copy-start.5
Sparse Core Ops, SparseCore 0:
  986.2 246.5 all-reduce.15
where the time goes:
time: 1600 us
  blocking collectives  1290 us (81%)
  waiting for transfers between devices  246 us (15%)
  matrix products  31.5 us (2%)
  between operations  27 us (2%)
    psum x3, blocking collectives, shards(): mode_b = lax.psum(part_b, 'row')  422 us
    psum x3, blocking collectives, shards(): mode_c = lax.psum(part_c, ('row', 'col'))  303 us
    psum x6, blocking collectives, shards(): mode_a = lax.psum(part_a, 'col')  295 us
    psum x2, blocking collectives, shards(): gram_a = lax.psum(gram(fa), 'row')  272 us
    psum x1, waiting for transfers between devices, shards(): mode_b = lax.psum(part_b, 'row')  246 us
  transfers between devices with their start and end apart: 1, of which 1 were waited for; matrix products, arithmetic and copies ran while one was open for 0% of the time, Pallas kernels for 0%

commit v1 on v0

v1 whole, which is shorter than its diff:
```python
import jax
import jax.numpy as jnp
from jax import lax
from jax.sharding import Mesh, PartitionSpec as P

ITERS = 6

HP = lax.Precision.HIGHEST


def gram(factor):
    return jnp.dot(factor, factor.T, precision=HP)


def pack(square):
    n = square.shape[1]
    rows = square.reshape(4, 8, n).transpose(1, 0, 2).reshape(8, 4 * n)
    return jnp.pad(rows, ((0, 0), (0, 128 - 4 * n)))


def unpack(rows, n):
    return rows[:, : 4 * n].reshape(8, 4, n).transpose(1, 0, 2).reshape(32, n)


def inverse_norm(matrix):
    return 1.0 / jnp.sqrt(jnp.sum(matrix * matrix) + 1e-06)


def descend(factor, hessian, contraction):
    return factor - inverse_norm(hessian) * (jnp.dot(hessian, factor, precision=HP) - contraction)


def sum_over(block, axis, size):
    copies = jnp.broadcast_to(block[None], (size,) + block.shape)
    return lax.all_to_all(copies, axis, 0, 0).sum(0)


def shards(tensor, factor_a, factor_b, factor_c):
    fa, fb, fc = (factor_a, factor_b, factor_c)
    x_lo = lax.axis_index("x_lo")
    chip = lax.axis_index("x_hi") * 2 + lax.axis_index("core")
    for step in range(ITERS):
        gram_c = gram(fc)
        part_y = jnp.einsum("kij,rj->kri", tensor, fb, precision=HP)
        part_z = jnp.einsum("kij,ri->krj", tensor, fa, precision=HP)
        part_a = jnp.einsum("rk,kri->ri", fc, part_y, precision=HP)
        part_c = jnp.einsum("kri,ri->rk", part_y, fa, precision=HP)
        part_b = jnp.einsum("rk,krj->rj", fc, part_z, precision=HP)
        for_row = jnp.concatenate([part_b[:, :128], part_b[:, 128:], pack(gram(fa))], 0)
        for_col = jnp.concatenate([part_a, pack(gram(fb)), jnp.zeros((32, 128), jnp.float32)], 0)
        same = jnp.arange(2)[:, None, None] == x_lo
        pair = jnp.where(same, for_row[None], for_col[None])
        pair = jnp.concatenate([pair, jnp.broadcast_to(pack(part_c)[None], (2, 8, 128))], 1)
        sent = jnp.broadcast_to(pair[:, None], (2, 4, 80, 128)).reshape(8, 80, 128)
        got = lax.all_to_all(sent, ("x_lo", "x_hi", "core"), 0, 0)
        sum_c = got[:, 72:].sum(0)
        got = got.reshape(2, 4, 80, 128)
        sum_row = lax.dynamic_index_in_dim(got, x_lo, 0, False)[:, :72].sum(0)
        other = lax.dynamic_index_in_dim(got, 1 - x_lo, 0, False)
        sum_col = for_col[:40] + lax.dynamic_index_in_dim(other, chip, 0, False)[:40]
        sum_row = sum_over(jnp.concatenate([sum_row, sum_c], 0), "z", 8)
        sum_col = sum_over(jnp.concatenate([sum_col, sum_row[72:]], 0), "y", 8)
        mode_b = jnp.concatenate([sum_row[:32], sum_row[32:64]], 1)
        gram_a = unpack(sum_row[64:72], 32)
        mode_a = sum_col[:32]
        gram_b = unpack(sum_col[32:40], 32)
        mode_c = unpack(sum_col[40:48], 8)
        next_a = descend(fa, gram_b * gram_c, mode_a)
        next_b = descend(fb, gram_a * gram_c, mode_b)
        next_c = descend(fc, gram_a * gram_b, mode_c)
        fa, fb, fc = (next_a, next_b, next_c)
    return (fa, fb, fc)


def solution(mesh):
    rows, cols = mesh.devices.shape
    devices = mesh.devices.reshape(2, rows // 4, 2, cols // 2, 2)
    fine = Mesh(devices, ("x_hi", "z", "core", "y", "x_lo"))
    row, col = (("x_hi", "z", "core"), ("y", "x_lo"))
    in_specs = (P(None, row, col), P(None, row), P(None, col), P())
    out_specs = (P(None, row), P(None, col), P())
    return jax.shard_map(shards, mesh=fine, in_specs=in_specs, out_specs=out_specs, check_vma=False)
```

time: 1600 us -> 324 us (0.20)
  blocking collectives: 1290 us -> 64.6 us
  waiting for transfers between devices: 246 us -> 133 us
  starting transfers between devices: 0.04 us -> 56.9 us
    psum x14 -> x0, blocking collectives: 1290 us -> none  [the longest x3 422 us: shards(): mode_b = lax.psum(part_b, 'row')]
    psum x1 -> x0, waiting for transfers between devices: 246 us -> none  [shards(): mode_b = lax.psum(part_b, 'row')]
    all_to_all x0 -> x13, waiting for transfers between devices: none -> 133 us  [the longest x12 126 us: sum_over(): return lax.all_to_all(copies, axis, 0, 0).sum(0)]
    all_to_all x0 -> x5, blocking collectives: none -> 64.6 us  [shards(): got = lax.all_to_all(sent, ('x_lo', 'x_hi', 'core'), 0, 0)]
    all_to_all x0 -> x13, starting transfers between devices: none -> 56.9 us  [the longest x12 46.7 us: sum_over(): return lax.all_to_all(copies, axis, 0, 0).sum(0)]
  transfers between devices with their start and end apart: 1 -> 13, of which waited for: 1 -> 13; matrix products, arithmetic and copies ran while one was open for 0% -> 0% of each run, Pallas kernels for 0% -> 0%
where the time goes in v1:
time: 324 us; the launch traced here: 321 us
  waiting for transfers between devices  133 us (41%)
  blocking collectives  64.6 us (20%)
  starting transfers between devices  56.9 us (18%)
  matrix products  30.2 us (9%)
  local copies, waits for them, and re-layouts  16.8 us (5%)
  between operations  14.4 us (4%)
  other arithmetic  5.14 us (2%)
    all_to_all x12, waiting for transfers between devices, sum_over(): return lax.all_to_all(copies, axis, 0, 0).sum(0)  126 us
    all_to_all x5, blocking collectives, shards(): got = lax.all_to_all(sent, ('x_lo', 'x_hi', 'core'), 0, 0)  64.6 us
    all_to_all x12, starting transfers between devices, sum_over(): return lax.all_to_all(copies, axis, 0, 0).sum(0)  46.7 us
    all_to_all x1, starting transfers between devices, shards(): got = lax.all_to_all(sent, ('x_lo', 'x_hi', 'core'), 0, 0)  10.2 us
    broadcast_in_dim x12, local copies, waits for them, and re-layouts, sum_over(): copies = jnp.broadcast_to(block[None], (size,) + block.shape)  8.5 us
    dot_general x18, matrix products, gram(): return jnp.dot(factor, factor.T, precision=HP)  7.63 us
    all_to_all x1, waiting for transfers between devices, shards(): got = lax.all_to_all(sent, ('x_lo', 'x_hi', 'core'), 0, 0)  7.11 us
  transfers between devices with their start and end apart: 13, of which 13 were waited for; matrix products, arithmetic and copies ran while one was open for 0% of the time, Pallas kernels for 0%

profile of v1, /device:TPU:1, one launch (start us, length us, event | category | flops | bytes accessed | tf_op | source)
XLA Modules:
  0.0 321.5 jit_solution(554407033637625763)
XLA Ops:
  0.7 1.0 convolution_bitcast_fusion.23
  2.5 1.0 convolution_bitcast_fusion.11
  4.3 0.7 copy-done.3
  7.1 0.7 broadcast_in_dim.255
  7.9 10.2 %all-to-all-start = ((f32[8,80,128]{2,1,0:T(8,128)}), f32[8,80,128]{2,1,0:T(8,128)S(1)}, u32[]{:S(2)}, u32[]{:S(2)}) async-start(f32[8,80,128]{2,1,0:T(8,128)} %bitcast.15), calls=%async_computation | async-start | bytes 655360 | tf_op jit(solution)/shard_map/all_to_all | solution.py:55
  18.1 7.1 %all-to-all-done = f32[8,80,128]{2,1,0:T(8,128)S(1)} async-done(((f32[8,80,128]{2,1,0:T(8,128)}), f32[8,80,128]{2,1,0:T(8,128)S(1)}, u32[]{:S(2)}, u32[]{:S(2)}) %all-to-all-start) | async-done | bytes 327712 | tf_op jit(solution)/shard_map/all_to_all | solution.py:55
  25.2 0.7 broadcast_in_dim.256
  26.0 5.6 %all-to-all-start.1 = ((f32[8,80,128]{2,1,0:T(8,128)}), f32[8,80,128]{2,1,0:T(8,128)S(1)}, u32[]{:S(2)}, u32[]{:S(2)}) async-start(f32[8,80,128]{2,1,0:T(8,128)} %broadcast_in_dim.256), calls=%async_computation.1 | async-start | bytes 655360 | tf_op jit(solution)/shard_map/all_to_all | solution.py:35
  31.6 11.6 %all-to-all-done.1 = f32[8,80,128]{2,1,0:T(8,128)S(1)} async-done(((f32[8,80,128]{2,1,0:T(8,128)}), f32[8,80,128]{2,1,0:T(8,128)S(1)}, u32[]{:S(2)}, u32[]{:S(2)}) %all-to-all-start.1) | async-done | bytes 327712 | tf_op jit(solution)/shard_map/all_to_all | solution.py:35
  43.2 0.7 broadcast_in_dim.257
  43.9 6.8 %all-to-all-start.2 = ((f32[8,48,128]{2,1,0:T(8,128)}), f32[8,48,128]{2,1,0:T(8,128)S(1)}, u32[]{:S(2)}, u32[]{:S(2)}) async-start(f32[8,48,128]{2,1,0:T(8,128)} %broadcast_in_dim.257), calls=%async_computation.2 | async-start | bytes 393216 | tf_op jit(solution)/shard_map/all_to_all | solution.py:35
  50.8 8.6 %all-to-all-done.2 = f32[8,48,128]{2,1,0:T(8,128)S(1)} async-done(((f32[8,48,128]{2,1,0:T(8,128)}), f32[8,48,128]{2,1,0:T(8,128)S(1)}, u32[]{:S(2)}, u32[]{:S(2)}) %all-to-all-start.2) | async-done | bytes 196640 | tf_op jit(solution)/shard_map/all_to_all | solution.py:35
  60.2 0.8 multiply_reduce_fusion.10
  62.0 1.0 convolution_bitcast_fusion.10
  64.1 0.7 convolution_bitcast_fusion.4
  68.0 13.7 %all_to_all.90 = f32[8,80,128]{2,1,0:T(8,128)S(1)} all-to-all(f32[8,80,128]{2,1,0:T(8,128)S(1)} %bitcast.498), channel_id=1, replica_groups=mesh['x_hi'=2,'z'=8,'core'=2,'y'=8,'x_lo'=2] {'x_lo','x_hi','core'}, dimensions={0} | all-to-all | bytes 655360 | tf_op jit(solution)/shard_map/all_to_all | solution.py:55
  81.7 0.7 broadcast_in_dim.262
  82.5 3.4 %all-to-all-start.4 = ((f32[8,80,128]{2,1,0:T(8,128)}), f32[8,80,128]{2,1,0:T(8,128)S(1)}, u32[]{:S(2)}, u32[]{:S(2)}) async-start(f32[8,80,128]{2,1,0:T(8,128)} %broadcast_in_dim.262), calls=%async_computation.4 | async-start | bytes 655360 | tf_op jit(solution)/shard_map/all_to_all | solution.py:35
  85.9 12.9 %all-to-all-done.4 = f32[8,80,128]{2,1,0:T(8,128)S(1)} async-done(((f32[8,80,128]{2,1,0:T(8,128)}), f32[8,80,128]{2,1,0:T(8,128)S(1)}, u32[]{:S(2)}, u32[]{:S(2)}) %all-to-all-start.4) | async-done | bytes 327712 | tf_op jit(solution)/shard_map/all_to_all | solution.py:35
  98.9 0.7 broadcast_in_dim.263
  99.6 3.4 %all-to-all-start.5 = ((f32[8,48,128]{2,1,0:T(8,128)}), f32[8,48,128]{2,1,0:T(8,128)S(1)}, u32[]{:S(2)}, u32[]{:S(2)}) async-start(f32[8,48,128]{2,1,0:T(8,128)} %broadcast_in_dim.263), calls=%async_computation.5 | async-start | bytes 393216 | tf_op jit(solution)/shard_map/all_to_all | solution.py:35
  103.0 8.3 %all-to-all-done.5 = f32[8,48,128]{2,1,0:T(8,128)S(1)} async-done(((f32[8,48,128]{2,1,0:T(8,128)}), f32[8,48,128]{2,1,0:T(8,128)S(1)}, u32[]{:S(2)}, u32[]{:S(2)}) %all-to-all-start.5) | async-done | bytes 196640 | tf_op jit(solution)/shard_map/all_to_all | solution.py:35
  112.1 0.8 multiply_reduce_fusion.8
  114.0 1.0 convolution_bitcast_fusion.9
  116.0 0.7 convolution_bitcast_fusion.3
  119.9 12.7 %all_to_all.91 = f32[8,80,128]{2,1,0:T(8,128)S(1)} all-to-all(f32[8,80,128]{2,1,0:T(8,128)S(1)} %bitcast.499), channel_id=1, replica_groups=mesh['x_hi'=2,'z'=8,'core'=2,'y'=8,'x_lo'=2] {'x_lo','x_hi','core'}, dimensions={0} | all-to-all | bytes 655360 | tf_op jit(solution)/shard_map/all_to_all | solution.py:55
  132.7 0.7 broadcast_in_dim.268
  133.5 3.4 %all-to-all-start.7 = ((f32[8,80,128]{2,1,0:T(8,128)}), f32[8,80,128]{2,1,0:T(8,128)S(1)}, u32[]{:S(2)}, u32[]{:S(2)}) async-start(f32[8,80,128]{2,1,0:T(8,128)} %broadcast_in_dim.268), calls=%async_computation.7 | async-start | bytes 655360 | tf_op jit(solution)/shard_map/all_to_all | solution.py:35
  136.9 12.9 %all-to-all-done.7 = f32[8,80,128]{2,1,0:T(8,128)S(1)} async-done(((f32[8,80,128]{2,1,0:T(8,128)}), f32[8,80,128]{2,1,0:T(8,128)S(1)}, u32[]{:S(2)}, u32[]{:S(2)}) %all-to-all-start.7) | async-done | bytes 327712 | tf_op jit(solution)/shard_map/all_to_all | solution.py:35
  149.9 0.7 broadcast_in_dim.269
  150.5 3.6 %all-to-all-start.8 = ((f32[8,48,128]{2,1,0:T(8,128)}), f32[8,48,128]{2,1,0:T(8,128)S(1)}, u32[]{:S(2)}, u32[]{:S(2)}) async-start(f32[8,48,128]{2,1,0:T(8,128)} %broadcast_in_dim.269), calls=%async_computation.8 | async-start | bytes 393216 | tf_op jit(solution)/shard_map/all_to_all | solution.py:35
  154.2 8.3 %all-to-all-done.8 = f32[8,48,128]{2,1,0:T(8,128)S(1)} async-done(((f32[8,48,128]{2,1,0:T(8,128)}), f32[8,48,128]{2,1,0:T(8,128)S(1)}, u32[]{:S(2)}, u32[]{:S(2)}) %all-to-all-start.8) | async-done | bytes 196640 | tf_op jit(solution)/shard_map/all_to_all | solution.py:35
  163.2 0.8 multiply_reduce_fusion.6
  165.1 1.0 convolution_bitcast_fusion.8
  171.0 12.6 %all_to_all.92 = f32[8,80,128]{2,1,0:T(8,128)S(1)} all-to-all(f32[8,80,128]{2,1,0:T(8,128)S(1)} %bitcast.500), channel_id=1, replica_groups=mesh['x_hi'=2,'z'=8,'core'=2,'y'=8,'x_lo'=2] {'x_lo','x_hi','core'}, dimensions={0} | all-to-all | bytes 655360 | tf_op jit(solution)/shard_map/all_to_all | solution.py:55
  183.7 0.7 broadcast_in_dim.274
  184.5 3.4 %all-to-all-start.10 = ((f32[8,80,128]{2,1,0:T(8,128)}), f32[8,80,128]{2,1,0:T(8,128)S(1)}, u32[]{:S(2)}, u32[]{:S(2)}) async-start(f32[8,80,128]{2,1,0:T(8,128)} %broadcast_in_dim.274), calls=%async_computation.10 | async-start | bytes 655360 | tf_op jit(solution)/shard_map/all_to_all | solution.py:35
  187.9 12.9 %all-to-all-done.10 = f32[8,80,128]{2,1,0:T(8,128)S(1)} async-done(((f32[8,80,128]{2,1,0:T(8,128)}), f32[8,80,128]{2,1,0:T(8,128)S(1)}, u32[]{:S(2)}, u32[]{:S(2)}) %all-to-all-start.10) | async-done | bytes 327712 | tf_op jit(solution)/shard_map/all_to_all | solution.py:35
  200.8 0.7 broadcast_in_dim.275
  201.5 3.4 %all-to-all-start.11 = ((f32[8,48,128]{2,1,0:T(8,128)}), f32[8,48,128]{2,1,0:T(8,128)S(1)}, u32[]{:S(2)}, u32[]{:S(2)}) async-start(f32[8,48,128]{2,1,0:T(8,128)} %broadcast_in_dim.275), calls=%async_computation.11 | async-start | bytes 393216 | tf_op jit(solution)/shard_map/all_to_all | solution.py:35
  205.0 8.3 %all-to-all-done.11 = f32[8,48,128]{2,1,0:T(8,128)S(1)} async-done(((f32[8,48,128]{2,1,0:T(8,128)}), f32[8,48,128]{2,1,0:T(8,128)S(1)}, u32[]{:S(2)}, u32[]{:S(2)}) %all-to-all-start.11) | async-done | bytes 196640 | tf_op jit(solution)/shard_map/all_to_all | solution.py:35
  214.1 0.8 multiply_reduce_fusion.4
  215.9 1.0 convolution_bitcast_fusion.7
  218.0 0.7 convolution_bitcast_fusion.1
  221.9 12.7 %all_to_all.93 = f32[8,80,128]{2,1,0:T(8,128)S(1)} all-to-all(f32[8,80,128]{2,1,0:T(8,128)S(1)} %bitcast.501), channel_id=1, replica_groups=mesh['x_hi'=2,'z'=8,'core'=2,'y'=8,'x_lo'=2] {'x_lo','x_hi','core'}, dimensions={0} | all-to-all | bytes 655360 | tf_op jit(solution)/shard_map/all_to_all | solution.py:55
  234.7 0.7 broadcast_in_dim.280
  235.4 3.4 %all-to-all-start.13 = ((f32[8,80,128]{2,1,0:T(8,128)}), f32[8,80,128]{2,1,0:T(8,128)S(1)}, u32[]{:S(2)}, u32[]{:S(2)}) async-start(f32[8,80,128]{2,1,0:T(8,128)} %broadcast_in_dim.280), calls=%async_computation.13 | async-start | bytes 655360 | tf_op jit(solution)/shard_map/all_to_all | solution.py:35
  238.9 12.9 %all-to-all-done.13 = f32[8,80,128]{2,1,0:T(8,128)S(1)} async-done(((f32[8,80,128]{2,1,0:T(8,128)}), f32[8,80,128]{2,1,0:T(8,128)S(1)}, u32[]{:S(2)}, u32[]{:S(2)}) %all-to-all-start.13) | async-done | bytes 327712 | tf_op jit(solution)/shard_map/all_to_all | solution.py:35
  251.8 0.7 broadcast_in_dim.281
  252.5 3.4 %all-to-all-start.14 = ((f32[8,48,128]{2,1,0:T(8,128)}), f32[8,48,128]{2,1,0:T(8,128)S(1)}, u32[]{:S(2)}, u32[]{:S(2)}) async-start(f32[8,48,128]{2,1,0:T(8,128)} %broadcast_in_dim.281), calls=%async_computation.14 | async-start | bytes 393216 | tf_op jit(solution)/shard_map/all_to_all | solution.py:35
  256.0 8.3 %all-to-all-done.14 = f32[8,48,128]{2,1,0:T(8,128)S(1)} async-done(((f32[8,48,128]{2,1,0:T(8,128)}), f32[8,48,128]{2,1,0:T(8,128)S(1)}, u32[]{:S(2)}, u32[]{:S(2)}) %all-to-all-start.14) | async-done | bytes 196640 | tf_op jit(solution)/shard_map/all_to_all | solution.py:35
  265.1 0.8 multiply_reduce_fusion.2
  266.9 1.0 convolution_bitcast_fusion.6
  272.9 12.7 %all_to_all.94 = f32[8,80,128]{2,1,0:T(8,128)S(1)} all-to-all(f32[8,80,128]{2,1,0:T(8,128)S(1)} %bitcast.502), channel_id=1, replica_groups=mesh['x_hi'=2,'z'=8,'core'=2,'y'=8,'x_lo'=2] {'x_lo','x_hi','core'}, dimensions={0} | all-to-all | bytes 655360 | tf_op jit(solution)/shard_map/all_to_all | solution.py:55
  285.7 0.7 broadcast_in_dim.286
  286.4 3.4 %all-to-all-start.16 = ((f32[8,80,128]{2,1,0:T(8,128)}), f32[8,80,128]{2,1,0:T(8,128)S(1)}, u32[]{:S(2)}, u32[]{:S(2)}) async-start(f32[8,80,128]{2,1,0:T(8,128)} %broadcast_in_dim.286), calls=%async_computation.16 | async-start | bytes 655360 | tf_op jit(solution)/shard_map/all_to_all | solution.py:35
  289.9 12.9 %all-to-all-done.16 = f32[8,80,128]{2,1,0:T(8,128)S(1)} async-done(((f32[8,80,128]{2,1,0:T(8,128)}), f32[8,80,128]{2,1,0:T(8,128)S(1)}, u32[]{:S(2)}, u32[]{:S(2)}) %all-to-all-start.16) | async-done | bytes 327712 | tf_op jit(solution)/shard_map/all_to_all | solution.py:35
  302.8 0.7 broadcast_in_dim.287
  303.5 3.4 %all-to-all-start.17 = ((f32[8,48,128]{2,1,0:T(8,128)}), f32[8,48,128]{2,1,0:T(8,128)S(1)}, u32[]{:S(2)}, u32[]{:S(2)}) async-start(f32[8,48,128]{2,1,0:T(8,128)} %broadcast_in_dim.287), calls=%async_computation.17 | async-start | bytes 393216 | tf_op jit(solution)/shard_map/all_to_all | solution.py:35
  307.0 8.3 %all-to-all-done.17 = f32[8,48,128]{2,1,0:T(8,128)S(1)} async-done(((f32[8,48,128]{2,1,0:T(8,128)}), f32[8,48,128]{2,1,0:T(8,128)S(1)}, u32[]{:S(2)}, u32[]{:S(2)}) %all-to-all-start.17) | async-done | bytes 196640 | tf_op jit(solution)/shard_map/all_to_all | solution.py:35
  316.1 0.8 multiply_reduce_fusion
  319.2 0.7 fusion.25
  320.0 0.8 fusion.13
  320.7 0.8 fusion.1
  (271 shorter events, 25.8 us)
Async XLA Ops:
  0.6 1.3 copy-start
  0.6 1.0 copy-start.2
  1.7 0.8 copy-start.1
  4.2 0.7 copy-start.3
  7.9 17.3 %all-to-all-start = ((f32[8,80,128]{2,1,0:T(8,128)}), f32[8,80,128]{2,1,0:T(8,128)S(1)}, u32[]{:S(2)}, u32[]{:S(2)}) async-start(f32[8,80,128]{2,1,0:T(8,128)} %bitcast.15), calls=%async_computation | async-start | bytes 655360 | tf_op jit(solution)/shard_map/all_to_all | solution.py:55
  26.0 17.2 %all-to-all-start.1 = ((f32[8,80,128]{2,1,0:T(8,128)}), f32[8,80,128]{2,1,0:T(8,128)S(1)}, u32[]{:S(2)}, u32[]{:S(2)}) async-start(f32[8,80,128]{2,1,0:T(8,128)} %broadcast_in_dim.256), calls=%async_computation.1 | async-start | bytes 655360 | tf_op jit(solution)/shard_map/all_to_all | solution.py:35
  43.9 15.6 %all-to-all-start.2 = ((f32[8,48,128]{2,1,0:T(8,128)}), f32[8,48,128]{2,1,0:T(8,128)S(1)}, u32[]{:S(2)}, u32[]{:S(2)}) async-start(f32[8,48,128]{2,1,0:T(8,128)} %broadcast_in_dim.257), calls=%async_computation.2 | async-start | bytes 393216 | tf_op jit(solution)/shard_map/all_to_all | solution.py:35
  82.5 16.3 %all-to-all-start.4 = ((f32[8,80,128]{2,1,0:T(8,128)}), f32[8,80,128]{2,1,0:T(8,128)S(1)}, u32[]{:S(2)}, u32[]{:S(2)}) async-start(f32[8,80,128]{2,1,0:T(8,128)} %broadcast_in_dim.262), calls=%async_computation.4 | async-start | bytes 655360 | tf_op jit(solution)/shard_map/all_to_all | solution.py:35
  99.6 11.8 %all-to-all-start.5 = ((f32[8,48,128]{2,1,0:T(8,128)}), f32[8,48,128]{2,1,0:T(8,128)S(1)}, u32[]{:S(2)}, u32[]{:S(2)}) async-start(f32[8,48,128]{2,1,0:T(8,128)} %broadcast_in_dim.263), calls=%async_computation.5 | async-start | bytes 393216 | tf_op jit(solution)/shard_map/all_to_all | solution.py:35
  133.5 16.3 %all-to-all-start.7 = ((f32[8,80,128]{2,1,0:T(8,128)}), f32[8,80,128]{2,1,0:T(8,128)S(1)}, u32[]{:S(2)}, u32[]{:S(2)}) async-start(f32[8,80,128]{2,1,0:T(8,128)} %broadcast_in_dim.268), calls=%async_computation.7 | async-start | bytes 655360 | tf_op jit(solution)/shard_map/all_to_all | solution.py:35
  150.5 11.9 %all-to-all-start.8 = ((f32[8,48,128]{2,1,0:T(8,128)}), f32[8,48,128]{2,1,0:T(8,128)S(1)}, u32[]{:S(2)}, u32[]{:S(2)}) async-start(f32[8,48,128]{2,1,0:T(8,128)} %broadcast_in_dim.269), calls=%async_computation.8 | async-start | bytes 393216 | tf_op jit(solution)/shard_map/all_to_all | solution.py:35
  184.5 16.3 %all-to-all-start.10 = ((f32[8,80,128]{2,1,0:T(8,128)}), f32[8,80,128]{2,1,0:T(8,128)S(1)}, u32[]{:S(2)}, u32[]{:S(2)}) async-start(f32[8,80,128]{2,1,0:T(8,128)} %broadcast_in_dim.274), calls=%async_computation.10 | async-start | bytes 655360 | tf_op jit(solution)/shard_map/all_to_all | solution.py:35
  201.5 11.8 %all-to-all-start.11 = ((f32[8,48,128]{2,1,0:T(8,128)}), f32[8,48,128]{2,1,0:T(8,128)S(1)}, u32[]{:S(2)}, u32[]{:S(2)}) async-start(f32[8,48,128]{2,1,0:T(8,128)} %broadcast_in_dim.275), calls=%async_computation.11 | async-start | bytes 393216 | tf_op jit(solution)/shard_map/all_to_all | solution.py:35
  235.4 16.3 %all-to-all-start.13 = ((f32[8,80,128]{2,1,0:T(8,128)}), f32[8,80,128]{2,1,0:T(8,128)S(1)}, u32[]{:S(2)}, u32[]{:S(2)}) async-start(f32[8,80,128]{2,1,0:T(8,128)} %broadcast_in_dim.280), calls=%async_computation.13 | async-start | bytes 655360 | tf_op jit(solution)/shard_map/all_to_all | solution.py:35
  252.5 11.8 %all-to-all-start.14 = ((f32[8,48,128]{2,1,0:T(8,128)}), f32[8,48,128]{2,1,0:T(8,128)S(1)}, u32[]{:S(2)}, u32[]{:S(2)}) async-start(f32[8,48,128]{2,1,0:T(8,128)} %broadcast_in_dim.281), calls=%async_computation.14 | async-start | bytes 393216 | tf_op jit(solution)/shard_map/all_to_all | solution.py:35
  286.4 16.3 %all-to-all-start.16 = ((f32[8,80,128]{2,1,0:T(8,128)}), f32[8,80,128]{2,1,0:T(8,128)S(1)}, u32[]{:S(2)}, u32[]{:S(2)}) async-start(f32[8,80,128]{2,1,0:T(8,128)} %broadcast_in_dim.286), calls=%async_computation.16 | async-start | bytes 655360 | tf_op jit(solution)/shard_map/all_to_all | solution.py:35
  303.5 11.8 %all-to-all-start.17 = ((f32[8,48,128]{2,1,0:T(8,128)}), f32[8,48,128]{2,1,0:T(8,128)S(1)}, u32[]{:S(2)}, u32[]{:S(2)}) async-start(f32[8,48,128]{2,1,0:T(8,128)} %broadcast_in_dim.287), calls=%async_computation.17 | async-start | bytes 393216 | tf_op jit(solution)/shard_map/all_to_all | solution.py:35

commit v2 on v1

v2 whole, which is shorter than its diff:
```python
import jax
import jax.numpy as jnp
from jax import lax
from jax.sharding import Mesh, PartitionSpec as P

ITERS = 6

HP = lax.Precision.HIGHEST
NEAR = ("x_lo", "x_hi", "core")


def gram(factor):
    return jnp.dot(factor, factor.T, precision=HP)


def inverse_norm(matrix):
    return 1.0 / jnp.sqrt(jnp.sum(matrix * matrix) + 1e-06)


def descend(factor, hessian, contraction):
    return factor - inverse_norm(hessian) * (jnp.dot(hessian, factor, precision=HP) - contraction)


def sum_over(block, axis, size):
    copies = jnp.broadcast_to(block[None], (size,) + block.shape)
    return lax.all_to_all(copies, axis, 0, 0).sum(0)


def tile(*pieces):
    return jnp.concatenate(pieces + (jnp.zeros((8, 128 - sum(p.shape[1] for p in pieces)), jnp.float32),), 1)


def row_message(part_b, gram_a, part_c, quarter):
    rows = slice(8 * quarter, 8 * quarter + 8)
    gap = jnp.zeros((8, 32), jnp.float32)
    return jnp.concatenate([part_b[rows, :128], part_b[rows, 128:], tile(gram_a[rows], gap, part_c[rows])], 0)


def col_message(part_a, gram_b, part_c, half, quarter):
    rows = slice(16 * half, 16 * half + 16)
    rows_b = gram_b[rows]
    part_c = part_c[8 * quarter : 8 * quarter + 8]
    return jnp.concatenate([part_a[rows], tile(rows_b[:8], rows_b[8:], part_c)], 0)


def shards(tensor, factor_a, factor_b, factor_c):
    fa, fb, fc = (factor_a, factor_b, factor_c)
    x_lo = lax.axis_index("x_lo")
    chip = lax.axis_index("x_hi") * 2 + lax.axis_index("core")
    same = jnp.arange(2)[:, None, None, None] == x_lo
    lane = jnp.arange(128)[None, :]
    lanes_c = (jnp.arange(24)[:, None] >= 16) & (lane >= 64)
    for step in range(ITERS):
        gram_a, gram_b, gram_c = (gram(fa), gram(fb), gram(fc))
        part_y = jnp.einsum("kij,rj->kri", tensor, fb, precision=HP)
        part_z = jnp.einsum("kij,ri->krj", tensor, fa, precision=HP)
        part_a = jnp.einsum("rk,kri->ri", fc, part_y, precision=HP)
        part_c = jnp.einsum("kri,ri->rk", part_y, fa, precision=HP)
        part_b = jnp.einsum("rk,krj->rj", fc, part_z, precision=HP)
        to_row = jnp.stack([row_message(part_b, gram_a, part_c, q) for q in range(4)])
        to_col = jnp.stack([jnp.stack([col_message(part_a, gram_b, part_c, h, q) for q in range(4)]) for h in range(2)])
        sent = jnp.where(same, to_row[None], to_col).reshape(8, 24, 128)
        got = lax.all_to_all(sent, NEAR, 0, 0).reshape(2, 4, 24, 128)
        near = got.sum(1)
        mine = lax.dynamic_index_in_dim(near, x_lo, 0, False)
        other = lax.dynamic_index_in_dim(near, 1 - x_lo, 0, False)
        for_row = jnp.where(lanes_c, mine + other, mine)
        own = lax.dynamic_index_in_dim(to_col[:, 0], x_lo, 0, False)
        across = lax.dynamic_index_in_dim(got, 1 - x_lo, 0, False)
        for_col = own + lax.dynamic_index_in_dim(across, chip, 0, False)
        for_row = sum_over(for_row, "z", 8)
        for_col = sum_over(jnp.where(lanes_c, for_row, for_col), "y", 8)
        for_row = jnp.where(lanes_c, for_col, for_row)
        sent = jnp.where(same, for_row[None, None], for_col[None, None])
        sent = jnp.broadcast_to(sent, (2, 4, 24, 128)).reshape(8, 24, 128)
        got = lax.all_to_all(sent, NEAR, 0, 0).reshape(2, 4, 24, 128)
        mine = lax.dynamic_index_in_dim(got, x_lo, 0, False)
        across = lax.dynamic_index_in_dim(got, 1 - x_lo, 0, False)
        other = lax.dynamic_index_in_dim(across, chip, 0, False)
        low = jnp.where(x_lo == 0, for_col, other)
        high = jnp.where(x_lo == 0, other, for_col)
        mode_a = jnp.concatenate([low[:16], high[:16]], 0)
        gram_b = jnp.concatenate([low[16:, :32], low[16:, 32:64], high[16:, :32], high[16:, 32:64]], 0)
        mode_b = jnp.concatenate([mine[:, :8].reshape(32, 128), mine[:, 8:16].reshape(32, 128)], 1)
        gram_a = mine[:, 16:, :32].reshape(32, 32)
        mode_c = mine[:, 16:, 64:72].reshape(32, 8)
        next_a = descend(fa, gram_b * gram_c, mode_a)
        next_b = descend(fb, gram_a * gram_c, mode_b)
        next_c = descend(fc, gram_a * gram_b, mode_c)
        fa, fb, fc = (next_a, next_b, next_c)
    return (fa, fb, fc)


def solution(mesh):
    rows, cols = mesh.devices.shape
    devices = mesh.devices.reshape(2, rows // 4, 2, cols // 2, 2)
    fine = Mesh(devices, ("x_hi", "z", "core", "y", "x_lo"))
    row, col = (("x_hi", "z", "core"), ("y", "x_lo"))
    in_specs = (P(None, row, col), P(None, row), P(None, col), P())
    out_specs = (P(None, row), P(None, col), P())
    return jax.shard_map(shards, mesh=fine, in_specs=in_specs, out_specs=out_specs, check_vma=False)
```

time: 324 us -> 313 us (0.966)
  blocking collectives: 64.6 us -> 157 us
  waiting for transfers between devices: 133 us -> 54.1 us
  starting transfers between devices: 56.9 us -> 39.4 us
  local copies, waits for them, and re-layouts: 16.8 us -> 7.89 us
  other arithmetic: 5.14 us -> 8.92 us
    all_to_all x5 -> x16, blocking collectives: 64.6 us -> 157 us  [the longest x10 92.1 us: shards(): got = lax.all_to_all(sent, NEAR, 0, 0).reshape(2, 4, 24, 128)]
    all_to_all x12 -> x6, waiting for transfers between devices: 126 us -> 44.4 us  [sum_over(): return lax.all_to_all(copies, axis, 0, 0).sum(0)]
    all_to_all x12 -> x6, starting transfers between devices: 46.7 us -> 22.5 us  [sum_over(): return lax.all_to_all(copies, axis, 0, 0).sum(0)]
    all_to_all x1 -> x2, starting transfers between devices: 10.2 us -> 17 us  [shards(): got = lax.all_to_all(sent, NEAR, 0, 0).reshape(2, 4, 24, 128)]
    broadcast_in_dim x12, local copies, waits for them, and re-layouts: 8.5 us -> 3.86 us  [sum_over(): copies = jnp.broadcast_to(block[None], (size,) + block.shape)]
    reshape x66 -> x18, local copies, waits for them, and re-layouts: 4.45 us -> 0.84 us  [the longest x12 0.82 us: shards(): mode_c = mine[:, 16:, 64:72].reshape(32, 8)]
    all_to_all x1 -> x2, waiting for transfers between devices: 7.11 us -> 9.73 us  [shards(): got = lax.all_to_all(sent, NEAR, 0, 0).reshape(2, 4, 24, 128)]
  transfers between devices with their start and end apart: 13 -> 8, of which waited for: 13 -> 8; matrix products, arithmetic and copies ran while one was open for 0% -> 0% of each run, Pallas kernels for 0% -> 0%
where the time goes in v2:
time: 313 us; the launch traced here: 311 us
  blocking collectives  157 us (50%)
  waiting for transfers between devices  54.1 us (17%)
  starting transfers between devices  39.4 us (13%)
  matrix products  30.2 us (10%)
  between operations  14.3 us (5%)
  other arithmetic  8.92 us (3%)
  local copies, waits for them, and re-layouts  7.89 us (3%)
    all_to_all x10, blocking collectives, shards(): got = lax.all_to_all(sent, NEAR, 0, 0).reshape(2, 4, 24, 128)  92.1 us
    all_to_all x6, blocking collectives, sum_over(): return lax.all_to_all(copies, axis, 0, 0).sum(0)  64.5 us
    all_to_all x6, waiting for transfers between devices, sum_over(): return lax.all_to_all(copies, axis, 0, 0).sum(0)  44.4 us
    all_to_all x6, starting transfers between devices, sum_over(): return lax.all_to_all(copies, axis, 0, 0).sum(0)  22.5 us
    all_to_all x2, starting transfers between devices, shards(): got = lax.all_to_all(sent, NEAR, 0, 0).reshape(2, 4, 24, 128)  17 us
    all_to_all x2, waiting for transfers between devices, shards(): got = lax.all_to_all(sent, NEAR, 0, 0).reshape(2, 4, 24, 128)  9.73 us
    dot_general x18, matrix products, gram(): return jnp.dot(factor, factor.T, precision=HP)  7.61 us
    dot_general x6, matrix products, shards(): part_y = jnp.einsum('kij,rj->kri', tensor, fb, precision=HP)  6.27 us
  transfers between devices with their start and end apart: 8, of which 8 were waited for; matrix products, arithmetic and copies ran while one was open for 0% of the time, Pallas kernels for 0%

profile of v2, /device:TPU:1, one launch (start us, length us, event | category | flops | bytes accessed | tf_op | source)
XLA Modules:
  0.0 311.4 jit_solution(8098305853400910998)
XLA Ops:
  0.7 1.0 fusion.277
  1.9 1.0 convolution_bitcast_fusion.5
  3.0 0.7 fusion.106
  6.3 0.7 bitcast_select_fusion.5
  7.0 10.1 %all-to-all-start = ((f32[8,24,128]{2,1,0:T(8,128)}), f32[8,24,128]{2,1,0:T(8,128)S(1)}, u32[]{:S(2)}, u32[]{:S(2)}) async-start(f32[8,24,128]{2,1,0:T(8,128)} %bitcast_select_fusion.5), calls=%async_computation | async-start | bytes 196608 | tf_op jit(solution)/shard_map/all_to_all | solution.py:63
  17.2 4.9 %all-to-all-done = f32[8,24,128]{2,1,0:T(8,128)S(1)} async-done(((f32[8,24,128]{2,1,0:T(8,128)}), f32[8,24,128]{2,1,0:T(8,128)S(1)}, u32[]{:S(2)}, u32[]{:S(2)}) %all-to-all-start) | async-done | bytes 98336 | tf_op jit(solution)/shard_map/all_to_all | solution.py:63
  22.1 0.6 broadcast_in_dim.302
  22.8 5.7 %all-to-all-start.1 = ((f32[8,24,128]{2,1,0:T(8,128)}), f32[8,24,128]{2,1,0:T(8,128)S(1)}, u32[]{:S(2)}, u32[]{:S(2)}) async-start(f32[8,24,128]{2,1,0:T(8,128)} %broadcast_in_dim.302), calls=%async_computation.1 | async-start | bytes 196608 | tf_op jit(solution)/shard_map/all_to_all | solution.py:26
  28.5 7.7 %all-to-all-done.1 = f32[8,24,128]{2,1,0:T(8,128)S(1)} async-done(((f32[8,24,128]{2,1,0:T(8,128)}), f32[8,24,128]{2,1,0:T(8,128)S(1)}, u32[]{:S(2)}, u32[]{:S(2)}) %all-to-all-start.1) | async-done | bytes 98336 | tf_op jit(solution)/shard_map/all_to_all | solution.py:26
  36.3 14.2 %all_to_all.120 = f32[8,24,128]{2,1,0:T(8,128)S(1)} all-to-all(f32[8,24,128]{2,1,0:T(8,128)S(1)} %broadcast_in_dim.303), channel_id=1, replica_groups=mesh['x_hi'=2,'z'=8,'core'=2,'y'=8,'x_lo'=2] {'y'}, dimensions={0} | all-to-all | bytes 196608 | tf_op jit(solution)/shard_map/all_to_all | solution.py:26
  50.6 0.6 broadcast_in_dim.307
  51.3 6.8 %all-to-all-start.3 = ((f32[8,24,128]{2,1,0:T(8,128)}), f32[8,24,128]{2,1,0:T(8,128)S(1)}, u32[]{:S(2)}, u32[]{:S(2)}) async-start(f32[8,24,128]{2,1,0:T(8,128)} %bitcast.30), calls=%async_computation.3 | async-start | bytes 196608 | tf_op jit(solution)/shard_map/all_to_all | solution.py:76
  58.1 4.9 %all-to-all-done.3 = f32[8,24,128]{2,1,0:T(8,128)S(1)} async-done(((f32[8,24,128]{2,1,0:T(8,128)}), f32[8,24,128]{2,1,0:T(8,128)S(1)}, u32[]{:S(2)}, u32[]{:S(2)}) %all-to-all-start.3) | async-done | bytes 98336 | tf_op jit(solution)/shard_map/all_to_all | solution.py:76
  63.2 0.6 fusion.105
  63.8 0.8 multiply_reduce_fusion.10
  65.5 0.7 fusion.102
  67.1 1.0 convolution_bitcast_fusion.4
  71.2 8.1 %all_to_all.121 = f32[8,24,128]{2,1,0:T(8,128)S(1)} all-to-all(f32[8,24,128]{2,1,0:T(8,128)S(1)} %bitcast_select_fusion.4), channel_id=1, replica_groups=mesh['x_hi'=2,'z'=8,'core'=2,'y'=8,'x_lo'=2] {'x_lo','x_hi','core'}, dimensions={0} | all-to-all | bytes 196608 | tf_op jit(solution)/shard_map/all_to_all | solution.py:63
  79.3 0.6 broadcast_in_dim.311
  80.0 3.4 %all-to-all-start.5 = ((f32[8,24,128]{2,1,0:T(8,128)}), f32[8,24,128]{2,1,0:T(8,128)S(1)}, u32[]{:S(2)}, u32[]{:S(2)}) async-start(f32[8,24,128]{2,1,0:T(8,128)} %broadcast_in_dim.311), calls=%async_computation.5 | async-start | bytes 196608 | tf_op jit(solution)/shard_map/all_to_all | solution.py:26
  83.4 7.3 %all-to-all-done.5 = f32[8,24,128]{2,1,0:T(8,128)S(1)} async-done(((f32[8,24,128]{2,1,0:T(8,128)}), f32[8,24,128]{2,1,0:T(8,128)S(1)}, u32[]{:S(2)}, u32[]{:S(2)}) %all-to-all-start.5) | async-done | bytes 98336 | tf_op jit(solution)/shard_map/all_to_all | solution.py:26
  90.8 10.1 %all_to_all.122 = f32[8,24,128]{2,1,0:T(8,128)S(1)} all-to-all(f32[8,24,128]{2,1,0:T(8,128)S(1)} %broadcast_in_dim.312), channel_id=1, replica_groups=mesh['x_hi'=2,'z'=8,'core'=2,'y'=8,'x_lo'=2] {'y'}, dimensions={0} | all-to-all | bytes 196608 | tf_op jit(solution)/shard_map/all_to_all | solution.py:26
  101.1 10.4 %all_to_all.123 = f32[8,24,128]{2,1,0:T(8,128)S(1)} all-to-all(f32[8,24,128]{2,1,0:T(8,128)S(1)} %bitcast.618), channel_id=1, replica_groups=mesh['x_hi'=2,'z'=8,'core'=2,'y'=8,'x_lo'=2] {'x_lo','x_hi','core'}, dimensions={0} | all-to-all | bytes 196608 | tf_op jit(solution)/shard_map/all_to_all | solution.py:76
  111.7 0.6 fusion.101
  112.3 0.8 multiply_reduce_fusion.8
  113.9 0.7 fusion.98
  115.6 1.0 convolution_bitcast_fusion.3
  119.7 8.0 %all_to_all.124 = f32[8,24,128]{2,1,0:T(8,128)S(1)} all-to-all(f32[8,24,128]{2,1,0:T(8,128)S(1)} %bitcast_select_fusion.3), channel_id=1, replica_groups=mesh['x_hi'=2,'z'=8,'core'=2,'y'=8,'x_lo'=2] {'x_lo','x_hi','core'}, dimensions={0} | all-to-all | bytes 196608 | tf_op jit(solution)/shard_map/all_to_all | solution.py:63
  127.8 0.6 broadcast_in_dim.319
  128.4 3.4 %all-to-all-start.9 = ((f32[8,24,128]{2,1,0:T(8,128)}), f32[8,24,128]{2,1,0:T(8,128)S(1)}, u32[]{:S(2)}, u32[]{:S(2)}) async-start(f32[8,24,128]{2,1,0:T(8,128)} %broadcast_in_dim.319), calls=%async_computation.9 | async-start | bytes 196608 | tf_op jit(solution)/shard_map/all_to_all | solution.py:26
  131.8 7.3 %all-to-all-done.9 = f32[8,24,128]{2,1,0:T(8,128)S(1)} async-done(((f32[8,24,128]{2,1,0:T(8,128)}), f32[8,24,128]{2,1,0:T(8,128)S(1)}, u32[]{:S(2)}, u32[]{:S(2)}) %all-to-all-start.9) | async-done | bytes 98336 | tf_op jit(solution)/shard_map/all_to_all | solution.py:26
  139.3 10.1 %all_to_all.125 = f32[8,24,128]{2,1,0:T(8,128)S(1)} all-to-all(f32[8,24,128]{2,1,0:T(8,128)S(1)} %broadcast_in_dim.320), channel_id=1, replica_groups=mesh['x_hi'=2,'z'=8,'core'=2,'y'=8,'x_lo'=2] {'y'}, dimensions={0} | all-to-all | bytes 196608 | tf_op jit(solution)/shard_map/all_to_all | solution.py:26
  149.5 10.4 %all_to_all.126 = f32[8,24,128]{2,1,0:T(8,128)S(1)} all-to-all(f32[8,24,128]{2,1,0:T(8,128)S(1)} %bitcast.619), channel_id=1, replica_groups=mesh['x_hi'=2,'z'=8,'core'=2,'y'=8,'x_lo'=2] {'x_lo','x_hi','core'}, dimensions={0} | all-to-all | bytes 196608 | tf_op jit(solution)/shard_map/all_to_all | solution.py:76
  160.7 0.8 multiply_reduce_fusion.6
  162.4 0.7 fusion.94
  164.1 1.0 convolution_bitcast_fusion.2
  168.2 8.0 %all_to_all.127 = f32[8,24,128]{2,1,0:T(8,128)S(1)} all-to-all(f32[8,24,128]{2,1,0:T(8,128)S(1)} %bitcast_select_fusion.2), channel_id=1, replica_groups=mesh['x_hi'=2,'z'=8,'core'=2,'y'=8,'x_lo'=2] {'x_lo','x_hi','core'}, dimensions={0} | all-to-all | bytes 196608 | tf_op jit(solution)/shard_map/all_to_all | solution.py:63
  176.3 0.6 broadcast_in_dim.327
  176.9 3.4 %all-to-all-start.13 = ((f32[8,24,128]{2,1,0:T(8,128)}), f32[8,24,128]{2,1,0:T(8,128)S(1)}, u32[]{:S(2)}, u32[]{:S(2)}) async-start(f32[8,24,128]{2,1,0:T(8,128)} %broadcast_in_dim.327), calls=%async_computation.13 | async-start | bytes 196608 | tf_op jit(solution)/shard_map/all_to_all | solution.py:26
  180.3 7.3 %all-to-all-done.13 = f32[8,24,128]{2,1,0:T(8,128)S(1)} async-done(((f32[8,24,128]{2,1,0:T(8,128)}), f32[8,24,128]{2,1,0:T(8,128)S(1)}, u32[]{:S(2)}, u32[]{:S(2)}) %all-to-all-start.13) | async-done | bytes 98336 | tf_op jit(solution)/shard_map/all_to_all | solution.py:26
  187.7 10.1 %all_to_all.128 = f32[8,24,128]{2,1,0:T(8,128)S(1)} all-to-all(f32[8,24,128]{2,1,0:T(8,128)S(1)} %broadcast_in_dim.328), channel_id=1, replica_groups=mesh['x_hi'=2,'z'=8,'core'=2,'y'=8,'x_lo'=2] {'y'}, dimensions={0} | all-to-all | bytes 196608 | tf_op jit(solution)/shard_map/all_to_all | solution.py:26
  198.0 10.4 %all_to_all.129 = f32[8,24,128]{2,1,0:T(8,128)S(1)} all-to-all(f32[8,24,128]{2,1,0:T(8,128)S(1)} %bitcast.620), channel_id=1, replica_groups=mesh['x_hi'=2,'z'=8,'core'=2,'y'=8,'x_lo'=2] {'x_lo','x_hi','core'}, dimensions={0} | all-to-all | bytes 196608 | tf_op jit(solution)/shard_map/all_to_all | solution.py:76
  209.2 0.8 multiply_reduce_fusion.4
  210.9 0.7 fusion.90
  212.5 1.0 convolution_bitcast_fusion.1
  216.6 8.0 %all_to_all.130 = f32[8,24,128]{2,1,0:T(8,128)S(1)} all-to-all(f32[8,24,128]{2,1,0:T(8,128)S(1)} %bitcast_select_fusion.1), channel_id=1, replica_groups=mesh['x_hi'=2,'z'=8,'core'=2,'y'=8,'x_lo'=2] {'x_lo','x_hi','core'}, dimensions={0} | all-to-all | bytes 196608 | tf_op jit(solution)/shard_map/all_to_all | solution.py:63
  224.7 0.6 broadcast_in_dim.335
  225.4 3.4 %all-to-all-start.17 = ((f32[8,24,128]{2,1,0:T(8,128)}), f32[8,24,128]{2,1,0:T(8,128)S(1)}, u32[]{:S(2)}, u32[]{:S(2)}) async-start(f32[8,24,128]{2,1,0:T(8,128)} %broadcast_in_dim.335), calls=%async_computation.17 | async-start | bytes 196608 | tf_op jit(solution)/shard_map/all_to_all | solution.py:26
  228.8 7.3 %all-to-all-done.17 = f32[8,24,128]{2,1,0:T(8,128)S(1)} async-done(((f32[8,24,128]{2,1,0:T(8,128)}), f32[8,24,128]{2,1,0:T(8,128)S(1)}, u32[]{:S(2)}, u32[]{:S(2)}) %all-to-all-start.17) | async-done | bytes 98336 | tf_op jit(solution)/shard_map/all_to_all | solution.py:26
  236.2 10.1 %all_to_all.131 = f32[8,24,128]{2,1,0:T(8,128)S(1)} all-to-all(f32[8,24,128]{2,1,0:T(8,128)S(1)} %broadcast_in_dim.336), channel_id=1, replica_groups=mesh['x_hi'=2,'z'=8,'core'=2,'y'=8,'x_lo'=2] {'y'}, dimensions={0} | all-to-all | bytes 196608 | tf_op jit(solution)/shard_map/all_to_all | solution.py:26
  246.4 10.4 %all_to_all.132 = f32[8,24,128]{2,1,0:T(8,128)S(1)} all-to-all(f32[8,24,128]{2,1,0:T(8,128)S(1)} %bitcast.621), channel_id=1, replica_groups=mesh['x_hi'=2,'z'=8,'core'=2,'y'=8,'x_lo'=2] {'x_lo','x_hi','core'}, dimensions={0} | all-to-all | bytes 196608 | tf_op jit(solution)/shard_map/all_to_all | solution.py:76
  257.7 0.8 multiply_reduce_fusion.2
  259.3 0.7 fusion.86
  261.0 1.0 convolution_bitcast_fusion
  265.1 8.0 %all_to_all.133 = f32[8,24,128]{2,1,0:T(8,128)S(1)} all-to-all(f32[8,24,128]{2,1,0:T(8,128)S(1)} %bitcast_select_fusion), channel_id=1, replica_groups=mesh['x_hi'=2,'z'=8,'core'=2,'y'=8,'x_lo'=2] {'x_lo','x_hi','core'}, dimensions={0} | all-to-all | bytes 196608 | tf_op jit(solution)/shard_map/all_to_all | solution.py:63
  273.2 0.6 broadcast_in_dim.343
  273.8 3.4 %all-to-all-start.21 = ((f32[8,24,128]{2,1,0:T(8,128)}), f32[8,24,128]{2,1,0:T(8,128)S(1)}, u32[]{:S(2)}, u32[]{:S(2)}) async-start(f32[8,24,128]{2,1,0:T(8,128)} %broadcast_in_dim.343), calls=%async_computation.21 | async-start | bytes 196608 | tf_op jit(solution)/shard_map/all_to_all | solution.py:26
  277.2 7.3 %all-to-all-done.21 = f32[8,24,128]{2,1,0:T(8,128)S(1)} async-done(((f32[8,24,128]{2,1,0:T(8,128)}), f32[8,24,128]{2,1,0:T(8,128)S(1)}, u32[]{:S(2)}, u32[]{:S(2)}) %all-to-all-start.21) | async-done | bytes 98336 | tf_op jit(solution)/shard_map/all_to_all | solution.py:26
  284.7 10.1 %all_to_all.134 = f32[8,24,128]{2,1,0:T(8,128)S(1)} all-to-all(f32[8,24,128]{2,1,0:T(8,128)S(1)} %broadcast_in_dim.344), channel_id=1, replica_groups=mesh['x_hi'=2,'z'=8,'core'=2,'y'=8,'x_lo'=2] {'y'}, dimensions={0} | all-to-all | bytes 196608 | tf_op jit(solution)/shard_map/all_to_all | solution.py:26
  294.9 10.4 %all_to_all.135 = f32[8,24,128]{2,1,0:T(8,128)S(1)} all-to-all(f32[8,24,128]{2,1,0:T(8,128)S(1)} %bitcast.622), channel_id=1, replica_groups=mesh['x_hi'=2,'z'=8,'core'=2,'y'=8,'x_lo'=2] {'x_lo','x_hi','core'}, dimensions={0} | all-to-all | bytes 196608 | tf_op jit(solution)/shard_map/all_to_all | solution.py:76
  306.1 0.8 multiply_reduce_fusion
  309.1 0.7 fusion.25
  309.8 0.8 fusion.1
  310.6 0.8 fusion.13
  (276 shorter events, 22.2 us)
Async XLA Ops:
  0.6 1.3 copy-start
  0.6 1.2 copy-start.1
  1.9 1.1 copy-start.2
  3.6 0.7 copy-start.3
  7.0 15.0 %all-to-all-start = ((f32[8,24,128]{2,1,0:T(8,128)}), f32[8,24,128]{2,1,0:T(8,128)S(1)}, u32[]{:S(2)}, u32[]{:S(2)}) async-start(f32[8,24,128]{2,1,0:T(8,128)} %bitcast_select_fusion.5), calls=%async_computation | async-start | bytes 196608 | tf_op jit(solution)/shard_map/all_to_all | solution.py:63
  22.8 13.4 %all-to-all-start.1 = ((f32[8,24,128]{2,1,0:T(8,128)}), f32[8,24,128]{2,1,0:T(8,128)S(1)}, u32[]{:S(2)}, u32[]{:S(2)}) async-start(f32[8,24,128]{2,1,0:T(8,128)} %broadcast_in_dim.302), calls=%async_computation.1 | async-start | bytes 196608 | tf_op jit(solution)/shard_map/all_to_all | solution.py:26
  51.3 11.7 %all-to-all-start.3 = ((f32[8,24,128]{2,1,0:T(8,128)}), f32[8,24,128]{2,1,0:T(8,128)S(1)}, u32[]{:S(2)}, u32[]{:S(2)}) async-start(f32[8,24,128]{2,1,0:T(8,128)} %bitcast.30), calls=%async_computation.3 | async-start | bytes 196608 | tf_op jit(solution)/shard_map/all_to_all | solution.py:76
  80.0 10.7 %all-to-all-start.5 = ((f32[8,24,128]{2,1,0:T(8,128)}), f32[8,24,128]{2,1,0:T(8,128)S(1)}, u32[]{:S(2)}, u32[]{:S(2)}) async-start(f32[8,24,128]{2,1,0:T(8,128)} %broadcast_in_dim.311), calls=%async_computation.5 | async-start | bytes 196608 | tf_op jit(solution)/shard_map/all_to_all | solution.py:26
  128.4 10.7 %all-to-all-start.9 = ((f32[8,24,128]{2,1,0:T(8,128)}), f32[8,24,128]{2,1,0:T(8,128)S(1)}, u32[]{:S(2)}, u32[]{:S(2)}) async-start(f32[8,24,128]{2,1,0:T(8,128)} %broadcast_in_dim.319), calls=%async_computation.9 | async-start | bytes 196608 | tf_op jit(solution)/shard_map/all_to_all | solution.py:26
  176.9 10.7 %all-to-all-start.13 = ((f32[8,24,128]{2,1,0:T(8,128)}), f32[8,24,128]{2,1,0:T(8,128)S(1)}, u32[]{:S(2)}, u32[]{:S(2)}) async-start(f32[8,24,128]{2,1,0:T(8,128)} %broadcast_in_dim.327), calls=%async_computation.13 | async-start | bytes 196608 | tf_op jit(solution)/shard_map/all_to_all | solution.py:26
  225.4 10.7 %all-to-all-start.17 = ((f32[8,24,128]{2,1,0:T(8,128)}), f32[8,24,128]{2,1,0:T(8,128)S(1)}, u32[]{:S(2)}, u32[]{:S(2)}) async-start(f32[8,24,128]{2,1,0:T(8,128)} %broadcast_in_dim.335), calls=%async_computation.17 | async-start | bytes 196608 | tf_op jit(solution)/shard_map/all_to_all | solution.py:26
  273.8 10.7 %all-to-all-start.21 = ((f32[8,24,128]{2,1,0:T(8,128)}), f32[8,24,128]{2,1,0:T(8,128)S(1)}, u32[]{:S(2)}, u32[]{:S(2)}) async-start(f32[8,24,128]{2,1,0:T(8,128)} %broadcast_in_dim.343), calls=%async_computation.21 | async-start | bytes 196608 | tf_op jit(solution)/shard_map/all_to_all | solution.py:26

commit v3 on v2

v3 whole, which is shorter than its diff:
```python
import functools

import jax
import jax.numpy as jnp
from jax import lax
from jax.experimental import pallas as pl
from jax.experimental.pallas import tpu as pltpu
from jax.sharding import Mesh, PartitionSpec as P

ITERS = 6

HP = lax.Precision.HIGHEST
F32, BF16 = (jnp.float32, jnp.bfloat16)
NEAR = ("x_lo", "x_hi", "core")
VMEM = pl.BlockSpec(memory_space=pltpu.VMEM)
SMEM = pl.BlockSpec(memory_space=pltpu.SMEM)


def product(a, b, contract=(1, 0), precision=HP):
    dims = (((contract[0],), (contract[1],)), ((), ()))
    return lax.dot_general(a, b, dims, precision=precision, preferred_element_type=F32)


def split(x):
    high = x.astype(BF16)
    return high, (x - high.astype(F32)).astype(BF16)


def inverse_norm(matrix):
    return 1.0 / jnp.sqrt(jnp.sum(matrix * matrix, keepdims=True) + 1e-06)


def descend(factor, hessian, contraction):
    return factor - inverse_norm(hessian) * (product(hessian, factor) - contraction)


def prepare(t_ref, wz_ref, wy_ref):
    for k in range(8):
        high, low = split(t_ref[k])
        wz_ref[:128, 256 * k : 256 * k + 256] = high
        wz_ref[128:, 256 * k : 256 * k + 256] = low
        high, low = split(t_ref[k].T)
        wy_ref[0, :, 128 * k : 128 * k + 128] = high
        wy_ref[1, :, 128 * k : 128 * k + 128] = low


def update(x_lo, chip, got_ref, col_ref, fa, fb, fc):
    mine = [got_ref[4 * x_lo + q] for q in range(4)]
    other = got_ref[4 * (1 - x_lo) + chip]
    low = jnp.where(x_lo == 0, col_ref[...], other)
    high = jnp.where(x_lo == 0, other, col_ref[...])
    mode_a = jnp.concatenate([low[:16], high[:16]], 0)
    gram_b = jnp.concatenate([low[16:, :32], low[16:, 32:64], high[16:, :32], high[16:, 32:64]], 0)
    mode_b = jnp.concatenate([jnp.concatenate([m[:8], m[8:16]], 1) for m in mine], 0)
    gram_a = jnp.concatenate([m[16:, :32] for m in mine], 0)
    mode_c = jnp.concatenate([m[16:, 64:72] for m in mine], 0)
    gram_c = product(fc, fc, (1, 1))
    next_a = descend(fa, gram_b * gram_c, mode_a)
    next_b = descend(fb, gram_a * gram_c, mode_b)
    next_c = descend(fc, gram_a * gram_b, mode_c)
    return next_a, next_b, next_c


def contract(x_lo, fa, fb, fc, wz_ref, wy_ref, sent_ref, own_ref):
    a_high, a_low = split(fa)
    b_high, b_low = split(fb)
    left = jnp.concatenate([jnp.concatenate([a_high, a_high], 1), jnp.concatenate([a_low, jnp.zeros_like(a_low)], 1)], 0)
    z = product(left, wz_ref[...], precision=None)
    z = z[:32] + z[32:]
    y = product(jnp.concatenate([b_high, b_low], 0), wy_ref[0], precision=None)
    y = y[:32] + y[32:] + product(b_high, wy_ref[1], precision=None)
    lane = lax.broadcasted_iota(jnp.int32, (32, 128), 1)
    part_a = jnp.zeros((32, 128), F32)
    part_b = jnp.zeros((32, 256), F32)
    part_c = jnp.zeros((32, 128), F32)
    for k in range(8):
        weight = fc[:, k : k + 1]
        y_k = y[:, 128 * k : 128 * k + 128]
        part_a += weight * y_k
        part_b += weight * z[:, 256 * k : 256 * k + 256]
        part_c = jnp.where(lane == 64 + k, jnp.sum(y_k * fa, 1, keepdims=True), part_c)
    gram_a = product(fa, jnp.concatenate([fa, jnp.zeros((96, 128), F32)], 0), (1, 1))
    gram_b = product(fb, jnp.concatenate([fb, jnp.zeros((96, 256), F32)], 0), (1, 1))
    row_tile = gram_a + part_c
    for q in range(4):
        rows = slice(8 * q, 8 * q + 8)
        at = 4 * x_lo + q
        sent_ref[at, 0:8] = part_b[rows, :128]
        sent_ref[at, 8:16] = part_b[rows, 128:]
        sent_ref[at, 16:24] = row_tile[rows]
    first = x_lo == 0
    tile_low = gram_b[:8] + pltpu.roll(gram_b[8:16], 32, 1)
    tile_high = gram_b[16:24] + pltpu.roll(gram_b[24:], 32, 1)
    own_ref[:16] = jnp.where(first, part_a[:16], part_a[16:])
    own_ref[16:] = jnp.where(first, tile_low, tile_high)
    across = jnp.where(first, part_a[16:], part_a[:16])
    tile = jnp.where(first, tile_high, tile_low)
    for q in range(4):
        at = 4 * (1 - x_lo) + q
        sent_ref[at, 0:16] = across
        sent_ref[at, 16:24] = tile + part_c[8 * q : 8 * q + 8]


def first_kernel(place_ref, fa_ref, fb_ref, fc_ref, wz_ref, wy_ref, sent_ref, own_ref):
    contract(place_ref[0], fa_ref[...], fb_ref[...], fc_ref[...], wz_ref, wy_ref, sent_ref, own_ref)


def middle_kernel(place_ref, got_ref, col_ref, fa_ref, fb_ref, fc_ref, wz_ref, wy_ref, na_ref, nb_ref, nc_ref, sent_ref, own_ref):
    x_lo = place_ref[0]
    fa, fb, fc = update(x_lo, place_ref[1], got_ref, col_ref, fa_ref[...], fb_ref[...], fc_ref[...])
    na_ref[...] = fa
    nb_ref[...] = fb
    nc_ref[...] = fc
    contract(x_lo, fa, fb, fc, wz_ref, wy_ref, sent_ref, own_ref)


def last_kernel(place_ref, got_ref, col_ref, fa_ref, fb_ref, fc_ref, na_ref, nb_ref, nc_ref):
    fa, fb, fc = update(place_ref[0], place_ref[1], got_ref, col_ref, fa_ref[...], fb_ref[...], fc_ref[...])
    na_ref[...] = fa
    nb_ref[...] = fb
    nc_ref[...] = fc


def call(kernel, outs, *args):
    shapes = [jax.ShapeDtypeStruct(s, d) for s, d in outs]
    specs = [SMEM if a.dtype == jnp.int32 else VMEM for a in args]
    params = pltpu.CompilerParams(vmem_limit_bytes=16 * 1024 * 1024)
    return pl.pallas_call(kernel, out_shape=shapes, in_specs=specs, out_specs=[VMEM] * len(shapes), compiler_params=params)(*args)


def sum_over(block, axis, size):
    copies = jnp.broadcast_to(block[None], (size,) + block.shape)
    return lax.all_to_all(copies, axis, 0, 0).sum(0)


FACTORS = [((32, 128), F32), ((32, 256), F32), ((32, 8), F32)]
MESSAGES = [((8, 24, 128), F32), ((24, 128), F32)]


def shards(size_z, size_y, tensor, factor_a, factor_b, factor_c):
    factors = (factor_a, factor_b, factor_c)
    x_lo = lax.axis_index("x_lo")
    chip = lax.axis_index("x_hi") * 2 + lax.axis_index("core")
    place = jnp.stack([x_lo, chip]).astype(jnp.int32)
    same = jnp.arange(2)[:, None, None, None] == x_lo
    lane = jnp.arange(128)[None, :]
    lanes_c = (jnp.arange(24)[:, None] >= 16) & (lane >= 64)
    weights = call(prepare, [((256, 2048), BF16), ((2, 256, 1024), BF16)], tensor)
    sent, own = call(first_kernel, MESSAGES, place, *factors, *weights)
    for step in range(ITERS):
        got = lax.all_to_all(sent, NEAR, 0, 0).reshape(2, 4, 24, 128)
        near = got.sum(1)
        mine = lax.dynamic_index_in_dim(near, x_lo, 0, False)
        other = lax.dynamic_index_in_dim(near, 1 - x_lo, 0, False)
        for_row = jnp.where(lanes_c, mine + other, mine)
        across = lax.dynamic_index_in_dim(got, 1 - x_lo, 0, False)
        for_col = own + lax.dynamic_index_in_dim(across, chip, 0, False)
        for_row = sum_over(for_row, "z", size_z)
        for_col = sum_over(jnp.where(lanes_c, for_row, for_col), "y", size_y)
        for_row = jnp.where(lanes_c, for_col, for_row)
        sent = jnp.where(same, for_row[None, None], for_col[None, None])
        sent = jnp.broadcast_to(sent, (2, 4, 24, 128)).reshape(8, 24, 128)
        got = lax.all_to_all(sent, NEAR, 0, 0)
        if step < ITERS - 1:
            *factors, sent, own = call(middle_kernel, FACTORS + MESSAGES, place, got, for_col, *factors, *weights)
        else:
            factors = call(last_kernel, FACTORS, place, got, for_col, *factors)
    return tuple(factors)


def solution(mesh):
    rows, cols = mesh.devices.shape
    devices = mesh.devices.reshape(2, rows // 4, 2, cols // 2, 2)
    fine = Mesh(devices, ("x_hi", "z", "core", "y", "x_lo"))
    row, col = (("x_hi", "z", "core"), ("y", "x_lo"))
    in_specs = (P(None, row, col), P(None, row), P(None, col), P())
    out_specs = (P(None, row), P(None, col), P())
    body = functools.partial(shards, rows // 4, cols // 2)
    return jax.shard_map(body, mesh=fine, in_specs=in_specs, out_specs=out_specs, check_vma=False)
```

time: 313 us -> 265 us (0.85)
  blocking collectives: 157 us -> 202 us
  waiting for transfers between devices: 54.1 us -> 20.1 us
  matrix products: 30.2 us -> 0 us
  starting transfers between devices: 39.4 us -> 22.6 us
  between operations: 14.3 us -> 0.83 us
  Pallas kernels: 0 us -> 11.1 us
  other arithmetic: 8.92 us -> 2.14 us
  local copies, waits for them, and re-layouts: 7.89 us -> 4.18 us
    all_to_all x0 -> x6, blocking collectives: none -> 62.6 us  [shards(): got = lax.all_to_all(sent, NEAR, 0, 0)]
    all_to_all x10 -> x5, blocking collectives: 92.1 us -> 40.2 us  [shards(): got = lax.all_to_all(sent, NEAR, 0, 0).reshape(2, 4, 24, 128)]
    all_to_all x6 -> x10, blocking collectives: 64.5 us -> 99.4 us  [sum_over(): return lax.all_to_all(copies, axis, 0, 0).sum(0)]
    dot_general x66 -> x0, matrix products: 30.2 us -> none  [the longest x18 7.61 us: gram(): return jnp.dot(factor, factor.T, precision=HP)]
    all_to_all x6 -> x2, waiting for transfers between devices: 44.4 us -> 15.2 us  [sum_over(): return lax.all_to_all(copies, axis, 0, 0).sum(0)]
    pallas_call x0 -> x8, Pallas kernels: none -> 11.1 us  [call(): pl.pallas_call(kernel, out_shape=shapes, in_specs=specs, out_specs=[VMEM]...]
    all_to_all x6 -> x2, starting transfers between devices: 22.5 us -> 12.5 us  [sum_over(): return lax.all_to_all(copies, axis, 0, 0).sum(0)]
    all_to_all x2 -> x1, starting transfers between devices: 17 us -> 10.1 us  [shards(): got = lax.all_to_all(sent, NEAR, 0, 0).reshape(2, 4, 24, 128)]
  transfers between devices with their start and end apart: 8 -> 3, of which waited for: 8 -> 3; matrix products, arithmetic and copies ran while one was open for 0% -> 0% of each run, Pallas kernels for 0% -> 0%
where the time goes in v3:
time: 265 us; the launch traced here: 263 us
  blocking collectives  202 us (76%)
  starting transfers between devices  22.6 us (9%)
  waiting for transfers between devices  20.1 us (8%)
  Pallas kernels  11.1 us (4%)
  local copies, waits for them, and re-layouts  4.18 us (2%)
    all_to_all x10, blocking collectives, sum_over(): return lax.all_to_all(copies, axis, 0, 0).sum(0)  99.4 us
    all_to_all x6, blocking collectives, shards(): got = lax.all_to_all(sent, NEAR, 0, 0)  62.6 us
    all_to_all x5, blocking collectives, shards(): got = lax.all_to_all(sent, NEAR, 0, 0).reshape(2, 4, 24, 128)  40.2 us
    all_to_all x2, waiting for transfers between devices, sum_over(): return lax.all_to_all(copies, axis, 0, 0).sum(0)  15.2 us
    all_to_all x2, starting transfers between devices, sum_over(): return lax.all_to_all(copies, axis, 0, 0).sum(0)  12.5 us
    pallas_call x8, Pallas kernels, call(): pl.pallas_call(kernel, out_shape=shapes, in_specs=specs, out_specs=[VMEM]...  11.1 us
    all_to_all x1, starting transfers between devices, shards(): got = lax.all_to_all(sent, NEAR, 0, 0).reshape(2, 4, 24, 128)  10.1 us
  transfers between devices with their start and end apart: 3, of which 3 were waited for; matrix products, arithmetic and copies ran while one was open for 0% of the time, Pallas kernels for 0%

profile of v3, /device:TPU:1, one launch (start us, length us, event | category | flops | bytes accessed | tf_op | source)
XLA Modules:
  0.0 263.3 jit_solution(13404776740566798997)
XLA Ops:
  0.6 0.7 copy-done.3
  1.3 0.1 copy.10.fc_ref
  1.4 1.2 copy-done
  2.6 0.6 shard_map.67
  3.2 0.1 pad_add_fusion.place_ref
  3.3 0.1 copy-done.1
  3.4 1.8 shard_map.68
  5.2 10.1 %all-to-all-start = ((f32[8,24,128]{2,1,0:T(8,128)}), f32[8,24,128]{2,1,0:T(8,128)S(1)}, u32[]{:S(2)}, u32[]{:S(2)}) async-start(f32[8,24,128]{2,1,0:T(8,128)} %get-tuple-element.34), calls=%async_computation | async-start | bytes 196608 | tf_op jit(solution)/shard_map/all_to_all | solution.py:151
  15.3 4.9 %all-to-all-done = f32[8,24,128]{2,1,0:T(8,128)S(1)} async-done(((f32[8,24,128]{2,1,0:T(8,128)}), f32[8,24,128]{2,1,0:T(8,128)S(1)}, u32[]{:S(2)}, u32[]{:S(2)}) %all-to-all-start) | async-done | bytes 98336 | tf_op jit(solution)/shard_map/all_to_all | solution.py:151
  20.2 0.1 fusion
  20.3 0.6 broadcast_in_dim.220
  20.9 5.7 %all-to-all-start.1 = ((f32[8,24,128]{2,1,0:T(8,128)}), f32[8,24,128]{2,1,0:T(8,128)S(1)}, u32[]{:S(2)}, u32[]{:S(2)}) async-start(f32[8,24,128]{2,1,0:T(8,128)} %broadcast_in_dim.220), calls=%async_computation.1 | async-start | bytes 196608 | tf_op jit(solution)/shard_map/all_to_all | solution.py:133
  26.6 7.7 %all-to-all-done.1 = f32[8,24,128]{2,1,0:T(8,128)S(1)} async-done(((f32[8,24,128]{2,1,0:T(8,128)}), f32[8,24,128]{2,1,0:T(8,128)S(1)}, u32[]{:S(2)}, u32[]{:S(2)}) %all-to-all-start.1) | async-done | bytes 98336 | tf_op jit(solution)/shard_map/all_to_all | solution.py:133
  34.3 0.1 and_select_fusion.11
  34.4 0.6 broadcast_in_dim.221
  35.0 6.8 %all-to-all-start.2 = ((f32[8,24,128]{2,1,0:T(8,128)}), f32[8,24,128]{2,1,0:T(8,128)S(1)}, u32[]{:S(2)}, u32[]{:S(2)}) async-start(f32[8,24,128]{2,1,0:T(8,128)} %broadcast_in_dim.221), calls=%async_computation.2 | async-start | bytes 196608 | tf_op jit(solution)/shard_map/all_to_all | solution.py:133
  41.8 7.6 %all-to-all-done.2 = f32[8,24,128]{2,1,0:T(8,128)S(1)} async-done(((f32[8,24,128]{2,1,0:T(8,128)}), f32[8,24,128]{2,1,0:T(8,128)S(1)}, u32[]{:S(2)}, u32[]{:S(2)}) %all-to-all-start.2) | async-done | bytes 98336 | tf_op jit(solution)/shard_map/all_to_all | solution.py:133
  49.4 0.1 and_select_fusion.10
  49.5 0.1 broadcast_select_fusion.5
  49.6 10.8 %all_to_all.120.got_ref = f32[8,24,128]{2,1,0:T(8,128)S(1)} all-to-all(f32[8,24,128]{2,1,0:T(8,128)S(1)} %bitcast.62), channel_id=1, replica_groups=mesh['x_hi'=2,'z'=8,'core'=2,'y'=8,'x_lo'=2] {'x_lo','x_hi','core'}, dimensions={0} | all-to-all | bytes 196608 | tf_op jit(solution)/shard_map/all_to_all | solution.py:163
  60.4 1.5 shard_map.69
  61.8 8.0 %all_to_all.121 = f32[8,24,128]{2,1,0:T(8,128)S(1)} all-to-all(f32[8,24,128]{2,1,0:T(8,128)S(1)} %get-tuple-element.36), channel_id=1, replica_groups=mesh['x_hi'=2,'z'=8,'core'=2,'y'=8,'x_lo'=2] {'x_lo','x_hi','core'}, dimensions={0} | all-to-all | bytes 196608 | tf_op jit(solution)/shard_map/all_to_all | solution.py:151
  69.9 0.1 fusion.1
  70.0 9.8 %all_to_all.122 = f32[8,24,128]{2,1,0:T(8,128)S(1)} all-to-all(f32[8,24,128]{2,1,0:T(8,128)S(1)} %broadcast_in_dim.226), channel_id=1, replica_groups=mesh['x_hi'=2,'z'=8,'core'=2,'y'=8,'x_lo'=2] {'z'}, dimensions={0} | all-to-all | bytes 196608 | tf_op jit(solution)/shard_map/all_to_all | solution.py:133
  79.8 0.1 and_select_fusion.9
  79.9 10.1 %all_to_all.123 = f32[8,24,128]{2,1,0:T(8,128)S(1)} all-to-all(f32[8,24,128]{2,1,0:T(8,128)S(1)} %broadcast_in_dim.227), channel_id=1, replica_groups=mesh['x_hi'=2,'z'=8,'core'=2,'y'=8,'x_lo'=2] {'y'}, dimensions={0} | all-to-all | bytes 196608 | tf_op jit(solution)/shard_map/all_to_all | solution.py:133
  90.0 0.1 and_select_fusion.8
  90.1 0.1 broadcast_select_fusion.4
  90.2 10.4 %all_to_all.124.got_ref = f32[8,24,128]{2,1,0:T(8,128)S(1)} all-to-all(f32[8,24,128]{2,1,0:T(8,128)S(1)} %bitcast.63), channel_id=1, replica_groups=mesh['x_hi'=2,'z'=8,'core'=2,'y'=8,'x_lo'=2] {'x_lo','x_hi','core'}, dimensions={0} | all-to-all | bytes 196608 | tf_op jit(solution)/shard_map/all_to_all | solution.py:163
  100.5 1.4 shard_map.70
  102.0 8.0 %all_to_all.125 = f32[8,24,128]{2,1,0:T(8,128)S(1)} all-to-all(f32[8,24,128]{2,1,0:T(8,128)S(1)} %get-tuple-element.41), channel_id=1, replica_groups=mesh['x_hi'=2,'z'=8,'core'=2,'y'=8,'x_lo'=2] {'x_lo','x_hi','core'}, dimensions={0} | all-to-all | bytes 196608 | tf_op jit(solution)/shard_map/all_to_all | solution.py:151
  110.0 0.1 fusion.2
  110.1 9.8 %all_to_all.126 = f32[8,24,128]{2,1,0:T(8,128)S(1)} all-to-all(f32[8,24,128]{2,1,0:T(8,128)S(1)} %broadcast_in_dim.232), channel_id=1, replica_groups=mesh['x_hi'=2,'z'=8,'core'=2,'y'=8,'x_lo'=2] {'z'}, dimensions={0} | all-to-all | bytes 196608 | tf_op jit(solution)/shard_map/all_to_all | solution.py:133
  120.0 0.1 and_select_fusion.7
  120.1 10.1 %all_to_all.127 = f32[8,24,128]{2,1,0:T(8,128)S(1)} all-to-all(f32[8,24,128]{2,1,0:T(8,128)S(1)} %broadcast_in_dim.233), channel_id=1, replica_groups=mesh['x_hi'=2,'z'=8,'core'=2,'y'=8,'x_lo'=2] {'y'}, dimensions={0} | all-to-all | bytes 196608 | tf_op jit(solution)/shard_map/all_to_all | solution.py:133
  130.1 0.1 and_select_fusion.6
  130.2 0.1 broadcast_select_fusion.3
  130.3 10.4 %all_to_all.128.got_ref = f32[8,24,128]{2,1,0:T(8,128)S(1)} all-to-all(f32[8,24,128]{2,1,0:T(8,128)S(1)} %bitcast.64), channel_id=1, replica_groups=mesh['x_hi'=2,'z'=8,'core'=2,'y'=8,'x_lo'=2] {'x_lo','x_hi','core'}, dimensions={0} | all-to-all | bytes 196608 | tf_op jit(solution)/shard_map/all_to_all | solution.py:163
  140.7 1.4 shard_map.71
  142.1 8.0 %all_to_all.129 = f32[8,24,128]{2,1,0:T(8,128)S(1)} all-to-all(f32[8,24,128]{2,1,0:T(8,128)S(1)} %get-tuple-element.46), channel_id=1, replica_groups=mesh['x_hi'=2,'z'=8,'core'=2,'y'=8,'x_lo'=2] {'x_lo','x_hi','core'}, dimensions={0} | all-to-all | bytes 196608 | tf_op jit(solution)/shard_map/all_to_all | solution.py:151
  150.2 0.1 fusion.3
  150.3 9.8 %all_to_all.130 = f32[8,24,128]{2,1,0:T(8,128)S(1)} all-to-all(f32[8,24,128]{2,1,0:T(8,128)S(1)} %broadcast_in_dim.238), channel_id=1, replica_groups=mesh['x_hi'=2,'z'=8,'core'=2,'y'=8,'x_lo'=2] {'z'}, dimensions={0} | all-to-all | bytes 196608 | tf_op jit(solution)/shard_map/all_to_all | solution.py:133
  160.1 0.1 and_select_fusion.5
  160.2 10.1 %all_to_all.131 = f32[8,24,128]{2,1,0:T(8,128)S(1)} all-to-all(f32[8,24,128]{2,1,0:T(8,128)S(1)} %broadcast_in_dim.239), channel_id=1, replica_groups=mesh['x_hi'=2,'z'=8,'core'=2,'y'=8,'x_lo'=2] {'y'}, dimensions={0} | all-to-all | bytes 196608 | tf_op jit(solution)/shard_map/all_to_all | solution.py:133
  170.4 0.1 broadcast_select_fusion.2
  170.5 10.4 %all_to_all.132.got_ref = f32[8,24,128]{2,1,0:T(8,128)S(1)} all-to-all(f32[8,24,128]{2,1,0:T(8,128)S(1)} %bitcast.65), channel_id=1, replica_groups=mesh['x_hi'=2,'z'=8,'core'=2,'y'=8,'x_lo'=2] {'x_lo','x_hi','core'}, dimensions={0} | all-to-all | bytes 196608 | tf_op jit(solution)/shard_map/all_to_all | solution.py:163
  180.8 1.5 shard_map.72
  182.3 8.0 %all_to_all.133 = f32[8,24,128]{2,1,0:T(8,128)S(1)} all-to-all(f32[8,24,128]{2,1,0:T(8,128)S(1)} %get-tuple-element.51), channel_id=1, replica_groups=mesh['x_hi'=2,'z'=8,'core'=2,'y'=8,'x_lo'=2] {'x_lo','x_hi','core'}, dimensions={0} | all-to-all | bytes 196608 | tf_op jit(solution)/shard_map/all_to_all | solution.py:151
  190.3 0.1 fusion.4
  190.4 9.8 %all_to_all.134 = f32[8,24,128]{2,1,0:T(8,128)S(1)} all-to-all(f32[8,24,128]{2,1,0:T(8,128)S(1)} %broadcast_in_dim.244), channel_id=1, replica_groups=mesh['x_hi'=2,'z'=8,'core'=2,'y'=8,'x_lo'=2] {'z'}, dimensions={0} | all-to-all | bytes 196608 | tf_op jit(solution)/shard_map/all_to_all | solution.py:133
  200.3 0.1 and_select_fusion.3
  200.4 10.1 %all_to_all.135 = f32[8,24,128]{2,1,0:T(8,128)S(1)} all-to-all(f32[8,24,128]{2,1,0:T(8,128)S(1)} %broadcast_in_dim.245), channel_id=1, replica_groups=mesh['x_hi'=2,'z'=8,'core'=2,'y'=8,'x_lo'=2] {'y'}, dimensions={0} | all-to-all | bytes 196608 | tf_op jit(solution)/shard_map/all_to_all | solution.py:133
  210.5 0.1 broadcast_select_fusion.1
  210.6 10.4 %all_to_all.136.got_ref = f32[8,24,128]{2,1,0:T(8,128)S(1)} all-to-all(f32[8,24,128]{2,1,0:T(8,128)S(1)} %bitcast.66), channel_id=1, replica_groups=mesh['x_hi'=2,'z'=8,'core'=2,'y'=8,'x_lo'=2] {'x_lo','x_hi','core'}, dimensions={0} | all-to-all | bytes 196608 | tf_op jit(solution)/shard_map/all_to_all | solution.py:163
  221.0 1.5 shard_map.73
  222.4 8.0 %all_to_all.137 = f32[8,24,128]{2,1,0:T(8,128)S(1)} all-to-all(f32[8,24,128]{2,1,0:T(8,128)S(1)} %get-tuple-element.56), channel_id=1, replica_groups=mesh['x_hi'=2,'z'=8,'core'=2,'y'=8,'x_lo'=2] {'x_lo','x_hi','core'}, dimensions={0} | all-to-all | bytes 196608 | tf_op jit(solution)/shard_map/all_to_all | solution.py:151
  230.5 0.1 fusion.5
  230.6 9.8 %all_to_all.138 = f32[8,24,128]{2,1,0:T(8,128)S(1)} all-to-all(f32[8,24,128]{2,1,0:T(8,128)S(1)} %broadcast_in_dim.250), channel_id=1, replica_groups=mesh['x_hi'=2,'z'=8,'core'=2,'y'=8,'x_lo'=2] {'z'}, dimensions={0} | all-to-all | bytes 196608 | tf_op jit(solution)/shard_map/all_to_all | solution.py:133
  240.4 0.1 and_select_fusion.1
  240.5 10.1 %all_to_all.139 = f32[8,24,128]{2,1,0:T(8,128)S(1)} all-to-all(f32[8,24,128]{2,1,0:T(8,128)S(1)} %broadcast_in_dim.251), channel_id=1, replica_groups=mesh['x_hi'=2,'z'=8,'core'=2,'y'=8,'x_lo'=2] {'y'}, dimensions={0} | all-to-all | bytes 196608 | tf_op jit(solution)/shard_map/all_to_all | solution.py:133
  250.6 0.1 broadcast_select_fusion
  250.7 10.4 %all_to_all.140.got_ref = f32[8,24,128]{2,1,0:T(8,128)S(1)} all-to-all(f32[8,24,128]{2,1,0:T(8,128)S(1)} %bitcast.67), channel_id=1, replica_groups=mesh['x_hi'=2,'z'=8,'core'=2,'y'=8,'x_lo'=2] {'x_lo','x_hi','core'}, dimensions={0} | all-to-all | bytes 196608 | tf_op jit(solution)/shard_map/all_to_all | solution.py:163
  261.1 1.5 shard_map.74
  262.6 0.7 copy.12
  (45 shorter events, 0.6 us)
Async XLA Ops:
  0.6 0.7 copy-start.3
  1.4 1.2 copy-start
  2.6 0.8 copy-start.1
  2.6 0.8 copy-start.2
  5.2 15.0 %all-to-all-start = ((f32[8,24,128]{2,1,0:T(8,128)}), f32[8,24,128]{2,1,0:T(8,128)S(1)}, u32[]{:S(2)}, u32[]{:S(2)}) async-start(f32[8,24,128]{2,1,0:T(8,128)} %get-tuple-element.34), calls=%async_computation | async-start | bytes 196608 | tf_op jit(solution)/shard_map/all_to_all | solution.py:151
  20.9 13.4 %all-to-all-start.1 = ((f32[8,24,128]{2,1,0:T(8,128)}), f32[8,24,128]{2,1,0:T(8,128)S(1)}, u32[]{:S(2)}, u32[]{:S(2)}) async-start(f32[8,24,128]{2,1,0:T(8,128)} %broadcast_in_dim.220), calls=%async_computation.1 | async-start | bytes 196608 | tf_op jit(solution)/shard_map/all_to_all | solution.py:133
  35.0 14.4 %all-to-all-start.2 = ((f32[8,24,128]{2,1,0:T(8,128)}), f32[8,24,128]{2,1,0:T(8,128)S(1)}, u32[]{:S(2)}, u32[]{:S(2)}) async-start(f32[8,24,128]{2,1,0:T(8,128)} %broadcast_in_dim.221), calls=%async_computation.2 | async-start | bytes 196608 | tf_op jit(solution)/shard_map/all_to_all | solution.py:133

commit v4 on v3

v4 whole, which is shorter than its diff:
```python
import functools

import jax
import jax.numpy as jnp
from jax import lax
from jax.experimental import pallas as pl
from jax.experimental.pallas import tpu as pltpu
from jax.sharding import Mesh, PartitionSpec as P

ITERS = 6

HP = lax.Precision.HIGHEST
F32, BF16 = (jnp.float32, jnp.bfloat16)
VMEM = pl.BlockSpec(memory_space=pltpu.VMEM)
SMEM = pl.BlockSpec(memory_space=pltpu.SMEM)


def product(a, b, contract=(1, 0), precision=HP):
    dims = (((contract[0],), (contract[1],)), ((), ()))
    return lax.dot_general(a, b, dims, precision=precision, preferred_element_type=F32)


def split(x):
    high = x.astype(BF16)
    return high, (x - high.astype(F32)).astype(BF16)


def inverse_norm(matrix):
    return 1.0 / jnp.sqrt(jnp.sum(matrix * matrix, keepdims=True) + 1e-06)


def descend(factor, hessian, contraction):
    return factor - inverse_norm(hessian) * (product(hessian, factor) - contraction)


def prepare(t_ref, wz_ref, wy_ref):
    for k in range(8):
        high, low = split(t_ref[k])
        wz_ref[:128, 256 * k : 256 * k + 256] = high
        wz_ref[128:, 256 * k : 256 * k + 256] = low
        high, low = split(t_ref[k].T)
        wy_ref[0, :, 128 * k : 128 * k + 128] = high
        wy_ref[1, :, 128 * k : 128 * k + 128] = low


def pack(square):
    tiles = [square[8 * q : 8 * q + 8] for q in range(4)]
    return tiles[0] + sum(pltpu.roll(tiles[q], 32 * q, 1) for q in range(1, 4))


def unpack(tile, width):
    return jnp.concatenate([tile[:, 32 * q : 32 * q + width] for q in range(4)], 0)


def widen(x):
    return jnp.concatenate([x, jnp.zeros((128 - x.shape[0], x.shape[1]), F32)], 0)


def update(core, both_ref, fa, fb, fc):
    rows, cols = (both_ref[0], both_ref[1])
    mode_a = jnp.where(core == 0, cols[:32], cols[32:64])
    mode_b = jnp.concatenate([rows[:32], rows[32:64]], 1)
    gram_a, gram_b = (unpack(rows[64:72], 32), unpack(cols[64:72], 32))
    gram_c = product(fc, fc, (1, 1))
    next_a = descend(fa, gram_b * gram_c, mode_a)
    next_b = descend(fb, gram_a * gram_c, mode_b)
    h_c = gram_a * gram_b
    scale = inverse_norm(h_c)
    return next_a, next_b, fc - scale * product(h_c, fc), scale


def add_mode_c(base, scale, ring_ref):
    total = ring_ref[0]
    for n in range(1, ring_ref.shape[0] // 2):
        total += ring_ref[2 * n]
    return base + scale * unpack(total, 8)


def multiply(fa, fb, wz_ref, wy_ref):
    a_high, a_low = split(fa)
    b_high, b_low = split(fb)
    left = jnp.concatenate([jnp.concatenate([a_high, a_high], 1), jnp.concatenate([a_low, jnp.zeros_like(a_low)], 1)], 0)
    z = product(left, wz_ref[...], precision=None)
    z = z[:32] + z[32:]
    y = product(jnp.concatenate([b_high, b_low], 0), wy_ref[0], precision=None)
    y = y[:32] + y[32:] + product(b_high, wy_ref[1], precision=None)
    lane = lax.broadcasted_iota(jnp.int32, (32, 128), 1)
    part_c = jnp.zeros((32, 128), F32)
    for k in range(8):
        part_c = jnp.where(lane == k, jnp.sum(y[:, 128 * k : 128 * k + 128] * fa, 1, keepdims=True), part_c)
    gram_a = product(fa, widen(fa), (1, 1))
    gram_b = product(fb, widen(fb), (1, 1))
    return y, z, pack(gram_a), pack(gram_b), pack(part_c)


def message(fc, y, z, gram_a, gram_b, part_c, sent_ref):
    part_a = jnp.zeros((32, 128), F32)
    part_b = jnp.zeros((32, 256), F32)
    for k in range(8):
        weight = fc[:, k : k + 1]
        part_a += weight * y[:, 128 * k : 128 * k + 128]
        part_b += weight * z[:, 256 * k : 256 * k + 256]
    for n in range(4):
        sent_ref[2 * n, 0:32] = part_b[:, :128]
        sent_ref[2 * n, 32:64] = part_b[:, 128:]
        sent_ref[2 * n, 64:72] = gram_a
        sent_ref[2 * n, 72:80] = part_c
        sent_ref[2 * n + 1, 0:32] = part_a
        sent_ref[2 * n + 1, 32:64] = jnp.zeros((32, 128), F32)
        sent_ref[2 * n + 1, 64:72] = gram_b
        sent_ref[2 * n + 1, 72:80] = part_c


def first_kernel(fa_ref, fb_ref, fc_ref, wz_ref, wy_ref, sent_ref):
    message(fc_ref[...], *multiply(fa_ref[...], fb_ref[...], wz_ref, wy_ref), sent_ref)


def near_kernel(place_ref, got_ref, out_ref):
    x_hi, x_lo, core = (place_ref[0], place_ref[1], place_ref[2])
    rows = [got_ref[4 * h + 2 * x_lo + c, 0:72] for h in range(2) for c in range(2)]
    rows = (rows[0] + rows[1]) + (rows[2] + rows[3])
    at = 4 * x_hi
    block_0 = got_ref[at, 0:32] + got_ref[at + 2, 0:32]
    block_1 = got_ref[at + 1, 0:32] + got_ref[at + 3, 0:32]
    gram_b = got_ref[at + 1, 64:72] + got_ref[at + 3, 64:72]
    cols = jnp.concatenate([block_0, block_1, gram_b], 0)
    part_c = got_ref[0, 72:80]
    for n in range(1, 8):
        part_c += got_ref[n, 72:80]
    out = jnp.where(core == 0, rows, cols)
    for n in range(out_ref.shape[0]):
        out_ref[n, 0:72] = out
        out_ref[n, 72:80] = part_c


def ring_kernel(got_ref, sum_ref, ring_ref):
    total = got_ref[0]
    for n in range(1, got_ref.shape[0]):
        total += got_ref[n]
    sum_ref[...] = total[:72]
    for n in range(ring_ref.shape[0]):
        ring_ref[n] = total[72:]


def factor_kernel(place_ref, both_ref, fa_ref, fb_ref, fc_ref, wz_ref, wy_ref, na_ref, nb_ref, base_ref, scale_ref, y_ref, z_ref, packs_ref):
    fa, fb, base, scale = update(place_ref[2], both_ref, fa_ref[...], fb_ref[...], fc_ref[...])
    na_ref[...] = fa
    nb_ref[...] = fb
    base_ref[...] = base
    scale_ref[...] = jnp.broadcast_to(scale, (8, 128))
    y, z, *packs = multiply(fa, fb, wz_ref, wy_ref)
    y_ref[...] = y
    z_ref[...] = z
    for n in range(3):
        packs_ref[n] = packs[n]


def send_kernel(ring_ref, base_ref, scale_ref, y_ref, z_ref, packs_ref, nc_ref, sent_ref):
    fc = add_mode_c(base_ref[...], scale_ref[:1, :1], ring_ref)
    nc_ref[...] = fc
    message(fc, y_ref[...], z_ref[...], packs_ref[0], packs_ref[1], packs_ref[2], sent_ref)


def last_kernel(place_ref, both_ref, ring_ref, fa_ref, fb_ref, fc_ref, na_ref, nb_ref, nc_ref):
    fa, fb, base, scale = update(place_ref[2], both_ref, fa_ref[...], fb_ref[...], fc_ref[...])
    na_ref[...] = fa
    nb_ref[...] = fb
    nc_ref[...] = add_mode_c(base, scale, ring_ref)


def call(kernel, outs, *args):
    shapes = [jax.ShapeDtypeStruct(s, d) for s, d in outs]
    specs = [SMEM if a.dtype == jnp.int32 else VMEM for a in args]
    params = pltpu.CompilerParams(vmem_limit_bytes=16 * 1024 * 1024)
    cost = pl.CostEstimate(flops=100_000_000, bytes_accessed=4_000_000, transcendentals=0)
    return pl.pallas_call(kernel, out_shape=shapes, in_specs=specs, out_specs=[VMEM] * len(shapes), compiler_params=params, cost_estimate=cost)(*args)


A, B, C = (((32, 128), F32), ((32, 256), F32), ((32, 8), F32))
SENT = ((8, 80, 128), F32)
PRODUCTS = [((8, 128), F32), ((32, 1024), F32), ((32, 2048), F32), ((3, 8, 128), F32)]
NEAR = ("x_hi", "x_lo", "core")
ALL = ("x_hi", "z", "core", "y", "x_lo")


def rings(size_z, size_y):
    def at(x_hi, z, core, y, x_lo):
        return (((x_hi * size_z + z) * 2 + core) * size_y + y) * 2 + x_lo

    pairs = [(x_hi, x_lo) for x_hi in range(2) for x_lo in range(2)]
    along_z = [[at(h, z, 0, y, l) for z in range(size_z)] for h, l in pairs for y in range(size_y)]
    along_y = [[at(h, z, 1, y, l) for y in range(size_y)] for h, l in pairs for z in range(size_z)]
    return along_z + along_y


def shards(size_z, size_y, tensor, factor_a, factor_b, factor_c):
    fa, fb, fc = (factor_a, factor_b, factor_c)
    place = jnp.stack([lax.axis_index(name) for name in NEAR]).astype(jnp.int32)
    groups = rings(size_z, size_y)
    weights = call(prepare, [((256, 2048), BF16), ((2, 256, 1024), BF16)], tensor)
    (sent,) = call(first_kernel, [SENT], fa, fb, fc, *weights)
    for step in range(ITERS):
        got = lax.all_to_all(sent, NEAR, 0, 0)
        (sent,) = call(near_kernel, [((size_z, 80, 128), F32)], place, got)
        got = lax.all_to_all(sent, ALL, 0, 0, axis_index_groups=groups)
        sums, ring = call(ring_kernel, [((72, 128), F32), ((2 * size_y, 8, 128), F32)], got)
        ring = lax.all_to_all(ring, ("y", "core"), 0, 0)
        both = lax.all_gather(sums, "core")
        if step < ITERS - 1:
            fa, fb, *rest = call(factor_kernel, [A, B, C] + PRODUCTS, place, both, fa, fb, fc, *weights)
            fc, sent = call(send_kernel, [C, SENT], ring, *rest)
        else:
            fa, fb, fc = call(last_kernel, [A, B, C], place, both, ring, fa, fb, fc)
    return (fa, fb, fc)


def solution(mesh):
    rows, cols = mesh.devices.shape
    devices = mesh.devices.reshape(2, rows // 4, 2, cols // 2, 2)
    fine = Mesh(devices, ("x_hi", "z", "core", "y", "x_lo"))
    row, col = (("x_hi", "z", "core"), ("y", "x_lo"))
    in_specs = (P(None, row, col), P(None, row), P(None, col), P())
    out_specs = (P(None, row), P(None, col), P())
    body = functools.partial(shards, rows // 4, cols // 2)
    return jax.shard_map(body, mesh=fine, in_specs=in_specs, out_specs=out_specs, check_vma=False)
```

time: 265 us -> 244 us (0.921)
  blocking collectives: 202 us -> 137 us
  starting transfers between devices: 22.6 us -> 47.3 us
  waiting for transfers between devices: 20.1 us -> 35.7 us
  Pallas kernels: 11.1 us -> 19 us
    all_to_all x15 -> x6, blocking collectives: 140 us -> 75.9 us  [shards(): got = lax.all_to_all(sent, ALL, 0, 0, axis_index_groups=groups)]
    all_to_all x3 -> x7, starting transfers between devices: 22.6 us -> 47.3 us  [the longest x6 37.1 us: shards(): ring = lax.all_to_all(ring, ('y', 'core'), 0, 0)]
    all_to_all x3 -> x7, waiting for transfers between devices: 20.1 us -> 35.7 us  [the longest x6 28.7 us: shards(): ring = lax.all_to_all(ring, ('y', 'core'), 0, 0)]
    all_to_all x6 -> x5, blocking collectives: 62.6 us -> 50.1 us  [shards(): got = lax.all_to_all(sent, NEAR, 0, 0)]
    all_gather x0 -> x6, blocking collectives: none -> 11.1 us  [shards(): both = lax.all_gather(sums, 'core')]
    pallas_call x8 -> x25, Pallas kernels: 11.1 us -> 19 us  [call(): pl.pallas_call(kernel, out_shape=shapes, in_specs=specs, out_specs=[VMEM]...]
  transfers between devices with their start and end apart: 3 -> 7, of which waited for: 3 -> 7; matrix products, arithmetic and copies ran while one was open for 0% -> 0% of each run, Pallas kernels for 0% -> 3%
where the time goes in v4:
time: 244 us; the launch traced here: 243 us
  blocking collectives  137 us (56%)
  starting transfers between devices  47.3 us (19%)
  waiting for transfers between devices  35.7 us (15%)
  Pallas kernels  19 us (8%)
  local copies, waits for them, and re-layouts  2.84 us (1%)
    all_to_all x6, blocking collectives, shards(): got = lax.all_to_all(sent, ALL, 0, 0, axis_index_groups=groups)  75.9 us
    all_to_all x5, blocking collectives, shards(): got = lax.all_to_all(sent, NEAR, 0, 0)  50.1 us
    all_to_all x6, starting transfers between devices, shards(): ring = lax.all_to_all(ring, ('y', 'core'), 0, 0)  37.1 us
    all_to_all x6, waiting for transfers between devices, shards(): ring = lax.all_to_all(ring, ('y', 'core'), 0, 0)  28.7 us
    pallas_call x25, Pallas kernels, call(): pl.pallas_call(kernel, out_shape=shapes, in_specs=specs, out_specs=[VMEM]...  19 us
    all_gather x6, blocking collectives, shards(): both = lax.all_gather(sums, 'core')  11.1 us
    all_to_all x1, starting transfers between devices, shards(): got = lax.all_to_all(sent, NEAR, 0, 0)  10.2 us
    all_to_all x1, waiting for transfers between devices, shards(): got = lax.all_to_all(sent, NEAR, 0, 0)  7.06 us
  transfers between devices with their start and end apart: 7, of which 7 were waited for; matrix products, arithmetic and copies ran while one was open for 0% of the time, Pallas kernels for 3%

profile of v4, /device:TPU:1, one launch (start us, length us, event | category | flops | bytes accessed | tf_op | source)
XLA Modules:
  0.0 242.8 jit_solution(2642295602477718906)
XLA Ops:
  0.6 0.8 copy.7.fc_ref
  1.4 0.0 copy-start
  1.4 1.2 copy-done
  2.6 0.0 copy-start.1
  2.6 0.6 shard_map.67
  3.2 0.2 copy-done.1
  3.4 0.0 copy-done.2
  3.4 1.4 shard_map.68
  4.8 10.2 %all-to-all-start = ((f32[8,80,128]{2,1,0:T(8,128)}), f32[8,80,128]{2,1,0:T(8,128)S(1)}, u32[]{:S(2)}, u32[]{:S(2)}) async-start(f32[8,80,128]{2,1,0:T(8,128)} %shard_map.68), calls=%async_computation | async-start | bytes 655360 | tf_op jit(solution)/shard_map/all_to_all | solution.py:203
  15.0 0.1 pad_add_fusion.place_ref
  15.1 7.1 %all-to-all-done.got_ref = f32[8,80,128]{2,1,0:T(8,128)S(1)} async-done(((f32[8,80,128]{2,1,0:T(8,128)}), f32[8,80,128]{2,1,0:T(8,128)S(1)}, u32[]{:S(2)}, u32[]{:S(2)}) %all-to-all-start) | async-done | bytes 327712 | tf_op jit(solution)/shard_map/all_to_all | solution.py:203
  22.1 0.6 shard_map.69
  22.7 12.4 %all_to_all.90.got_ref = f32[8,80,128]{2,1,0:T(8,128)S(1)} all-to-all(f32[8,80,128]{2,1,0:T(8,128)S(1)} %shard_map.69), channel_id=1, replica_groups={{0,32,64,96,128,160,192,224},{2,34,66,98,130,162,194,226},{4,36,68,100,..., dimensions={0} | all-to-all | bytes 655360 | tf_op jit(solution)/shard_map/all_to_all | solution.py:205
  35.1 0.6 shard_map.70
  35.8 12.7 %all-to-all-start.2 = ((f32[16,8,128]{2,1,0:T(8,128)}), f32[16,8,128]{2,1,0:T(8,128)S(1)}, u32[]{:S(2)}, u32[]{:S(2)}) async-start(f32[16,8,128]{2,1,0:T(8,128)} %get-tuple-element.64), calls=%async_computation.2 | async-start | bytes 131072 | tf_op jit(solution)/shard_map/all_to_all | solution.py:207
  48.5 1.8 all-gather
  50.3 1.4 shard_map.71
  51.8 4.5 %all-to-all-done.2.ring_ref = f32[16,8,128]{2,1,0:T(8,128)S(1)} async-done(((f32[16,8,128]{2,1,0:T(8,128)}), f32[16,8,128]{2,1,0:T(8,128)S(1)}, u32[]{:S(2)}, u32[]{:S(2)}) %all-to-all-start.2) | async-done | bytes 65568 | tf_op jit(solution)/shard_map/all_to_all | solution.py:207
  56.3 0.2 shard_map.72
  56.5 10.0 %all_to_all.91.got_ref = f32[8,80,128]{2,1,0:T(8,128)S(1)} all-to-all(f32[8,80,128]{2,1,0:T(8,128)S(1)} %get-tuple-element.71), channel_id=1, replica_groups=mesh['x_hi'=2,'z'=8,'core'=2,'y'=8,'x_lo'=2] {'x_hi','x_lo','core'}, dimensions={0} | all-to-all | bytes 655360 | tf_op jit(solution)/shard_map/all_to_all | solution.py:203
  66.5 0.6 shard_map.73
  67.1 12.7 %all_to_all.92.got_ref = f32[8,80,128]{2,1,0:T(8,128)S(1)} all-to-all(f32[8,80,128]{2,1,0:T(8,128)S(1)} %shard_map.73), channel_id=1, replica_groups={{0,32,64,96,128,160,192,224},{2,34,66,98,130,162,194,226},{4,36,68,100,..., dimensions={0} | all-to-all | bytes 655360 | tf_op jit(solution)/shard_map/all_to_all | solution.py:205
  79.8 0.6 shard_map.74
  80.4 4.9 %all-to-all-start.5 = ((f32[16,8,128]{2,1,0:T(8,128)}), f32[16,8,128]{2,1,0:T(8,128)S(1)}, u32[]{:S(2)}, u32[]{:S(2)}) async-start(f32[16,8,128]{2,1,0:T(8,128)} %get-tuple-element.72), calls=%async_computation.5 | async-start | bytes 131072 | tf_op jit(solution)/shard_map/all_to_all | solution.py:207
  85.3 1.8 all-gather.1
  87.2 1.4 shard_map.75
  88.6 4.5 %all-to-all-done.5.ring_ref = f32[16,8,128]{2,1,0:T(8,128)S(1)} async-done(((f32[16,8,128]{2,1,0:T(8,128)}), f32[16,8,128]{2,1,0:T(8,128)S(1)}, u32[]{:S(2)}, u32[]{:S(2)}) %all-to-all-start.5) | async-done | bytes 65568 | tf_op jit(solution)/shard_map/all_to_all | solution.py:207
  93.1 0.2 shard_map.76
  93.3 10.0 %all_to_all.93.got_ref = f32[8,80,128]{2,1,0:T(8,128)S(1)} all-to-all(f32[8,80,128]{2,1,0:T(8,128)S(1)} %get-tuple-element.82), channel_id=1, replica_groups=mesh['x_hi'=2,'z'=8,'core'=2,'y'=8,'x_lo'=2] {'x_hi','x_lo','core'}, dimensions={0} | all-to-all | bytes 655360 | tf_op jit(solution)/shard_map/all_to_all | solution.py:203
  103.4 0.6 shard_map.77
  103.9 12.7 %all_to_all.94.got_ref = f32[8,80,128]{2,1,0:T(8,128)S(1)} all-to-all(f32[8,80,128]{2,1,0:T(8,128)S(1)} %shard_map.77), channel_id=1, replica_groups={{0,32,64,96,128,160,192,224},{2,34,66,98,130,162,194,226},{4,36,68,100,..., dimensions={0} | all-to-all | bytes 655360 | tf_op jit(solution)/shard_map/all_to_all | solution.py:205
  116.6 0.6 shard_map.78
  117.3 4.9 %all-to-all-start.8 = ((f32[16,8,128]{2,1,0:T(8,128)}), f32[16,8,128]{2,1,0:T(8,128)S(1)}, u32[]{:S(2)}, u32[]{:S(2)}) async-start(f32[16,8,128]{2,1,0:T(8,128)} %get-tuple-element.83), calls=%async_computation.8 | async-start | bytes 131072 | tf_op jit(solution)/shard_map/all_to_all | solution.py:207
  122.2 1.8 all-gather.2
  124.0 1.5 shard_map.79
  125.5 4.5 %all-to-all-done.8.ring_ref = f32[16,8,128]{2,1,0:T(8,128)S(1)} async-done(((f32[16,8,128]{2,1,0:T(8,128)}), f32[16,8,128]{2,1,0:T(8,128)S(1)}, u32[]{:S(2)}, u32[]{:S(2)}) %all-to-all-start.8) | async-done | bytes 65568 | tf_op jit(solution)/shard_map/all_to_all | solution.py:207
  130.0 0.2 shard_map.80
  130.2 10.0 %all_to_all.95.got_ref = f32[8,80,128]{2,1,0:T(8,128)S(1)} all-to-all(f32[8,80,128]{2,1,0:T(8,128)S(1)} %get-tuple-element.93), channel_id=1, replica_groups=mesh['x_hi'=2,'z'=8,'core'=2,'y'=8,'x_lo'=2] {'x_hi','x_lo','core'}, dimensions={0} | all-to-all | bytes 655360 | tf_op jit(solution)/shard_map/all_to_all | solution.py:203
  140.2 0.6 shard_map.81
  140.8 12.7 %all_to_all.96.got_ref = f32[8,80,128]{2,1,0:T(8,128)S(1)} all-to-all(f32[8,80,128]{2,1,0:T(8,128)S(1)} %shard_map.81), channel_id=1, replica_groups={{0,32,64,96,128,160,192,224},{2,34,66,98,130,162,194,226},{4,36,68,100,..., dimensions={0} | all-to-all | bytes 655360 | tf_op jit(solution)/shard_map/all_to_all | solution.py:205
  153.5 0.6 shard_map.82
  154.1 4.9 %all-to-all-start.11 = ((f32[16,8,128]{2,1,0:T(8,128)}), f32[16,8,128]{2,1,0:T(8,128)S(1)}, u32[]{:S(2)}, u32[]{:S(2)}) async-start(f32[16,8,128]{2,1,0:T(8,128)} %get-tuple-element.94), calls=%async_computation.11 | async-start | bytes 131072 | tf_op jit(solution)/shard_map/all_to_all | solution.py:207
  159.0 1.8 all-gather.3
  160.9 1.4 shard_map.83
  162.3 4.5 %all-to-all-done.11.ring_ref = f32[16,8,128]{2,1,0:T(8,128)S(1)} async-done(((f32[16,8,128]{2,1,0:T(8,128)}), f32[16,8,128]{2,1,0:T(8,128)S(1)}, u32[]{:S(2)}, u32[]{:S(2)}) %all-to-all-start.11) | async-done | bytes 65568 | tf_op jit(solution)/shard_map/all_to_all | solution.py:207
  166.9 0.2 shard_map.84
  167.1 10.0 %all_to_all.97.got_ref = f32[8,80,128]{2,1,0:T(8,128)S(1)} all-to-all(f32[8,80,128]{2,1,0:T(8,128)S(1)} %get-tuple-element.104), channel_id=1, replica_groups=mesh['x_hi'=2,'z'=8,'core'=2,'y'=8,'x_lo'=2] {'x_hi','x_lo','core'}, dimensions={0} | all-to-all | bytes 655360 | tf_op jit(solution)/shard_map/all_to_all | solution.py:203
  177.1 0.6 shard_map.85
  177.7 12.7 %all_to_all.98.got_ref = f32[8,80,128]{2,1,0:T(8,128)S(1)} all-to-all(f32[8,80,128]{2,1,0:T(8,128)S(1)} %shard_map.85), channel_id=1, replica_groups={{0,32,64,96,128,160,192,224},{2,34,66,98,130,162,194,226},{4,36,68,100,..., dimensions={0} | all-to-all | bytes 655360 | tf_op jit(solution)/shard_map/all_to_all | solution.py:205
  190.4 0.6 shard_map.86
  191.0 4.9 %all-to-all-start.14 = ((f32[16,8,128]{2,1,0:T(8,128)}), f32[16,8,128]{2,1,0:T(8,128)S(1)}, u32[]{:S(2)}, u32[]{:S(2)}) async-start(f32[16,8,128]{2,1,0:T(8,128)} %get-tuple-element.105), calls=%async_computation.14 | async-start | bytes 131072 | tf_op jit(solution)/shard_map/all_to_all | solution.py:207
  195.9 1.8 all-gather.4
  197.7 1.5 shard_map.87
  199.2 4.5 %all-to-all-done.14.ring_ref = f32[16,8,128]{2,1,0:T(8,128)S(1)} async-done(((f32[16,8,128]{2,1,0:T(8,128)}), f32[16,8,128]{2,1,0:T(8,128)S(1)}, u32[]{:S(2)}, u32[]{:S(2)}) %all-to-all-start.14) | async-done | bytes 65568 | tf_op jit(solution)/shard_map/all_to_all | solution.py:207
  203.7 0.2 shard_map.88
  203.9 10.0 %all_to_all.99.got_ref = f32[8,80,128]{2,1,0:T(8,128)S(1)} all-to-all(f32[8,80,128]{2,1,0:T(8,128)S(1)} %get-tuple-element.115), channel_id=1, replica_groups=mesh['x_hi'=2,'z'=8,'core'=2,'y'=8,'x_lo'=2] {'x_hi','x_lo','core'}, dimensions={0} | all-to-all | bytes 655360 | tf_op jit(solution)/shard_map/all_to_all | solution.py:203
  213.9 0.6 shard_map.89
  214.5 12.7 %all_to_all.100.got_ref = f32[8,80,128]{2,1,0:T(8,128)S(1)} all-to-all(f32[8,80,128]{2,1,0:T(8,128)S(1)} %shard_map.89), channel_id=1, replica_groups={{0,32,64,96,128,160,192,224},{2,34,66,98,130,162,194,226},{4,36,68,100,..., dimensions={0} | all-to-all | bytes 655360 | tf_op jit(solution)/shard_map/all_to_all | solution.py:205
  227.2 0.6 shard_map.90
  227.8 4.9 %all-to-all-start.17 = ((f32[16,8,128]{2,1,0:T(8,128)}), f32[16,8,128]{2,1,0:T(8,128)S(1)}, u32[]{:S(2)}, u32[]{:S(2)}) async-start(f32[16,8,128]{2,1,0:T(8,128)} %get-tuple-element.117), calls=%async_computation.17 | async-start | bytes 131072 | tf_op jit(solution)/shard_map/all_to_all | solution.py:207
  232.7 1.8 all-gather.5
  234.6 6.0 %all-to-all-done.17.ring_ref = f32[16,8,128]{2,1,0:T(8,128)S(1)} async-done(((f32[16,8,128]{2,1,0:T(8,128)}), f32[16,8,128]{2,1,0:T(8,128)S(1)}, u32[]{:S(2)}, u32[]{:S(2)}) %all-to-all-start.17) | async-done | bytes 65568 | tf_op jit(solution)/shard_map/all_to_all | solution.py:207
  240.6 1.5 shard_map.91
  242.1 0.7 copy.9
  (1 shorter events, 0.0 us)
Async XLA Ops:
  1.4 1.2 copy-start
  2.6 0.8 copy-start.1
  2.6 0.8 copy-start.2
  4.8 17.3 %all-to-all-start = ((f32[8,80,128]{2,1,0:T(8,128)}), f32[8,80,128]{2,1,0:T(8,128)S(1)}, u32[]{:S(2)}, u32[]{:S(2)}) async-start(f32[8,80,128]{2,1,0:T(8,128)} %shard_map.68), calls=%async_computation | async-start | bytes 655360 | tf_op jit(solution)/shard_map/all_to_all | solution.py:203
  35.8 20.5 %all-to-all-start.2 = ((f32[16,8,128]{2,1,0:T(8,128)}), f32[16,8,128]{2,1,0:T(8,128)S(1)}, u32[]{:S(2)}, u32[]{:S(2)}) async-start(f32[16,8,128]{2,1,0:T(8,128)} %get-tuple-element.64), calls=%async_computation.2 | async-start | bytes 131072 | tf_op jit(solution)/shard_map/all_to_all | solution.py:207
  80.4 12.7 %all-to-all-start.5 = ((f32[16,8,128]{2,1,0:T(8,128)}), f32[16,8,128]{2,1,0:T(8,128)S(1)}, u32[]{:S(2)}, u32[]{:S(2)}) async-start(f32[16,8,128]{2,1,0:T(8,128)} %get-tuple-element.72), calls=%async_computation.5 | async-start | bytes 131072 | tf_op jit(solution)/shard_map/all_to_all | solution.py:207
  117.3 12.7 %all-to-all-start.8 = ((f32[16,8,128]{2,1,0:T(8,128)}), f32[16,8,128]{2,1,0:T(8,128)S(1)}, u32[]{:S(2)}, u32[]{:S(2)}) async-start(f32[16,8,128]{2,1,0:T(8,128)} %get-tuple-element.83), calls=%async_computation.8 | async-start | bytes 131072 | tf_op jit(solution)/shard_map/all_to_all | solution.py:207
  154.1 12.7 %all-to-all-start.11 = ((f32[16,8,128]{2,1,0:T(8,128)}), f32[16,8,128]{2,1,0:T(8,128)S(1)}, u32[]{:S(2)}, u32[]{:S(2)}) async-start(f32[16,8,128]{2,1,0:T(8,128)} %get-tuple-element.94), calls=%async_computation.11 | async-start | bytes 131072 | tf_op jit(solution)/shard_map/all_to_all | solution.py:207
  191.0 12.7 %all-to-all-start.14 = ((f32[16,8,128]{2,1,0:T(8,128)}), f32[16,8,128]{2,1,0:T(8,128)S(1)}, u32[]{:S(2)}, u32[]{:S(2)}) async-start(f32[16,8,128]{2,1,0:T(8,128)} %get-tuple-element.105), calls=%async_computation.14 | async-start | bytes 131072 | tf_op jit(solution)/shard_map/all_to_all | solution.py:207
  227.8 12.7 %all-to-all-start.17 = ((f32[16,8,128]{2,1,0:T(8,128)}), f32[16,8,128]{2,1,0:T(8,128)S(1)}, u32[]{:S(2)}, u32[]{:S(2)}) async-start(f32[16,8,128]{2,1,0:T(8,128)} %get-tuple-element.117), calls=%async_computation.17 | async-start | bytes 131072 | tf_op jit(solution)/shard_map/all_to_all | solution.py:207

commit v5 on v4

v5 whole, which is shorter than its diff:
```python
import functools

import jax
import jax.numpy as jnp
from jax import lax
from jax.experimental import pallas as pl
from jax.experimental.pallas import tpu as pltpu
from jax.sharding import Mesh, PartitionSpec as P

ITERS = 6

HP = lax.Precision.HIGHEST
F32, BF16 = (jnp.float32, jnp.bfloat16)
VMEM = pl.BlockSpec(memory_space=pltpu.VMEM)
SMEM = pl.BlockSpec(memory_space=pltpu.SMEM)


def product(a, b, contract=(1, 0), precision=HP):
    dims = (((contract[0],), (contract[1],)), ((), ()))
    return lax.dot_general(a, b, dims, precision=precision, preferred_element_type=F32)


def split(x):
    high = x.astype(BF16)
    return high, (x - high.astype(F32)).astype(BF16)


def inverse_norm(matrix):
    return 1.0 / jnp.sqrt(jnp.sum(matrix * matrix, keepdims=True) + 1e-06)


def descend(factor, hessian, contraction):
    return factor - inverse_norm(hessian) * (product(hessian, factor) - contraction)


def prepare(t_ref, wz_ref, wy_ref):
    for k in range(8):
        high, low = split(t_ref[k])
        wz_ref[:128, 256 * k : 256 * k + 256] = high
        wz_ref[128:, 256 * k : 256 * k + 256] = low
        high, low = split(t_ref[k].T)
        wy_ref[0, :, 128 * k : 128 * k + 128] = high
        wy_ref[1, :, 128 * k : 128 * k + 128] = low


def pack(square, first, step):
    tiles = [square[8 * q : 8 * q + 8] for q in range(4)]
    return sum(pltpu.roll(tiles[q], first + step * q, 1) if first + q else tiles[q] for q in range(4))


def widen(x):
    return jnp.concatenate([x, jnp.zeros((128 - x.shape[0], x.shape[1]), F32)], 0)


def unpack_gram(halves):
    return jnp.concatenate([half[32:40, 32 * q : 32 * q + 32] for half in halves for q in range(2)], 0)


def update(core, both_ref, fa, fb, fc):
    rows = [both_ref[0, h] for h in range(2)]
    cols = [both_ref[1, h] for h in range(2)]
    mode_a = jnp.concatenate([jnp.where(core == 0, col[:16], col[16:32]) for col in cols], 0)
    mode_b = jnp.concatenate([jnp.concatenate([row[:16], row[16:32]], 1) for row in rows], 0)
    gram_a, gram_b = (unpack_gram(rows), unpack_gram(cols))
    gram_c = product(fc, fc, (1, 1))
    next_a = descend(fa, gram_b * gram_c, mode_a)
    next_b = descend(fb, gram_a * gram_c, mode_b)
    h_c = gram_a * gram_b
    scale = inverse_norm(h_c)
    return next_a, next_b, fc - scale * product(h_c, fc), scale


def add_mode_c(base, scale, ring_ref):
    total = ring_ref[0]
    for n in range(1, ring_ref.shape[0] // 2):
        total += ring_ref[2 * n]
    mode_c = jnp.concatenate([total[:, 64 + 8 * q : 72 + 8 * q] for q in range(4)], 0)
    return base + scale * mode_c


def multiply(fa, fb, wz_ref, wy_ref):
    a_high, a_low = split(fa)
    b_high, b_low = split(fb)
    left = jnp.concatenate([jnp.concatenate([a_high, a_high], 1), jnp.concatenate([a_low, jnp.zeros_like(a_low)], 1)], 0)
    z = product(left, wz_ref[...], precision=None)
    z = z[:32] + z[32:]
    y = product(jnp.concatenate([b_high, b_low], 0), wy_ref[0], precision=None)
    y = y[:32] + y[32:] + product(b_high, wy_ref[1], precision=None)
    lane = lax.broadcasted_iota(jnp.int32, (32, 128), 1)
    part_c = jnp.zeros((32, 128), F32)
    for k in range(8):
        part_c = jnp.where(lane == k, jnp.sum(y[:, 128 * k : 128 * k + 128] * fa, 1, keepdims=True), part_c)
    gram_a = product(fa, widen(fa), (1, 1))
    gram_b = product(fb, widen(fb), (1, 1))
    return y, z, pack(gram_a, 0, 32), pack(gram_b, 0, 32), pack(part_c, 64, 8)


def message(fc, y, z, gram_a, part_c, sent_ref):
    part_a = jnp.zeros((32, 128), F32)
    part_b = jnp.zeros((32, 256), F32)
    for k in range(8):
        weight = fc[:, k : k + 1]
        part_a += weight * y[:, 128 * k : 128 * k + 128]
        part_b += weight * z[:, 256 * k : 256 * k + 256]
    sent_ref[0:32] = part_b[:, :128]
    sent_ref[32:64] = part_b[:, 128:]
    sent_ref[64:96] = part_a
    sent_ref[96:104] = gram_a
    sent_ref[104:112] = part_c


def first_kernel(fa_ref, fb_ref, fc_ref, wz_ref, wy_ref, gram_ref, sent_ref):
    y, z, gram_a, gram_b, part_c = multiply(fa_ref[...], fb_ref[...], wz_ref, wy_ref)
    gram_ref[...] = gram_b
    message(fc_ref[...], y, z, gram_a, part_c, sent_ref)


def chip_kernel(place_ref, both_ref, gram_ref, out_ref):
    first = place_ref[0] == 0
    low = jnp.where(first, both_ref[0, 0:32] + both_ref[1, 0:32], both_ref[0, 64:96])
    high = jnp.where(first, both_ref[0, 32:64] + both_ref[1, 32:64], both_ref[1, 64:96])
    gram = jnp.where(first, both_ref[0, 96:104] + both_ref[1, 96:104], gram_ref[...])
    part_c = both_ref[0, 104:112] + both_ref[1, 104:112]
    lane = lax.broadcasted_iota(jnp.int32, (8, 128), 1)
    ring = out_ref.shape[0] // 2
    for h in range(2):
        tile = jnp.where(lane < 64, pltpu.roll(gram, 64, 1) if h else gram, part_c)
        for n in range(h * ring, h * ring + ring):
            out_ref[n, 0:16] = low[16 * h : 16 * h + 16]
            out_ref[n, 16:32] = high[16 * h : 16 * h + 16]
            out_ref[n, 32:40] = tile


def ring_kernel(got_ref, sum_ref, ring_ref):
    total = got_ref[0]
    for n in range(1, got_ref.shape[0]):
        total += got_ref[n]
    sum_ref[...] = total
    for n in range(ring_ref.shape[0]):
        ring_ref[n] = total[32:]


def factor_kernel(place_ref, both_ref, fa_ref, fb_ref, fc_ref, wz_ref, wy_ref, na_ref, nb_ref, gram_ref, base_ref, scale_ref, y_ref, z_ref, packs_ref):
    fa, fb, base, scale = update(place_ref[0], both_ref, fa_ref[...], fb_ref[...], fc_ref[...])
    na_ref[...] = fa
    nb_ref[...] = fb
    base_ref[...] = base
    scale_ref[...] = jnp.broadcast_to(scale, (8, 128))
    y, z, gram_a, gram_b, part_c = multiply(fa, fb, wz_ref, wy_ref)
    y_ref[...] = y
    z_ref[...] = z
    gram_ref[...] = gram_b
    packs_ref[0] = gram_a
    packs_ref[1] = part_c


def send_kernel(ring_ref, base_ref, scale_ref, y_ref, z_ref, packs_ref, nc_ref, sent_ref):
    fc = add_mode_c(base_ref[...], scale_ref[:1, :1], ring_ref)
    nc_ref[...] = fc
    message(fc, y_ref[...], z_ref[...], packs_ref[0], packs_ref[1], sent_ref)


def last_kernel(place_ref, both_ref, ring_ref, fa_ref, fb_ref, fc_ref, na_ref, nb_ref, nc_ref):
    fa, fb, base, scale = update(place_ref[0], both_ref, fa_ref[...], fb_ref[...], fc_ref[...])
    na_ref[...] = fa
    nb_ref[...] = fb
    nc_ref[...] = add_mode_c(base, scale, ring_ref)


def call(kernel, outs, *args):
    shapes = [jax.ShapeDtypeStruct(s, d) for s, d in outs]
    specs = [SMEM if a.dtype == jnp.int32 else VMEM for a in args]
    params = pltpu.CompilerParams(vmem_limit_bytes=16 * 1024 * 1024)
    cost = pl.CostEstimate(flops=100_000_000, bytes_accessed=4_000_000, transcendentals=0)
    return pl.pallas_call(kernel, out_shape=shapes, in_specs=specs, out_specs=[VMEM] * len(shapes), compiler_params=params, cost_estimate=cost)(*args)


A, B, C = (((32, 128), F32), ((32, 256), F32), ((32, 8), F32))
TILE, SENT = (((8, 128), F32), ((112, 128), F32))
PRODUCTS = [TILE, ((32, 1024), F32), ((32, 2048), F32), ((2, 8, 128), F32)]
ALL = ("x_hi", "z", "core", "y", "x_lo")


def groups_of(size_z, size_y):
    def at(x_hi, z, core, y, x_lo):
        return (((x_hi * size_z + z) * 2 + core) * size_y + y) * 2 + x_lo

    two, zs, ys = (range(2), range(size_z), range(size_y))
    rings = [[at(h, z, 0, y, l) for h in two for z in zs] for l in two for y in ys]
    rings += [[at(h, z, 1, y, l) for l in two for y in ys] for h in two for z in zs]
    pairs = [[at(h, z, 0, y, l) for h in two] for z in zs for y in ys for l in two]
    pairs += [[at(h, z, 1, y, l) for l in two] for z in zs for y in ys for h in two]
    return rings, pairs


def shards(size_z, size_y, tensor, factor_a, factor_b, factor_c):
    fa, fb, fc = (factor_a, factor_b, factor_c)
    place = lax.axis_index("core").reshape(1).astype(jnp.int32)
    rings, pairs = groups_of(size_z, size_y)
    weights = call(prepare, [((256, 2048), BF16), ((2, 256, 1024), BF16)], tensor)
    gram_b, sent = call(first_kernel, [TILE, SENT], fa, fb, fc, *weights)
    for step in range(ITERS):
        both = lax.all_gather(sent, "core")
        (sent,) = call(chip_kernel, [((2 * size_z, 40, 128), F32)], place, both, gram_b)
        got = lax.all_to_all(sent, ALL, 0, 0, axis_index_groups=rings)
        sums, ring = call(ring_kernel, [((40, 128), F32), ((4 * size_y, 8, 128), F32)], got)
        ring = lax.all_to_all(ring, ("y", "x_lo", "core"), 0, 0)
        both = lax.all_gather(sums, ALL, axis_index_groups=pairs)
        both = lax.all_gather(both, "core")
        if step < ITERS - 1:
            fa, fb, gram_b, *rest = call(factor_kernel, [A, B, TILE, C] + PRODUCTS, place, both, fa, fb, fc, *weights)
            fc, sent = call(send_kernel, [C, SENT], ring, *rest)
        else:
            fa, fb, fc = call(last_kernel, [A, B, C], place, both, ring, fa, fb, fc)
    return (fa, fb, fc)


def solution(mesh):
    rows, cols = mesh.devices.shape
    devices = mesh.devices.reshape(2, rows // 4, 2, cols // 2, 2)
    fine = Mesh(devices, ("x_hi", "z", "core", "y", "x_lo"))
    row, col = (("x_hi", "z", "core"), ("y", "x_lo"))
    in_specs = (P(None, row, col), P(None, row), P(None, col), P())
    out_specs = (P(None, row), P(None, col), P())
    body = functools.partial(shards, rows // 4, cols // 2)
    return jax.shard_map(body, mesh=fine, in_specs=in_specs, out_specs=out_specs, check_vma=False)
```

time: 244 us -> 227 us (0.930)
  waiting for transfers between devices: 35.7 us -> 3.68 us
  blocking collectives: 137 us -> 152 us
  starting transfers between devices: 47.3 us -> 54.4 us
  Pallas kernels: 19 us -> 12.7 us
    all_gather x6 -> x18, blocking collectives: 11.1 us -> 66.3 us  [the longest x6 25.6 us: shards(): both = lax.all_gather(both, 'core')]
    all_to_all x11 -> x6, blocking collectives: 126 us -> 85.8 us  [shards(): got = lax.all_to_all(sent, ALL, 0, 0, axis_index_groups=rings)]
    all_to_all x7 -> x6, waiting for transfers between devices: 35.7 us -> 3.68 us  [shards(): ring = lax.all_to_all(ring, ('y', 'x_lo', 'core'), 0, 0)]
    all_to_all x7 -> x6, starting transfers between devices: 47.3 us -> 54.4 us  [shards(): ring = lax.all_to_all(ring, ('y', 'x_lo', 'core'), 0, 0)]
    pallas_call x25, Pallas kernels: 19 us -> 12.7 us  [call(): pl.pallas_call(kernel, out_shape=shapes, in_specs=specs, out_specs=[VMEM]...]
  transfers between devices with their start and end apart: 7 -> 6, of which waited for: 7 -> 6; matrix products, arithmetic and copies ran while one was open for 0% -> 0% of each run, Pallas kernels for 3% -> 2%
where the time goes in v5:
time: 227 us; the launch traced here: 226 us
  blocking collectives  152 us (67%)
  starting transfers between devices  54.4 us (24%)
  Pallas kernels  12.7 us (6%)
  waiting for transfers between devices  3.68 us (2%)
  local copies, waits for them, and re-layouts  2.83 us (1%)
    all_to_all x6, blocking collectives, shards(): got = lax.all_to_all(sent, ALL, 0, 0, axis_index_groups=rings)  85.8 us
    all_to_all x6, starting transfers between devices, shards(): ring = lax.all_to_all(ring, ('y', 'x_lo', 'core'), 0, 0)  54.4 us
    all_gather x6, blocking collectives, shards(): both = lax.all_gather(both, 'core')  25.6 us
    all_gather x6, blocking collectives, shards(): both = lax.all_gather(sums, ALL, axis_index_groups=pairs)  21.6 us
    all_gather x6, blocking collectives, shards(): both = lax.all_gather(sent, 'core')  19 us
    pallas_call x25, Pallas kernels, call(): pl.pallas_call(kernel, out_shape=shapes, in_specs=specs, out_specs=[VMEM]...  12.7 us
  transfers between devices with their start and end apart: 6, of which 6 were waited for; matrix products, arithmetic and copies ran while one was open for 0% of the time, Pallas kernels for 2%

profile of v5, /device:TPU:1, one launch (start us, length us, event | category | flops | bytes accessed | tf_op | source)
XLA Modules:
  0.0 226.4 jit_solution(1749042132471548357)
XLA Ops:
  0.6 0.7 copy-done.3
  1.4 1.2 copy-done
  2.6 0.6 shard_map.67
  3.2 0.2 copy-done.1
  3.4 0.7 shard_map.68
  4.0 8.4 %all-gather = f32[224,128]{1,0:T(8,128)S(1)} all-gather(f32[112,128]{1,0:T(8,128)S(1)} %get-tuple-element.71), channel_id=2, replica_groups=mesh['x_hi'=2,'z'=8,'core'=2,'y'=8,'x_lo'=2] {'core'}, dimensions={0}, use_global_device_ids=true | all-gather | bytes 172032 | tf_op jit(solution)/shard_map/all_gather | solution.py:203
  12.5 0.1 shard_map.69
  12.5 10.8 %all_to_all.60.got_ref = f32[16,40,128]{2,1,0:T(8,128)S(1)} all-to-all(f32[16,40,128]{2,1,0:T(8,128)S(1)} %shard_map.69), channel_id=1, replica_groups={{0,32,64,96,128,160,192,224,256,288,320,352,384,416,448,480},{2,34,66,9..., dimensions={0} | all-to-all | bytes 655360 | tf_op jit(solution)/shard_map/all_to_all | solution.py:205
  23.3 0.7 shard_map.70
  24.0 14.9 %all-to-all-start.1 = ((f32[32,8,128]{2,1,0:T(8,128)}), f32[32,8,128]{2,1,0:T(8,128)S(1)}, u32[]{:S(2)}, u32[]{:S(2)}) async-start(f32[32,8,128]{2,1,0:T(8,128)} %get-tuple-element.73), calls=%async_computation.1 | async-start | bytes 262144 | tf_op jit(solution)/shard_map/all_to_all | solution.py:207
  38.9 3.6 %all-gather.1 = f32[80,128]{1,0:T(8,128)S(1)} all-gather(f32[40,128]{1,0:T(8,128)S(1)} %get-tuple-element.74), channel_id=3, replica_groups={{0,256},{1,257},{2,258},{3,259},{4,260},{5,261},{6,262},{7,263},{8,264}..., dimensions={0}, use_global_device_ids=true | all-gather | bytes 61440 | tf_op jit(solution)/shard_map/all_gather | solution.py:208
  42.5 4.3 %all-gather.2 = f32[4,40,128]{2,1,0:T(8,128)S(1)} all-gather(f32[2,40,128]{2,1,0:T(8,128)S(1)} %bitcast.31), channel_id=4, replica_groups=mesh['x_hi'=2,'z'=8,'core'=2,'y'=8,'x_lo'=2] {'core'}, dimensions={0}, use_global_device_ids=true | all-gather | bytes 122880 | tf_op jit(solution)/shard_map/all_gather | solution.py:209
  46.7 0.9 shard_map.71
  47.7 0.5 all-to-all-done.1.ring_ref
  48.1 0.3 shard_map.72
  48.4 2.1 all-gather.3
  50.5 0.1 shard_map.73
  50.6 15.0 %all_to_all.61.got_ref = f32[16,40,128]{2,1,0:T(8,128)S(1)} all-to-all(f32[16,40,128]{2,1,0:T(8,128)S(1)} %shard_map.73), channel_id=1, replica_groups={{0,32,64,96,128,160,192,224,256,288,320,352,384,416,448,480},{2,34,66,9..., dimensions={0} | all-to-all | bytes 655360 | tf_op jit(solution)/shard_map/all_to_all | solution.py:205
  65.6 0.7 shard_map.74
  66.3 7.9 %all-to-all-start.3 = ((f32[32,8,128]{2,1,0:T(8,128)}), f32[32,8,128]{2,1,0:T(8,128)S(1)}, u32[]{:S(2)}, u32[]{:S(2)}) async-start(f32[32,8,128]{2,1,0:T(8,128)} %get-tuple-element.82), calls=%async_computation.3 | async-start | bytes 262144 | tf_op jit(solution)/shard_map/all_to_all | solution.py:207
  74.2 3.6 %all-gather.4 = f32[80,128]{1,0:T(8,128)S(1)} all-gather(f32[40,128]{1,0:T(8,128)S(1)} %get-tuple-element.83), channel_id=6, replica_groups={{0,256},{1,257},{2,258},{3,259},{4,260},{5,261},{6,262},{7,263},{8,264}..., dimensions={0}, use_global_device_ids=true | all-gather | bytes 61440 | tf_op jit(solution)/shard_map/all_gather | solution.py:208
  77.8 4.3 %all-gather.5 = f32[4,40,128]{2,1,0:T(8,128)S(1)} all-gather(f32[2,40,128]{2,1,0:T(8,128)S(1)} %bitcast.32), channel_id=7, replica_groups=mesh['x_hi'=2,'z'=8,'core'=2,'y'=8,'x_lo'=2] {'core'}, dimensions={0}, use_global_device_ids=true | all-gather | bytes 122880 | tf_op jit(solution)/shard_map/all_gather | solution.py:209
  82.1 0.9 shard_map.75
  83.0 0.5 all-to-all-done.3.ring_ref
  83.5 0.3 shard_map.76
  83.7 2.1 all-gather.6
  85.9 15.0 %all_to_all.62.got_ref = f32[16,40,128]{2,1,0:T(8,128)S(1)} all-to-all(f32[16,40,128]{2,1,0:T(8,128)S(1)} %shard_map.77), channel_id=1, replica_groups={{0,32,64,96,128,160,192,224,256,288,320,352,384,416,448,480},{2,34,66,9..., dimensions={0} | all-to-all | bytes 655360 | tf_op jit(solution)/shard_map/all_to_all | solution.py:205
  100.9 0.7 shard_map.78
  101.6 7.9 %all-to-all-start.5 = ((f32[32,8,128]{2,1,0:T(8,128)}), f32[32,8,128]{2,1,0:T(8,128)S(1)}, u32[]{:S(2)}, u32[]{:S(2)}) async-start(f32[32,8,128]{2,1,0:T(8,128)} %get-tuple-element.94), calls=%async_computation.5 | async-start | bytes 262144 | tf_op jit(solution)/shard_map/all_to_all | solution.py:207
  109.5 3.6 %all-gather.7 = f32[80,128]{1,0:T(8,128)S(1)} all-gather(f32[40,128]{1,0:T(8,128)S(1)} %get-tuple-element.95), channel_id=9, replica_groups={{0,256},{1,257},{2,258},{3,259},{4,260},{5,261},{6,262},{7,263},{8,264}..., dimensions={0}, use_global_device_ids=true | all-gather | bytes 61440 | tf_op jit(solution)/shard_map/all_gather | solution.py:208
  113.1 4.3 %all-gather.8 = f32[4,40,128]{2,1,0:T(8,128)S(1)} all-gather(f32[2,40,128]{2,1,0:T(8,128)S(1)} %bitcast.33), channel_id=10, replica_groups=mesh['x_hi'=2,'z'=8,'core'=2,'y'=8,'x_lo'=2] {'core'}, dimensions={0}, use_global_device_ids=true | all-gather | bytes 122880 | tf_op jit(solution)/shard_map/all_gather | solution.py:209
  117.4 0.9 shard_map.79
  118.3 0.5 all-to-all-done.5.ring_ref
  118.8 0.3 shard_map.80
  119.1 2.1 all-gather.9
  121.2 0.1 shard_map.81
  121.3 15.0 %all_to_all.63.got_ref = f32[16,40,128]{2,1,0:T(8,128)S(1)} all-to-all(f32[16,40,128]{2,1,0:T(8,128)S(1)} %shard_map.81), channel_id=1, replica_groups={{0,32,64,96,128,160,192,224,256,288,320,352,384,416,448,480},{2,34,66,9..., dimensions={0} | all-to-all | bytes 655360 | tf_op jit(solution)/shard_map/all_to_all | solution.py:205
  136.3 0.7 shard_map.82
  136.9 7.9 %all-to-all-start.7 = ((f32[32,8,128]{2,1,0:T(8,128)}), f32[32,8,128]{2,1,0:T(8,128)S(1)}, u32[]{:S(2)}, u32[]{:S(2)}) async-start(f32[32,8,128]{2,1,0:T(8,128)} %get-tuple-element.106), calls=%async_computation.7 | async-start | bytes 262144 | tf_op jit(solution)/shard_map/all_to_all | solution.py:207
  144.9 3.6 %all-gather.10 = f32[80,128]{1,0:T(8,128)S(1)} all-gather(f32[40,128]{1,0:T(8,128)S(1)} %get-tuple-element.107), channel_id=12, replica_groups={{0,256},{1,257},{2,258},{3,259},{4,260},{5,261},{6,262},{7,263},{8,264}..., dimensions={0}, use_global_device_ids=true | all-gather | bytes 61440 | tf_op jit(solution)/shard_map/all_gather | solution.py:208
  148.5 4.3 %all-gather.11 = f32[4,40,128]{2,1,0:T(8,128)S(1)} all-gather(f32[2,40,128]{2,1,0:T(8,128)S(1)} %bitcast.34), channel_id=13, replica_groups=mesh['x_hi'=2,'z'=8,'core'=2,'y'=8,'x_lo'=2] {'core'}, dimensions={0}, use_global_device_ids=true | all-gather | bytes 122880 | tf_op jit(solution)/shard_map/all_gather | solution.py:209
  152.7 0.9 shard_map.83
  153.7 0.5 all-to-all-done.7.ring_ref
  154.1 0.3 shard_map.84
  154.4 2.1 all-gather.12
  156.5 0.1 shard_map.85
  156.6 15.0 %all_to_all.64.got_ref = f32[16,40,128]{2,1,0:T(8,128)S(1)} all-to-all(f32[16,40,128]{2,1,0:T(8,128)S(1)} %shard_map.85), channel_id=1, replica_groups={{0,32,64,96,128,160,192,224,256,288,320,352,384,416,448,480},{2,34,66,9..., dimensions={0} | all-to-all | bytes 655360 | tf_op jit(solution)/shard_map/all_to_all | solution.py:205
  171.6 0.7 shard_map.86
  172.3 7.9 %all-to-all-start.9 = ((f32[32,8,128]{2,1,0:T(8,128)}), f32[32,8,128]{2,1,0:T(8,128)S(1)}, u32[]{:S(2)}, u32[]{:S(2)}) async-start(f32[32,8,128]{2,1,0:T(8,128)} %get-tuple-element.118), calls=%async_computation.9 | async-start | bytes 262144 | tf_op jit(solution)/shard_map/all_to_all | solution.py:207
  180.2 3.6 %all-gather.13 = f32[80,128]{1,0:T(8,128)S(1)} all-gather(f32[40,128]{1,0:T(8,128)S(1)} %get-tuple-element.119), channel_id=15, replica_groups={{0,256},{1,257},{2,258},{3,259},{4,260},{5,261},{6,262},{7,263},{8,264}..., dimensions={0}, use_global_device_ids=true | all-gather | bytes 61440 | tf_op jit(solution)/shard_map/all_gather | solution.py:208
  183.8 4.3 %all-gather.14 = f32[4,40,128]{2,1,0:T(8,128)S(1)} all-gather(f32[2,40,128]{2,1,0:T(8,128)S(1)} %bitcast.35), channel_id=16, replica_groups=mesh['x_hi'=2,'z'=8,'core'=2,'y'=8,'x_lo'=2] {'core'}, dimensions={0}, use_global_device_ids=true | all-gather | bytes 122880 | tf_op jit(solution)/shard_map/all_gather | solution.py:209
  188.1 0.9 shard_map.87
  189.0 0.5 all-to-all-done.9.ring_ref
  189.5 0.3 shard_map.88
  189.7 2.1 all-gather.15
  191.8 0.1 shard_map.89
  191.9 15.0 %all_to_all.65.got_ref = f32[16,40,128]{2,1,0:T(8,128)S(1)} all-to-all(f32[16,40,128]{2,1,0:T(8,128)S(1)} %shard_map.89), channel_id=1, replica_groups={{0,32,64,96,128,160,192,224,256,288,320,352,384,416,448,480},{2,34,66,9..., dimensions={0} | all-to-all | bytes 655360 | tf_op jit(solution)/shard_map/all_to_all | solution.py:205
  206.9 0.7 shard_map.90
  207.6 7.9 %all-to-all-start.11 = ((f32[32,8,128]{2,1,0:T(8,128)}), f32[32,8,128]{2,1,0:T(8,128)S(1)}, u32[]{:S(2)}, u32[]{:S(2)}) async-start(f32[32,8,128]{2,1,0:T(8,128)} %get-tuple-element.131), calls=%async_computation.11 | async-start | bytes 262144 | tf_op jit(solution)/shard_map/all_to_all | solution.py:207
  215.5 3.6 %all-gather.16 = f32[80,128]{1,0:T(8,128)S(1)} all-gather(f32[40,128]{1,0:T(8,128)S(1)} %get-tuple-element.130), channel_id=18, replica_groups={{0,256},{1,257},{2,258},{3,259},{4,260},{5,261},{6,262},{7,263},{8,264}..., dimensions={0}, use_global_device_ids=true | all-gather | bytes 61440 | tf_op jit(solution)/shard_map/all_gather | solution.py:208
  219.1 4.3 %all-gather.17 = f32[4,40,128]{2,1,0:T(8,128)S(1)} all-gather(f32[2,40,128]{2,1,0:T(8,128)S(1)} %bitcast.36), channel_id=19, replica_groups=mesh['x_hi'=2,'z'=8,'core'=2,'y'=8,'x_lo'=2] {'core'}, dimensions={0}, use_global_device_ids=true | all-gather | bytes 122880 | tf_op jit(solution)/shard_map/all_gather | solution.py:209
  223.4 1.4 all-to-all-done.11.ring_ref
  224.8 1.0 shard_map.91
  225.8 0.7 copy.12
  (7 shorter events, 0.2 us)
Async XLA Ops:
  0.6 0.7 copy-start.3
  1.4 1.2 copy-start
  2.6 0.8 copy-start.1
  2.6 0.8 copy-start.2
  24.0 24.1 %all-to-all-start.1 = ((f32[32,8,128]{2,1,0:T(8,128)}), f32[32,8,128]{2,1,0:T(8,128)S(1)}, u32[]{:S(2)}, u32[]{:S(2)}) async-start(f32[32,8,128]{2,1,0:T(8,128)} %get-tuple-element.73), calls=%async_computation.1 | async-start | bytes 262144 | tf_op jit(solution)/shard_map/all_to_all | solution.py:207
  66.3 17.2 %all-to-all-start.3 = ((f32[32,8,128]{2,1,0:T(8,128)}), f32[32,8,128]{2,1,0:T(8,128)S(1)}, u32[]{:S(2)}, u32[]{:S(2)}) async-start(f32[32,8,128]{2,1,0:T(8,128)} %get-tuple-element.82), calls=%async_computation.3 | async-start | bytes 262144 | tf_op jit(solution)/shard_map/all_to_all | solution.py:207
  101.6 17.2 %all-to-all-start.5 = ((f32[32,8,128]{2,1,0:T(8,128)}), f32[32,8,128]{2,1,0:T(8,128)S(1)}, u32[]{:S(2)}, u32[]{:S(2)}) async-start(f32[32,8,128]{2,1,0:T(8,128)} %get-tuple-element.94), calls=%async_computation.5 | async-start | bytes 262144 | tf_op jit(solution)/shard_map/all_to_all | solution.py:207
  136.9 17.2 %all-to-all-start.7 = ((f32[32,8,128]{2,1,0:T(8,128)}), f32[32,8,128]{2,1,0:T(8,128)S(1)}, u32[]{:S(2)}, u32[]{:S(2)}) async-start(f32[32,8,128]{2,1,0:T(8,128)} %get-tuple-element.106), calls=%async_computation.7 | async-start | bytes 262144 | tf_op jit(solution)/shard_map/all_to_all | solution.py:207
  172.3 17.2 %all-to-all-start.9 = ((f32[32,8,128]{2,1,0:T(8,128)}), f32[32,8,128]{2,1,0:T(8,128)S(1)}, u32[]{:S(2)}, u32[]{:S(2)}) async-start(f32[32,8,128]{2,1,0:T(8,128)} %get-tuple-element.118), calls=%async_computation.9 | async-start | bytes 262144 | tf_op jit(solution)/shard_map/all_to_all | solution.py:207
  207.6 17.2 %all-to-all-start.11 = ((f32[32,8,128]{2,1,0:T(8,128)}), f32[32,8,128]{2,1,0:T(8,128)S(1)}, u32[]{:S(2)}, u32[]{:S(2)}) async-start(f32[32,8,128]{2,1,0:T(8,128)} %get-tuple-element.131), calls=%async_computation.11 | async-start | bytes 262144 | tf_op jit(solution)/shard_map/all_to_all | solution.py:207

commit v6 on v5

--- a/solution.py
+++ b/solution.py
@@ -73,7 +73,7 @@
 def add_mode_c(base, scale, ring_ref):
     total = ring_ref[0]
     for n in range(1, ring_ref.shape[0] // 2):
-        total += ring_ref[2 * n]
+        total += ring_ref[n]
     mode_c = jnp.concatenate([total[:, 64 + 8 * q : 72 + 8 * q] for q in range(4)], 0)
     return base + scale * mode_c
 
@@ -122,10 +122,9 @@
     gram = jnp.where(first, both_ref[0, 96:104] + both_ref[1, 96:104], gram_ref[...])
     part_c = both_ref[0, 104:112] + both_ref[1, 104:112]
     lane = lax.broadcasted_iota(jnp.int32, (8, 128), 1)
-    ring = out_ref.shape[0] // 2
     for h in range(2):
         tile = jnp.where(lane < 64, pltpu.roll(gram, 64, 1) if h else gram, part_c)
-        for n in range(h * ring, h * ring + ring):
+        for n in range(h, out_ref.shape[0], 2):
             out_ref[n, 0:16] = low[16 * h : 16 * h + 16]
             out_ref[n, 16:32] = high[16 * h : 16 * h + 16]
             out_ref[n, 32:40] = tile
@@ -187,8 +186,8 @@
 
     two, zs, ys = (range(2), range(size_z), range(size_y))
     rings = [[at(h, z, 0, y, l) for h in two for z in zs] for l in two for y in ys]
-    rings += [[at(h, z, 1, y, l) for l in two for y in ys] for h in two for z in zs]
-    pairs = [[at(h, z, 0, y, l) for h in two] for z in zs for y in ys for l in two]
+    rings += [[at(h, z, 1, y, l) for y in ys for l in two] for h in two for z in zs]
+    pairs = [[at(h, z, 0, y, l), at(h, z + 1, 0, y, l)] for h in two for z in zs[::2] for y in ys for l in two]
     pairs += [[at(h, z, 1, y, l) for l in two] for z in zs for y in ys for h in two]
     return rings, pairs
 
@@ -204,7 +203,7 @@
         (sent,) = call(chip_kernel, [((2 * size_z, 40, 128), F32)], place, both, gram_b)
         got = lax.all_to_all(sent, ALL, 0, 0, axis_index_groups=rings)
         sums, ring = call(ring_kernel, [((40, 128), F32), ((4 * size_y, 8, 128), F32)], got)
-        ring = lax.all_to_all(ring, ("y", "x_lo", "core"), 0, 0)
+        ring = lax.all_to_all(ring, ("core", "y", "x_lo"), 0, 0)
         both = lax.all_gather(sums, ALL, axis_index_groups=pairs)
         both = lax.all_gather(both, "core")
         if step < ITERS - 1:

time: 227 us -> 219 us (0.965)
  starting transfers between devices: 54.4 us -> 40.5 us
  waiting for transfers between devices: 3.68 us -> 13.5 us
  blocking collectives: 152 us -> 148 us
    all_to_all x6, starting transfers between devices: 54.4 us -> 40.5 us  [shards(): ring = lax.all_to_all(ring, ('core', 'y', 'x_lo'), 0, 0)]
    all_to_all x6, waiting for transfers between devices: 3.68 us -> 13.5 us  [shards(): ring = lax.all_to_all(ring, ('core', 'y', 'x_lo'), 0, 0)]
    all_gather x6, blocking collectives: 25.6 us -> 16.4 us  [shards(): both = lax.all_gather(both, 'core')]
    all_to_all x6, blocking collectives: 85.8 us -> 90.7 us  [shards(): got = lax.all_to_all(sent, ALL, 0, 0, axis_index_groups=rings)]
where the time goes in v6:
time: 219 us; the launch traced here: 218 us
  blocking collectives  148 us (68%)
  starting transfers between devices  40.5 us (18%)
  waiting for transfers between devices  13.5 us (6%)
  Pallas kernels  12.7 us (6%)
  local copies, waits for them, and re-layouts  2.83 us (1%)
    all_to_all x6, blocking collectives, shards(): got = lax.all_to_all(sent, ALL, 0, 0, axis_index_groups=rings)  90.7 us
    all_to_all x6, starting transfers between devices, shards(): ring = lax.all_to_all(ring, ('core', 'y', 'x_lo'), 0, 0)  40.5 us
    all_gather x6, blocking collectives, shards(): both = lax.all_gather(sums, ALL, axis_index_groups=pairs)  21.6 us
    all_gather x6, blocking collectives, shards(): both = lax.all_gather(sent, 'core')  19.3 us
    all_gather x6, blocking collectives, shards(): both = lax.all_gather(both, 'core')  16.4 us
    all_to_all x6, waiting for transfers between devices, shards(): ring = lax.all_to_all(ring, ('core', 'y', 'x_lo'), 0, 0)  13.5 us
    pallas_call x25, Pallas kernels, call(): pl.pallas_call(kernel, out_shape=shapes, in_specs=specs, out_specs=[VMEM]...  12.7 us
  transfers between devices with their start and end apart: 6, of which 6 were waited for; matrix products, arithmetic and copies ran while one was open for 0% of the time, Pallas kernels for 2%

profile of v6, /device:TPU:1, one launch (start us, length us, event | category | flops | bytes accessed | tf_op | source)
XLA Modules:
  0.0 218.2 jit_solution(14848332358206025911)
XLA Ops:
  0.6 0.7 copy-done.3
  1.4 1.2 copy-done
  2.6 0.6 shard_map.67
  3.2 0.2 copy-done.1
  3.4 0.7 shard_map.68
  4.0 8.4 %all-gather = f32[224,128]{1,0:T(8,128)S(1)} all-gather(f32[112,128]{1,0:T(8,128)S(1)} %get-tuple-element.71), channel_id=2, replica_groups=mesh['x_hi'=2,'z'=8,'core'=2,'y'=8,'x_lo'=2] {'core'}, dimensions={0}, use_global_device_ids=true | all-gather | bytes 172032 | tf_op jit(solution)/shard_map/all_gather | solution.py:202
  12.5 0.1 shard_map.69
  12.5 12.7 %all_to_all.60.got_ref = f32[16,40,128]{2,1,0:T(8,128)S(1)} all-to-all(f32[16,40,128]{2,1,0:T(8,128)S(1)} %shard_map.69), channel_id=1, replica_groups={{0,32,64,96,128,160,192,224,256,288,320,352,384,416,448,480},{2,34,66,9..., dimensions={0} | all-to-all | bytes 655360 | tf_op jit(solution)/shard_map/all_to_all | solution.py:204
  25.3 0.7 shard_map.70
  26.0 12.9 %all-to-all-start.1 = ((f32[32,8,128]{2,1,0:T(8,128)}), f32[32,8,128]{2,1,0:T(8,128)S(1)}, u32[]{:S(2)}, u32[]{:S(2)}) async-start(f32[32,8,128]{2,1,0:T(8,128)} %get-tuple-element.73), calls=%async_computation.1 | async-start | bytes 262144 | tf_op jit(solution)/shard_map/all_to_all | solution.py:206
  38.9 3.6 %all-gather.1 = f32[80,128]{1,0:T(8,128)S(1)} all-gather(f32[40,128]{1,0:T(8,128)S(1)} %get-tuple-element.74), channel_id=3, replica_groups={{0,32},{1,33},{2,34},{3,35},{4,36},{5,37},{6,38},{7,39},{8,40},{9,41},{..., dimensions={0}, use_global_device_ids=true | all-gather | bytes 61440 | tf_op jit(solution)/shard_map/all_gather | solution.py:207
  42.5 2.7 %all-gather.2 = f32[4,40,128]{2,1,0:T(8,128)S(1)} all-gather(f32[2,40,128]{2,1,0:T(8,128)S(1)} %bitcast.31), channel_id=4, replica_groups=mesh['x_hi'=2,'z'=8,'core'=2,'y'=8,'x_lo'=2] {'core'}, dimensions={0}, use_global_device_ids=true | all-gather | bytes 122880 | tf_op jit(solution)/shard_map/all_gather | solution.py:208
  45.2 0.9 shard_map.71
  46.1 2.1 all-to-all-done.1.ring_ref
  48.2 0.3 shard_map.72
  48.5 2.2 all-gather.3
  50.7 0.1 shard_map.73
  50.8 15.6 %all_to_all.61.got_ref = f32[16,40,128]{2,1,0:T(8,128)S(1)} all-to-all(f32[16,40,128]{2,1,0:T(8,128)S(1)} %shard_map.73), channel_id=1, replica_groups={{0,32,64,96,128,160,192,224,256,288,320,352,384,416,448,480},{2,34,66,9..., dimensions={0} | all-to-all | bytes 655360 | tf_op jit(solution)/shard_map/all_to_all | solution.py:204
  66.4 0.7 shard_map.74
  67.0 5.5 %all-to-all-start.3 = ((f32[32,8,128]{2,1,0:T(8,128)}), f32[32,8,128]{2,1,0:T(8,128)S(1)}, u32[]{:S(2)}, u32[]{:S(2)}) async-start(f32[32,8,128]{2,1,0:T(8,128)} %get-tuple-element.82), calls=%async_computation.3 | async-start | bytes 262144 | tf_op jit(solution)/shard_map/all_to_all | solution.py:206
  72.5 3.6 %all-gather.4 = f32[80,128]{1,0:T(8,128)S(1)} all-gather(f32[40,128]{1,0:T(8,128)S(1)} %get-tuple-element.83), channel_id=6, replica_groups={{0,32},{1,33},{2,34},{3,35},{4,36},{5,37},{6,38},{7,39},{8,40},{9,41},{..., dimensions={0}, use_global_device_ids=true | all-gather | bytes 61440 | tf_op jit(solution)/shard_map/all_gather | solution.py:207
  76.1 2.7 %all-gather.5 = f32[4,40,128]{2,1,0:T(8,128)S(1)} all-gather(f32[2,40,128]{2,1,0:T(8,128)S(1)} %bitcast.32), channel_id=7, replica_groups=mesh['x_hi'=2,'z'=8,'core'=2,'y'=8,'x_lo'=2] {'core'}, dimensions={0}, use_global_device_ids=true | all-gather | bytes 122880 | tf_op jit(solution)/shard_map/all_gather | solution.py:208
  78.9 0.9 shard_map.75
  79.8 2.1 all-to-all-done.3.ring_ref
  81.9 0.3 shard_map.76
  82.2 2.2 all-gather.6
  84.3 0.1 shard_map.77
  84.4 15.6 %all_to_all.62.got_ref = f32[16,40,128]{2,1,0:T(8,128)S(1)} all-to-all(f32[16,40,128]{2,1,0:T(8,128)S(1)} %shard_map.77), channel_id=1, replica_groups={{0,32,64,96,128,160,192,224,256,288,320,352,384,416,448,480},{2,34,66,9..., dimensions={0} | all-to-all | bytes 655360 | tf_op jit(solution)/shard_map/all_to_all | solution.py:204
  100.0 0.7 shard_map.78
  100.7 5.5 %all-to-all-start.5 = ((f32[32,8,128]{2,1,0:T(8,128)}), f32[32,8,128]{2,1,0:T(8,128)S(1)}, u32[]{:S(2)}, u32[]{:S(2)}) async-start(f32[32,8,128]{2,1,0:T(8,128)} %get-tuple-element.94), calls=%async_computation.5 | async-start | bytes 262144 | tf_op jit(solution)/shard_map/all_to_all | solution.py:206
  106.2 3.6 %all-gather.7 = f32[80,128]{1,0:T(8,128)S(1)} all-gather(f32[40,128]{1,0:T(8,128)S(1)} %get-tuple-element.95), channel_id=9, replica_groups={{0,32},{1,33},{2,34},{3,35},{4,36},{5,37},{6,38},{7,39},{8,40},{9,41},{..., dimensions={0}, use_global_device_ids=true | all-gather | bytes 61440 | tf_op jit(solution)/shard_map/all_gather | solution.py:207
  109.8 2.7 %all-gather.8 = f32[4,40,128]{2,1,0:T(8,128)S(1)} all-gather(f32[2,40,128]{2,1,0:T(8,128)S(1)} %bitcast.33), channel_id=10, replica_groups=mesh['x_hi'=2,'z'=8,'core'=2,'y'=8,'x_lo'=2] {'core'}, dimensions={0}, use_global_device_ids=true | all-gather | bytes 122880 | tf_op jit(solution)/shard_map/all_gather | solution.py:208
  112.5 0.9 shard_map.79
  113.5 2.1 all-to-all-done.5.ring_ref
  115.6 0.3 shard_map.80
  115.8 2.2 all-gather.9
  118.0 0.1 shard_map.81
  118.1 15.6 %all_to_all.63.got_ref = f32[16,40,128]{2,1,0:T(8,128)S(1)} all-to-all(f32[16,40,128]{2,1,0:T(8,128)S(1)} %shard_map.81), channel_id=1, replica_groups={{0,32,64,96,128,160,192,224,256,288,320,352,384,416,448,480},{2,34,66,9..., dimensions={0} | all-to-all | bytes 655360 | tf_op jit(solution)/shard_map/all_to_all | solution.py:204
  133.7 0.7 shard_map.82
  134.4 5.5 %all-to-all-start.7 = ((f32[32,8,128]{2,1,0:T(8,128)}), f32[32,8,128]{2,1,0:T(8,128)S(1)}, u32[]{:S(2)}, u32[]{:S(2)}) async-start(f32[32,8,128]{2,1,0:T(8,128)} %get-tuple-element.106), calls=%async_computation.7 | async-start | bytes 262144 | tf_op jit(solution)/shard_map/all_to_all | solution.py:206
  139.9 3.6 %all-gather.10 = f32[80,128]{1,0:T(8,128)S(1)} all-gather(f32[40,128]{1,0:T(8,128)S(1)} %get-tuple-element.107), channel_id=12, replica_groups={{0,32},{1,33},{2,34},{3,35},{4,36},{5,37},{6,38},{7,39},{8,40},{9,41},{..., dimensions={0}, use_global_device_ids=true | all-gather | bytes 61440 | tf_op jit(solution)/shard_map/all_gather | solution.py:207
  143.5 2.7 %all-gather.11 = f32[4,40,128]{2,1,0:T(8,128)S(1)} all-gather(f32[2,40,128]{2,1,0:T(8,128)S(1)} %bitcast.34), channel_id=13, replica_groups=mesh['x_hi'=2,'z'=8,'core'=2,'y'=8,'x_lo'=2] {'core'}, dimensions={0}, use_global_device_ids=true | all-gather | bytes 122880 | tf_op jit(solution)/shard_map/all_gather | solution.py:208
  146.2 0.9 shard_map.83
  147.1 2.1 all-to-all-done.7.ring_ref
  149.2 0.3 shard_map.84
  149.5 2.2 all-gather.12
  151.7 0.1 shard_map.85
  151.8 15.6 %all_to_all.64.got_ref = f32[16,40,128]{2,1,0:T(8,128)S(1)} all-to-all(f32[16,40,128]{2,1,0:T(8,128)S(1)} %shard_map.85), channel_id=1, replica_groups={{0,32,64,96,128,160,192,224,256,288,320,352,384,416,448,480},{2,34,66,9..., dimensions={0} | all-to-all | bytes 655360 | tf_op jit(solution)/shard_map/all_to_all | solution.py:204
  167.3 0.7 shard_map.86
  168.0 5.5 %all-to-all-start.9 = ((f32[32,8,128]{2,1,0:T(8,128)}), f32[32,8,128]{2,1,0:T(8,128)S(1)}, u32[]{:S(2)}, u32[]{:S(2)}) async-start(f32[32,8,128]{2,1,0:T(8,128)} %get-tuple-element.118), calls=%async_computation.9 | async-start | bytes 262144 | tf_op jit(solution)/shard_map/all_to_all | solution.py:206
  173.5 3.6 %all-gather.13 = f32[80,128]{1,0:T(8,128)S(1)} all-gather(f32[40,128]{1,0:T(8,128)S(1)} %get-tuple-element.119), channel_id=15, replica_groups={{0,32},{1,33},{2,34},{3,35},{4,36},{5,37},{6,38},{7,39},{8,40},{9,41},{..., dimensions={0}, use_global_device_ids=true | all-gather | bytes 61440 | tf_op jit(solution)/shard_map/all_gather | solution.py:207
  177.1 2.7 %all-gather.14 = f32[4,40,128]{2,1,0:T(8,128)S(1)} all-gather(f32[2,40,128]{2,1,0:T(8,128)S(1)} %bitcast.35), channel_id=16, replica_groups=mesh['x_hi'=2,'z'=8,'core'=2,'y'=8,'x_lo'=2] {'core'}, dimensions={0}, use_global_device_ids=true | all-gather | bytes 122880 | tf_op jit(solution)/shard_map/all_gather | solution.py:208
  179.9 0.9 shard_map.87
  180.8 2.1 all-to-all-done.9.ring_ref
  182.9 0.3 shard_map.88
  183.2 2.2 all-gather.15
  185.4 15.6 %all_to_all.65.got_ref = f32[16,40,128]{2,1,0:T(8,128)S(1)} all-to-all(f32[16,40,128]{2,1,0:T(8,128)S(1)} %shard_map.89), channel_id=1, replica_groups={{0,32,64,96,128,160,192,224,256,288,320,352,384,416,448,480},{2,34,66,9..., dimensions={0} | all-to-all | bytes 655360 | tf_op jit(solution)/shard_map/all_to_all | solution.py:204
  201.0 0.7 shard_map.90
  201.7 5.5 %all-to-all-start.11 = ((f32[32,8,128]{2,1,0:T(8,128)}), f32[32,8,128]{2,1,0:T(8,128)S(1)}, u32[]{:S(2)}, u32[]{:S(2)}) async-start(f32[32,8,128]{2,1,0:T(8,128)} %get-tuple-element.131), calls=%async_computation.11 | async-start | bytes 262144 | tf_op jit(solution)/shard_map/all_to_all | solution.py:206
  207.2 3.6 %all-gather.16 = f32[80,128]{1,0:T(8,128)S(1)} all-gather(f32[40,128]{1,0:T(8,128)S(1)} %get-tuple-element.130), channel_id=18, replica_groups={{0,32},{1,33},{2,34},{3,35},{4,36},{5,37},{6,38},{7,39},{8,40},{9,41},{..., dimensions={0}, use_global_device_ids=true | all-gather | bytes 61440 | tf_op jit(solution)/shard_map/all_gather | solution.py:207
  210.8 2.7 %all-gather.17 = f32[4,40,128]{2,1,0:T(8,128)S(1)} all-gather(f32[2,40,128]{2,1,0:T(8,128)S(1)} %bitcast.36), channel_id=19, replica_groups=mesh['x_hi'=2,'z'=8,'core'=2,'y'=8,'x_lo'=2] {'core'}, dimensions={0}, use_global_device_ids=true | all-gather | bytes 122880 | tf_op jit(solution)/shard_map/all_gather | solution.py:208
  213.5 3.0 %all-to-all-done.11.ring_ref = f32[32,8,128]{2,1,0:T(8,128)S(1)} async-done(((f32[32,8,128]{2,1,0:T(8,128)}), f32[32,8,128]{2,1,0:T(8,128)S(1)}, u32[]{:S(2)}, u32[]{:S(2)}) %all-to-all-start.11) | async-done | bytes 131104 | tf_op jit(solution)/shard_map/all_to_all | solution.py:206
  216.6 1.0 shard_map.91
  217.6 0.7 copy.12
  (7 shorter events, 0.2 us)
Async XLA Ops:
  0.6 0.7 copy-start.3
  1.4 1.2 copy-start
  2.6 0.8 copy-start.1
  2.6 0.8 copy-start.2
  26.0 22.3 %all-to-all-start.1 = ((f32[32,8,128]{2,1,0:T(8,128)}), f32[32,8,128]{2,1,0:T(8,128)S(1)}, u32[]{:S(2)}, u32[]{:S(2)}) async-start(f32[32,8,128]{2,1,0:T(8,128)} %get-tuple-element.73), calls=%async_computation.1 | async-start | bytes 262144 | tf_op jit(solution)/shard_map/all_to_all | solution.py:206
  67.0 14.9 %all-to-all-start.3 = ((f32[32,8,128]{2,1,0:T(8,128)}), f32[32,8,128]{2,1,0:T(8,128)S(1)}, u32[]{:S(2)}, u32[]{:S(2)}) async-start(f32[32,8,128]{2,1,0:T(8,128)} %get-tuple-element.82), calls=%async_computation.3 | async-start | bytes 262144 | tf_op jit(solution)/shard_map/all_to_all | solution.py:206
  100.7 14.9 %all-to-all-start.5 = ((f32[32,8,128]{2,1,0:T(8,128)}), f32[32,8,128]{2,1,0:T(8,128)S(1)}, u32[]{:S(2)}, u32[]{:S(2)}) async-start(f32[32,8,128]{2,1,0:T(8,128)} %get-tuple-element.94), calls=%async_computation.5 | async-start | bytes 262144 | tf_op jit(solution)/shard_map/all_to_all | solution.py:206
  134.4 14.9 %all-to-all-start.7 = ((f32[32,8,128]{2,1,0:T(8,128)}), f32[32,8,128]{2,1,0:T(8,128)S(1)}, u32[]{:S(2)}, u32[]{:S(2)}) async-start(f32[32,8,128]{2,1,0:T(8,128)} %get-tuple-element.106), calls=%async_computation.7 | async-start | bytes 262144 | tf_op jit(solution)/shard_map/all_to_all | solution.py:206
  168.0 14.9 %all-to-all-start.9 = ((f32[32,8,128]{2,1,0:T(8,128)}), f32[32,8,128]{2,1,0:T(8,128)S(1)}, u32[]{:S(2)}, u32[]{:S(2)}) async-start(f32[32,8,128]{2,1,0:T(8,128)} %get-tuple-element.118), calls=%async_computation.9 | async-start | bytes 262144 | tf_op jit(solution)/shard_map/all_to_all | solution.py:206
  201.7 14.9 %all-to-all-start.11 = ((f32[32,8,128]{2,1,0:T(8,128)}), f32[32,8,128]{2,1,0:T(8,128)S(1)}, u32[]{:S(2)}, u32[]{:S(2)}) async-start(f32[32,8,128]{2,1,0:T(8,128)} %get-tuple-element.131), calls=%async_computation.11 | async-start | bytes 262144 | tf_op jit(solution)/shard_map/all_to_all | solution.py:206

commit v7 on v6

--- a/solution.py
+++ b/solution.py
@@ -95,39 +95,63 @@
     return y, z, pack(gram_a, 0, 32), pack(gram_b, 0, 32), pack(part_c, 64, 8)
 
 
-def message(fc, y, z, gram_a, part_c, sent_ref):
-    part_a = jnp.zeros((32, 128), F32)
-    part_b = jnp.zeros((32, 256), F32)
-    for k in range(8):
-        weight = fc[:, k : k + 1]
-        part_a += weight * y[:, 128 * k : 128 * k + 128]
-        part_b += weight * z[:, 256 * k : 256 * k + 256]
-    sent_ref[0:32] = part_b[:, :128]
-    sent_ref[32:64] = part_b[:, 128:]
-    sent_ref[64:96] = part_a
-    sent_ref[96:104] = gram_a
-    sent_ref[104:112] = part_c
-
-
-def first_kernel(fa_ref, fb_ref, fc_ref, wz_ref, wy_ref, gram_ref, sent_ref):
-    y, z, gram_a, gram_b, part_c = multiply(fa_ref[...], fb_ref[...], wz_ref, wy_ref)
+def columns(wide):
+    square = (lax.broadcasted_iota(jnp.int32, (8, 8), 0) == lax.broadcasted_iota(jnp.int32, (8, 8), 1)).astype(F32)
+    return product(wide, square, (0, 0))
+
+
+def keep_or_send(core, products, keep_ref, send_ref, gram_ref):
+    y, z, gram_a, gram_b, part_c = products
+    for block in range(16):
+        rows = slice(32 * block, 32 * block + 32)
+        z_block = z[:, 128 * block : 128 * block + 128]
+        y_block = y[:, 128 * (block % 8) : 128 * (block % 8) + 128]
+        keep_ref[rows] = jnp.where(core == 0, z_block, y_block)
+        send_ref[rows] = jnp.where(core == 0, y_block, z_block)
+    send_ref[512:520] = gram_a
+    send_ref[520:528] = part_c
     gram_ref[...] = gram_b
-    message(fc_ref[...], y, z, gram_a, part_c, sent_ref)
-
-
-def chip_kernel(place_ref, both_ref, gram_ref, out_ref):
-    first = place_ref[0] == 0
-    low = jnp.where(first, both_ref[0, 0:32] + both_ref[1, 0:32], both_ref[0, 64:96])
-    high = jnp.where(first, both_ref[0, 32:64] + both_ref[1, 32:64], both_ref[1, 64:96])
-    gram = jnp.where(first, both_ref[0, 96:104] + both_ref[1, 96:104], gram_ref[...])
-    part_c = both_ref[0, 104:112] + both_ref[1, 104:112]
-    lane = lax.broadcasted_iota(jnp.int32, (8, 128), 1)
-    for h in range(2):
-        tile = jnp.where(lane < 64, pltpu.roll(gram, 64, 1) if h else gram, part_c)
-        for n in range(h, out_ref.shape[0], 2):
-            out_ref[n, 0:16] = low[16 * h : 16 * h + 16]
-            out_ref[n, 16:32] = high[16 * h : 16 * h + 16]
-            out_ref[n, 32:40] = tile
+
+
+def message(core, fc, both_ref, keep_ref, gram_ref, out_ref):
+    def write(low, high, gram):
+        part_c = both_ref[0, 520:528] + both_ref[1, 520:528]
+        lane = lax.broadcasted_iota(jnp.int32, (8, 128), 1)
+        for h in range(2):
+            tile = jnp.where(lane < 64, pltpu.roll(gram, 64, 1) if h else gram, part_c)
+            for n in range(h, out_ref.shape[0], 2):
+                out_ref[n, 0:16] = low[16 * h : 16 * h + 16]
+                out_ref[n, 16:32] = high[16 * h : 16 * h + 16]
+                out_ref[n, 32:40] = tile
+
+    @pl.when(core == 0)
+    def _():
+        low, high = (jnp.zeros((32, 128), F32), jnp.zeros((32, 128), F32))
+        for k in range(8):
+            weight = fc[:, k : k + 1]
+            low += weight * (keep_ref[64 * k : 64 * k + 32] + both_ref[1, 64 * k : 64 * k + 32])
+            high += weight * (keep_ref[64 * k + 32 : 64 * k + 64] + both_ref[1, 64 * k + 32 : 64 * k + 64])
+        write(low, high, both_ref[0, 512:520] + both_ref[1, 512:520])
+
+    @pl.when(core == 1)
+    def _():
+        low, high = (jnp.zeros((32, 128), F32), jnp.zeros((32, 128), F32))
+        for k in range(8):
+            weight = fc[:, k : k + 1]
+            low += weight * both_ref[0, 32 * k : 32 * k + 32]
+            high += weight * keep_ref[32 * k : 32 * k + 32]
+        write(low, high, gram_ref[...])
+
+
+def start_kernel(place_ref, t_ref, fa_ref, fb_ref, wz_ref, wy_ref, keep_ref, send_ref, gram_ref):
+    prepare(t_ref, wz_ref, wy_ref)
+    keep_or_send(place_ref[0], multiply(fa_ref[...], fb_ref[...], wz_ref, wy_ref), keep_ref, send_ref, gram_ref)
+
+
+def first_kernel(place_ref, fc_ref, both_ref, keep_ref, gram_ref, nc_ref, out_ref):
+    fc = columns(fc_ref[...])
+    nc_ref[...] = fc
+    message(place_ref[0], fc, both_ref, keep_ref, gram_ref, out_ref)
 
 
 def ring_kernel(got_ref, sum_ref, ring_ref):
@@ -139,31 +163,27 @@
         ring_ref[n] = total[32:]
 
 
-def factor_kernel(place_ref, both_ref, fa_ref, fb_ref, fc_ref, wz_ref, wy_ref, na_ref, nb_ref, gram_ref, base_ref, scale_ref, y_ref, z_ref, packs_ref):
-    fa, fb, base, scale = update(place_ref[0], both_ref, fa_ref[...], fb_ref[...], fc_ref[...])
+def factor_kernel(place_ref, both_ref, fa_ref, fb_ref, fc_ref, wz_ref, wy_ref, na_ref, nb_ref, base_ref, scale_ref, keep_ref, send_ref, gram_ref):
+    core = place_ref[0]
+    fa, fb, base, scale = update(core, both_ref, fa_ref[...], fb_ref[...], fc_ref[...])
     na_ref[...] = fa
     nb_ref[...] = fb
     base_ref[...] = base
     scale_ref[...] = jnp.broadcast_to(scale, (8, 128))
-    y, z, gram_a, gram_b, part_c = multiply(fa, fb, wz_ref, wy_ref)
-    y_ref[...] = y
-    z_ref[...] = z
-    gram_ref[...] = gram_b
-    packs_ref[0] = gram_a
-    packs_ref[1] = part_c
-
-
-def send_kernel(ring_ref, base_ref, scale_ref, y_ref, z_ref, packs_ref, nc_ref, sent_ref):
+    keep_or_send(core, multiply(fa, fb, wz_ref, wy_ref), keep_ref, send_ref, gram_ref)
+
+
+def chip_kernel(place_ref, ring_ref, base_ref, scale_ref, both_ref, keep_ref, gram_ref, nc_ref, out_ref):
     fc = add_mode_c(base_ref[...], scale_ref[:1, :1], ring_ref)
     nc_ref[...] = fc
-    message(fc, y_ref[...], z_ref[...], packs_ref[0], packs_ref[1], sent_ref)
+    message(place_ref[0], fc, both_ref, keep_ref, gram_ref, out_ref)
 
 
 def last_kernel(place_ref, both_ref, ring_ref, fa_ref, fb_ref, fc_ref, na_ref, nb_ref, nc_ref):
     fa, fb, base, scale = update(place_ref[0], both_ref, fa_ref[...], fb_ref[...], fc_ref[...])
     na_ref[...] = fa
     nb_ref[...] = fb
-    nc_ref[...] = add_mode_c(base, scale, ring_ref)
+    nc_ref[...] = add_mode_c(base, scale, ring_ref).T
 
 
 def call(kernel, outs, *args):
@@ -175,8 +195,8 @@
 
 
 A, B, C = (((32, 128), F32), ((32, 256), F32), ((32, 8), F32))
-TILE, SENT = (((8, 128), F32), ((112, 128), F32))
-PRODUCTS = [TILE, ((32, 1024), F32), ((32, 2048), F32), ((2, 8, 128), F32)]
+TILE = ((8, 128), F32)
+PRODUCTS = [((512, 128), F32), ((528, 128), F32), TILE]
 ALL = ("x_hi", "z", "core", "y", "x_lo")
 
 
@@ -196,22 +216,24 @@
     fa, fb, fc = (factor_a, factor_b, factor_c)
     place = lax.axis_index("core").reshape(1).astype(jnp.int32)
     rings, pairs = groups_of(size_z, size_y)
-    weights = call(prepare, [((256, 2048), BF16), ((2, 256, 1024), BF16)], tensor)
-    gram_b, sent = call(first_kernel, [TILE, SENT], fa, fb, fc, *weights)
+    out = ((2 * size_z, 40, 128), F32)
+    weights = [((256, 2048), BF16), ((2, 256, 1024), BF16)]
+    *weights, keep, send, gram_b = call(start_kernel, weights + PRODUCTS, place, tensor, fa, fb)
+    both = lax.all_gather(send, "core")
+    fc, sent = call(first_kernel, [C, out], place, fc.T, both, keep, gram_b)
     for step in range(ITERS):
-        both = lax.all_gather(sent, "core")
-        (sent,) = call(chip_kernel, [((2 * size_z, 40, 128), F32)], place, both, gram_b)
         got = lax.all_to_all(sent, ALL, 0, 0, axis_index_groups=rings)
         sums, ring = call(ring_kernel, [((40, 128), F32), ((4 * size_y, 8, 128), F32)], got)
         ring = lax.all_to_all(ring, ("core", "y", "x_lo"), 0, 0)
         both = lax.all_gather(sums, ALL, axis_index_groups=pairs)
         both = lax.all_gather(both, "core")
         if step < ITERS - 1:
-            fa, fb, gram_b, *rest = call(factor_kernel, [A, B, TILE, C] + PRODUCTS, place, both, fa, fb, fc, *weights)
-            fc, sent = call(send_kernel, [C, SENT], ring, *rest)
+            fa, fb, base, scale, keep, send, gram_b = call(factor_kernel, [A, B, C, TILE] + PRODUCTS, place, both, fa, fb, fc, *weights)
+            both = lax.all_gather(send, "core")
+            fc, sent = call(chip_kernel, [C, out], place, ring, base, scale, both, keep, gram_b)
         else:
-            fa, fb, fc = call(last_kernel, [A, B, C], place, both, ring, fa, fb, fc)
-    return (fa, fb, fc)
+            fa, fb, fc = call(last_kernel, [A, B, ((8, 32), F32)], place, both, ring, fa, fb, fc)
+    return (fa, fb, fc.T)
 
 
 def solution(mesh):

time: 219 us -> 222 us (1.014)
  blocking collectives: 148 us -> 159 us
  waiting for transfers between devices: 13.5 us -> 3.03 us
    all_to_all x6, blocking collectives: 90.7 us -> 101 us  [shards(): got = lax.all_to_all(sent, ALL, 0, 0, axis_index_groups=rings)]
    all_to_all x6, waiting for transfers between devices: 13.5 us -> 3.03 us  [shards(): ring = lax.all_to_all(ring, ('core', 'y', 'x_lo'), 0, 0)]
    pallas_call x25 -> x19, Pallas kernels: 12.7 us -> 12.4 us  [call(): pl.pallas_call(kernel, out_shape=shapes, in_specs=specs, out_specs=[VMEM]...]
  transfers between devices with their start and end apart: 6 -> 6, of which waited for: 6 -> 1; matrix products, arithmetic and copies ran while one was open for 0% -> 0% of each run, Pallas kernels for 2% -> 2%
where the time goes in v7:
time: 222 us; the launch traced here: 220 us
  blocking collectives  159 us (72%)
  starting transfers between devices  41.9 us (19%)
  Pallas kernels  12.4 us (6%)
  local copies, waits for them, and re-layouts  3.39 us (2%)
  waiting for transfers between devices  3.03 us (1%)
    all_to_all x6, blocking collectives, shards(): got = lax.all_to_all(sent, ALL, 0, 0, axis_index_groups=rings)  101 us
    all_to_all x6, starting transfers between devices, shards(): ring = lax.all_to_all(ring, ('core', 'y', 'x_lo'), 0, 0)  41.9 us
    all_gather x6, blocking collectives, shards(): both = lax.all_gather(sums, ALL, axis_index_groups=pairs)  21.6 us
    all_gather x6, blocking collectives, shards(): both = lax.all_gather(send, 'core')  19.6 us
    all_gather x6, blocking collectives, shards(): both = lax.all_gather(both, 'core')  16.5 us
    pallas_call x19, Pallas kernels, call(): pl.pallas_call(kernel, out_shape=shapes, in_specs=specs, out_specs=[VMEM]...  12.4 us
  transfers between devices with their start and end apart: 6, of which 1 were waited for; matrix products, arithmetic and copies ran while one was open for 0% of the time, Pallas kernels for 2%

profile of v7, /device:TPU:1, one launch (start us, length us, event | category | flops | bytes accessed | tf_op | source)
XLA Modules:
  0.0 220.5 jit_solution(2410737112909646929)
XLA Ops:
  0.6 0.0 copy-start
  0.6 1.2 copy-done
  1.9 0.0 copy-start.1
  1.9 0.8 copy-done.1
  2.6 0.0 copy-start.3
  2.6 0.7 copy-done.3
  3.3 0.9 shard_map.67
  4.2 8.7 %all-gather = f32[1056,128]{1,0:T(8,128)S(1)} all-gather(f32[528,128]{1,0:T(8,128)S(1)} %get-tuple-element.70), channel_id=2, replica_groups=mesh['x_hi'=2,'z'=8,'core'=2,'y'=8,'x_lo'=2] {'core'}, dimensions={0}, use_global_device_ids=true | all-gather | bytes 811008 | tf_op jit(solution)/shard_map/all_gather | solution.py:222
  12.9 0.7 copy-done.5
  13.6 0.3 shard_map.68
  14.0 12.8 %all_to_all.60.got_ref = f32[16,40,128]{2,1,0:T(8,128)S(1)} all-to-all(f32[16,40,128]{2,1,0:T(8,128)S(1)} %get-tuple-element.73), channel_id=1, replica_groups={{0,32,64,96,128,160,192,224,256,288,320,352,384,416,448,480},{2,34,66,9..., dimensions={0} | all-to-all | bytes 655360 | tf_op jit(solution)/shard_map/all_to_all | solution.py:225
  26.7 0.7 shard_map.69
  27.4 12.9 %all-to-all-start.1 = ((f32[32,8,128]{2,1,0:T(8,128)}), f32[32,8,128]{2,1,0:T(8,128)S(1)}, u32[]{:S(2)}, u32[]{:S(2)}) async-start(f32[32,8,128]{2,1,0:T(8,128)} %get-tuple-element.74), calls=%async_computation.1 | async-start | bytes 262144 | tf_op jit(solution)/shard_map/all_to_all | solution.py:227
  40.3 3.6 %all-gather.1 = f32[80,128]{1,0:T(8,128)S(1)} all-gather(f32[40,128]{1,0:T(8,128)S(1)} %get-tuple-element.75), channel_id=3, replica_groups={{0,32},{1,33},{2,34},{3,35},{4,36},{5,37},{6,38},{7,39},{8,40},{9,41},{..., dimensions={0}, use_global_device_ids=true | all-gather | bytes 61440 | tf_op jit(solution)/shard_map/all_gather | solution.py:228
  43.9 2.9 %all-gather.2 = f32[4,40,128]{2,1,0:T(8,128)S(1)} all-gather(f32[2,40,128]{2,1,0:T(8,128)S(1)} %bitcast.34), channel_id=4, replica_groups=mesh['x_hi'=2,'z'=8,'core'=2,'y'=8,'x_lo'=2] {'core'}, dimensions={0}, use_global_device_ids=true | all-gather | bytes 122880 | tf_op jit(solution)/shard_map/all_gather | solution.py:229
  46.8 0.0 copy-done.2
  46.8 0.0 copy-done.4
  46.8 0.9 shard_map.70
  47.7 2.2 all-gather.3
  49.9 0.0 all-to-all-done.1.ring_ref
  49.9 0.3 shard_map.71
  50.2 17.7 %all_to_all.61.got_ref = f32[16,40,128]{2,1,0:T(8,128)S(1)} all-to-all(f32[16,40,128]{2,1,0:T(8,128)S(1)} %get-tuple-element.84), channel_id=1, replica_groups={{0,32,64,96,128,160,192,224,256,288,320,352,384,416,448,480},{2,34,66,9..., dimensions={0} | all-to-all | bytes 655360 | tf_op jit(solution)/shard_map/all_to_all | solution.py:225
  67.9 0.7 shard_map.72
  68.6 5.8 %all-to-all-start.3 = ((f32[32,8,128]{2,1,0:T(8,128)}), f32[32,8,128]{2,1,0:T(8,128)S(1)}, u32[]{:S(2)}, u32[]{:S(2)}) async-start(f32[32,8,128]{2,1,0:T(8,128)} %get-tuple-element.85), calls=%async_computation.3 | async-start | bytes 262144 | tf_op jit(solution)/shard_map/all_to_all | solution.py:227
  74.4 3.6 %all-gather.4 = f32[80,128]{1,0:T(8,128)S(1)} all-gather(f32[40,128]{1,0:T(8,128)S(1)} %get-tuple-element.86), channel_id=6, replica_groups={{0,32},{1,33},{2,34},{3,35},{4,36},{5,37},{6,38},{7,39},{8,40},{9,41},{..., dimensions={0}, use_global_device_ids=true | all-gather | bytes 61440 | tf_op jit(solution)/shard_map/all_gather | solution.py:228
  78.0 2.7 %all-gather.5 = f32[4,40,128]{2,1,0:T(8,128)S(1)} all-gather(f32[2,40,128]{2,1,0:T(8,128)S(1)} %bitcast.35), channel_id=7, replica_groups=mesh['x_hi'=2,'z'=8,'core'=2,'y'=8,'x_lo'=2] {'core'}, dimensions={0}, use_global_device_ids=true | all-gather | bytes 122880 | tf_op jit(solution)/shard_map/all_gather | solution.py:229
  80.7 0.9 shard_map.73
  81.7 2.2 all-gather.6
  83.9 0.0 all-to-all-done.3.ring_ref
  83.9 0.3 shard_map.74
  84.2 17.7 %all_to_all.62.got_ref = f32[16,40,128]{2,1,0:T(8,128)S(1)} all-to-all(f32[16,40,128]{2,1,0:T(8,128)S(1)} %get-tuple-element.95), channel_id=1, replica_groups={{0,32,64,96,128,160,192,224,256,288,320,352,384,416,448,480},{2,34,66,9..., dimensions={0} | all-to-all | bytes 655360 | tf_op jit(solution)/shard_map/all_to_all | solution.py:225
  101.8 0.7 shard_map.75
  102.5 5.8 %all-to-all-start.5 = ((f32[32,8,128]{2,1,0:T(8,128)}), f32[32,8,128]{2,1,0:T(8,128)S(1)}, u32[]{:S(2)}, u32[]{:S(2)}) async-start(f32[32,8,128]{2,1,0:T(8,128)} %get-tuple-element.96), calls=%async_computation.5 | async-start | bytes 262144 | tf_op jit(solution)/shard_map/all_to_all | solution.py:227
  108.3 3.6 %all-gather.7 = f32[80,128]{1,0:T(8,128)S(1)} all-gather(f32[40,128]{1,0:T(8,128)S(1)} %get-tuple-element.97), channel_id=9, replica_groups={{0,32},{1,33},{2,34},{3,35},{4,36},{5,37},{6,38},{7,39},{8,40},{9,41},{..., dimensions={0}, use_global_device_ids=true | all-gather | bytes 61440 | tf_op jit(solution)/shard_map/all_gather | solution.py:228
  111.9 2.7 %all-gather.8 = f32[4,40,128]{2,1,0:T(8,128)S(1)} all-gather(f32[2,40,128]{2,1,0:T(8,128)S(1)} %bitcast.36), channel_id=10, replica_groups=mesh['x_hi'=2,'z'=8,'core'=2,'y'=8,'x_lo'=2] {'core'}, dimensions={0}, use_global_device_ids=true | all-gather | bytes 122880 | tf_op jit(solution)/shard_map/all_gather | solution.py:229
  114.7 0.9 shard_map.76
  115.6 2.2 all-gather.9
  117.8 0.0 all-to-all-done.5.ring_ref
  117.8 0.3 shard_map.77
  118.1 17.7 %all_to_all.63.got_ref = f32[16,40,128]{2,1,0:T(8,128)S(1)} all-to-all(f32[16,40,128]{2,1,0:T(8,128)S(1)} %get-tuple-element.106), channel_id=1, replica_groups={{0,32,64,96,128,160,192,224,256,288,320,352,384,416,448,480},{2,34,66,9..., dimensions={0} | all-to-all | bytes 655360 | tf_op jit(solution)/shard_map/all_to_all | solution.py:225
  135.8 0.7 shard_map.78
  136.4 5.8 %all-to-all-start.7 = ((f32[32,8,128]{2,1,0:T(8,128)}), f32[32,8,128]{2,1,0:T(8,128)S(1)}, u32[]{:S(2)}, u32[]{:S(2)}) async-start(f32[32,8,128]{2,1,0:T(8,128)} %get-tuple-element.107), calls=%async_computation.7 | async-start | bytes 262144 | tf_op jit(solution)/shard_map/all_to_all | solution.py:227
  142.2 3.6 %all-gather.10 = f32[80,128]{1,0:T(8,128)S(1)} all-gather(f32[40,128]{1,0:T(8,128)S(1)} %get-tuple-element.108), channel_id=12, replica_groups={{0,32},{1,33},{2,34},{3,35},{4,36},{5,37},{6,38},{7,39},{8,40},{9,41},{..., dimensions={0}, use_global_device_ids=true | all-gather | bytes 61440 | tf_op jit(solution)/shard_map/all_gather | solution.py:228
  145.8 2.7 %all-gather.11 = f32[4,40,128]{2,1,0:T(8,128)S(1)} all-gather(f32[2,40,128]{2,1,0:T(8,128)S(1)} %bitcast.37), channel_id=13, replica_groups=mesh['x_hi'=2,'z'=8,'core'=2,'y'=8,'x_lo'=2] {'core'}, dimensions={0}, use_global_device_ids=true | all-gather | bytes 122880 | tf_op jit(solution)/shard_map/all_gather | solution.py:229
  148.6 0.9 shard_map.79
  149.5 2.2 all-gather.12
  151.7 0.0 all-to-all-done.7.ring_ref
  151.7 0.3 shard_map.80
  152.0 17.7 %all_to_all.64.got_ref = f32[16,40,128]{2,1,0:T(8,128)S(1)} all-to-all(f32[16,40,128]{2,1,0:T(8,128)S(1)} %get-tuple-element.117), channel_id=1, replica_groups={{0,32,64,96,128,160,192,224,256,288,320,352,384,416,448,480},{2,34,66,9..., dimensions={0} | all-to-all | bytes 655360 | tf_op jit(solution)/shard_map/all_to_all | solution.py:225
  169.7 0.7 shard_map.81
  170.4 5.8 %all-to-all-start.9 = ((f32[32,8,128]{2,1,0:T(8,128)}), f32[32,8,128]{2,1,0:T(8,128)S(1)}, u32[]{:S(2)}, u32[]{:S(2)}) async-start(f32[32,8,128]{2,1,0:T(8,128)} %get-tuple-element.118), calls=%async_computation.9 | async-start | bytes 262144 | tf_op jit(solution)/shard_map/all_to_all | solution.py:227
  176.2 3.6 %all-gather.13 = f32[80,128]{1,0:T(8,128)S(1)} all-gather(f32[40,128]{1,0:T(8,128)S(1)} %get-tuple-element.119), channel_id=15, replica_groups={{0,32},{1,33},{2,34},{3,35},{4,36},{5,37},{6,38},{7,39},{8,40},{9,41},{..., dimensions={0}, use_global_device_ids=true | all-gather | bytes 61440 | tf_op jit(solution)/shard_map/all_gather | solution.py:228
  179.8 2.7 %all-gather.14 = f32[4,40,128]{2,1,0:T(8,128)S(1)} all-gather(f32[2,40,128]{2,1,0:T(8,128)S(1)} %bitcast.38), channel_id=16, replica_groups=mesh['x_hi'=2,'z'=8,'core'=2,'y'=8,'x_lo'=2] {'core'}, dimensions={0}, use_global_device_ids=true | all-gather | bytes 122880 | tf_op jit(solution)/shard_map/all_gather | solution.py:229
  182.5 0.9 shard_map.82
  183.4 2.2 all-gather.15
  185.6 0.0 all-to-all-done.9.ring_ref
  185.6 0.3 shard_map.83
  185.9 17.7 %all_to_all.65.got_ref = f32[16,40,128]{2,1,0:T(8,128)S(1)} all-to-all(f32[16,40,128]{2,1,0:T(8,128)S(1)} %get-tuple-element.128), channel_id=1, replica_groups={{0,32,64,96,128,160,192,224,256,288,320,352,384,416,448,480},{2,34,66,9..., dimensions={0} | all-to-all | bytes 655360 | tf_op jit(solution)/shard_map/all_to_all | solution.py:225
  203.6 0.7 shard_map.84
  204.3 5.8 %all-to-all-start.11 = ((f32[32,8,128]{2,1,0:T(8,128)}), f32[32,8,128]{2,1,0:T(8,128)S(1)}, u32[]{:S(2)}, u32[]{:S(2)}) async-start(f32[32,8,128]{2,1,0:T(8,128)} %get-tuple-element.130), calls=%async_computation.11 | async-start | bytes 262144 | tf_op jit(solution)/shard_map/all_to_all | solution.py:227
  210.1 3.6 %all-gather.16 = f32[80,128]{1,0:T(8,128)S(1)} all-gather(f32[40,128]{1,0:T(8,128)S(1)} %get-tuple-element.129), channel_id=18, replica_groups={{0,32},{1,33},{2,34},{3,35},{4,36},{5,37},{6,38},{7,39},{8,40},{9,41},{..., dimensions={0}, use_global_device_ids=true | all-gather | bytes 61440 | tf_op jit(solution)/shard_map/all_gather | solution.py:228
  213.7 2.7 %all-gather.17 = f32[4,40,128]{2,1,0:T(8,128)S(1)} all-gather(f32[2,40,128]{2,1,0:T(8,128)S(1)} %bitcast.39), channel_id=19, replica_groups=mesh['x_hi'=2,'z'=8,'core'=2,'y'=8,'x_lo'=2] {'core'}, dimensions={0}, use_global_device_ids=true | all-gather | bytes 122880 | tf_op jit(solution)/shard_map/all_gather | solution.py:229
  216.4 3.0 %all-to-all-done.11.ring_ref = f32[32,8,128]{2,1,0:T(8,128)S(1)} async-done(((f32[32,8,128]{2,1,0:T(8,128)}), f32[32,8,128]{2,1,0:T(8,128)S(1)}, u32[]{:S(2)}, u32[]{:S(2)}) %all-to-all-start.11) | async-done | bytes 131104 | tf_op jit(solution)/shard_map/all_to_all | solution.py:227
  219.4 1.0 shard_map.85
  (3 shorter events, 0.0 us)
Async XLA Ops:
  0.6 1.2 copy-start
  1.9 0.8 copy-start.1
  2.6 0.7 copy-start.3
  12.9 0.7 copy-start.5
  27.4 22.6 %all-to-all-start.1 = ((f32[32,8,128]{2,1,0:T(8,128)}), f32[32,8,128]{2,1,0:T(8,128)S(1)}, u32[]{:S(2)}, u32[]{:S(2)}) async-start(f32[32,8,128]{2,1,0:T(8,128)} %get-tuple-element.74), calls=%async_computation.1 | async-start | bytes 262144 | tf_op jit(solution)/shard_map/all_to_all | solution.py:227
  43.9 2.9 %copy-start.2 = (f32[32,256]{1,0:T(8,128)S(1)}, f32[32,256]{1,0:T(8,128)}, u32[]{:S(2)}) copy-start(f32[32,256]{1,0:T(8,128)} %fb_ref.3) | copy-start | bytes 98308
  43.9 2.9 %copy-start.4 = (f32[32,128]{1,0:T(8,128)S(1)}, f32[32,128]{1,0:T(8,128)}, u32[]{:S(2)}) copy-start(f32[32,128]{1,0:T(8,128)} %fa_ref.3) | copy-start | bytes 49156
  68.6 15.3 %all-to-all-start.3 = ((f32[32,8,128]{2,1,0:T(8,128)}), f32[32,8,128]{2,1,0:T(8,128)S(1)}, u32[]{:S(2)}, u32[]{:S(2)}) async-start(f32[32,8,128]{2,1,0:T(8,128)} %get-tuple-element.85), calls=%async_computation.3 | async-start | bytes 262144 | tf_op jit(solution)/shard_map/all_to_all | solution.py:227
  102.5 15.3 %all-to-all-start.5 = ((f32[32,8,128]{2,1,0:T(8,128)}), f32[32,8,128]{2,1,0:T(8,128)S(1)}, u32[]{:S(2)}, u32[]{:S(2)}) async-start(f32[32,8,128]{2,1,0:T(8,128)} %get-tuple-element.96), calls=%async_computation.5 | async-start | bytes 262144 | tf_op jit(solution)/shard_map/all_to_all | solution.py:227
  136.4 15.3 %all-to-all-start.7 = ((f32[32,8,128]{2,1,0:T(8,128)}), f32[32,8,128]{2,1,0:T(8,128)S(1)}, u32[]{:S(2)}, u32[]{:S(2)}) async-start(f32[32,8,128]{2,1,0:T(8,128)} %get-tuple-element.107), calls=%async_computation.7 | async-start | bytes 262144 | tf_op jit(solution)/shard_map/all_to_all | solution.py:227
  170.4 15.3 %all-to-all-start.9 = ((f32[32,8,128]{2,1,0:T(8,128)}), f32[32,8,128]{2,1,0:T(8,128)S(1)}, u32[]{:S(2)}, u32[]{:S(2)}) async-start(f32[32,8,128]{2,1,0:T(8,128)} %get-tuple-element.118), calls=%async_computation.9 | async-start | bytes 262144 | tf_op jit(solution)/shard_map/all_to_all | solution.py:227
  204.3 15.2 %all-to-all-start.11 = ((f32[32,8,128]{2,1,0:T(8,128)}), f32[32,8,128]{2,1,0:T(8,128)S(1)}, u32[]{:S(2)}, u32[]{:S(2)}) async-start(f32[32,8,128]{2,1,0:T(8,128)} %get-tuple-element.130), calls=%async_computation.11 | async-start | bytes 262144 | tf_op jit(solution)/shard_map/all_to_all | solution.py:227

commit v8 on v7

--- a/solution.py
+++ b/solution.py
@@ -70,10 +70,7 @@
     return next_a, next_b, fc - scale * product(h_c, fc), scale
 
 
-def add_mode_c(base, scale, ring_ref):
-    total = ring_ref[0]
-    for n in range(1, ring_ref.shape[0] // 2):
-        total += ring_ref[n]
+def add_mode_c(base, scale, total):
     mode_c = jnp.concatenate([total[:, 64 + 8 * q : 72 + 8 * q] for q in range(4)], 0)
     return base + scale * mode_c
 
@@ -110,16 +107,19 @@
         send_ref[rows] = jnp.where(core == 0, y_block, z_block)
     send_ref[512:520] = gram_a
     send_ref[520:528] = part_c
+    send_ref[528:536] = part_c
     gram_ref[...] = gram_b
 
 
 def message(core, fc, both_ref, keep_ref, gram_ref, out_ref):
-    def write(low, high, gram):
+    size = out_ref.shape[0]
+
+    def write(low, high, gram, slots):
         part_c = both_ref[0, 520:528] + both_ref[1, 520:528]
         lane = lax.broadcasted_iota(jnp.int32, (8, 128), 1)
         for h in range(2):
             tile = jnp.where(lane < 64, pltpu.roll(gram, 64, 1) if h else gram, part_c)
-            for n in range(h, out_ref.shape[0], 2):
+            for n in slots[h]:
                 out_ref[n, 0:16] = low[16 * h : 16 * h + 16]
                 out_ref[n, 16:32] = high[16 * h : 16 * h + 16]
                 out_ref[n, 32:40] = tile
@@ -131,7 +131,7 @@
             weight = fc[:, k : k + 1]
             low += weight * (keep_ref[64 * k : 64 * k + 32] + both_ref[1, 64 * k : 64 * k + 32])
             high += weight * (keep_ref[64 * k + 32 : 64 * k + 64] + both_ref[1, 64 * k + 32 : 64 * k + 64])
-        write(low, high, both_ref[0, 512:520] + both_ref[1, 512:520])
+        write(low, high, both_ref[0, 512:520] + both_ref[1, 512:520], [range(0, size, 2), range(1, size, 2)])
 
     @pl.when(core == 1)
     def _():
@@ -140,7 +140,7 @@
             weight = fc[:, k : k + 1]
             low += weight * both_ref[0, 32 * k : 32 * k + 32]
             high += weight * keep_ref[32 * k : 32 * k + 32]
-        write(low, high, gram_ref[...])
+        write(low, high, gram_ref[...], [range(size // 2), range(size // 2, size)])
 
 
 def start_kernel(place_ref, t_ref, fa_ref, fb_ref, wz_ref, wy_ref, keep_ref, send_ref, gram_ref):
@@ -173,17 +173,22 @@
     keep_or_send(core, multiply(fa, fb, wz_ref, wy_ref), keep_ref, send_ref, gram_ref)
 
 
-def chip_kernel(place_ref, ring_ref, base_ref, scale_ref, both_ref, keep_ref, gram_ref, nc_ref, out_ref):
-    fc = add_mode_c(base_ref[...], scale_ref[:1, :1], ring_ref)
+def chip_kernel(place_ref, base_ref, scale_ref, both_ref, keep_ref, gram_ref, nc_ref, out_ref):
+    fc = add_mode_c(base_ref[...], scale_ref[:1, :1], both_ref[0, 528:536])
     nc_ref[...] = fc
     message(place_ref[0], fc, both_ref, keep_ref, gram_ref, out_ref)
 
 
-def last_kernel(place_ref, both_ref, ring_ref, fa_ref, fb_ref, fc_ref, na_ref, nb_ref, nc_ref):
+def last_factor_kernel(place_ref, both_ref, fa_ref, fb_ref, fc_ref, na_ref, nb_ref, base_ref, scale_ref):
     fa, fb, base, scale = update(place_ref[0], both_ref, fa_ref[...], fb_ref[...], fc_ref[...])
     na_ref[...] = fa
     nb_ref[...] = fb
-    nc_ref[...] = add_mode_c(base, scale, ring_ref).T
+    base_ref[...] = base
+    scale_ref[...] = jnp.broadcast_to(scale, (8, 128))
+
+
+def last_c_kernel(total_ref, base_ref, scale_ref, nc_ref):
+    nc_ref[...] = add_mode_c(base_ref[...], scale_ref[:1, :1], total_ref[0]).T
 
 
 def call(kernel, outs, *args):
@@ -196,7 +201,7 @@
 
 A, B, C = (((32, 128), F32), ((32, 256), F32), ((32, 8), F32))
 TILE = ((8, 128), F32)
-PRODUCTS = [((512, 128), F32), ((528, 128), F32), TILE]
+PRODUCTS = [((512, 128), F32), ((536, 128), F32), TILE]
 ALL = ("x_hi", "z", "core", "y", "x_lo")
 
 
@@ -206,7 +211,7 @@
 
     two, zs, ys = (range(2), range(size_z), range(size_y))
     rings = [[at(h, z, 0, y, l) for h in two for z in zs] for l in two for y in ys]
-    rings += [[at(h, z, 1, y, l) for y in ys for l in two] for h in two for z in zs]
+    rings += [[at(h, z, 1, y, l) for l in two for y in ys] for h in two for z in zs]
     pairs = [[at(h, z, 0, y, l), at(h, z + 1, 0, y, l)] for h in two for z in zs[::2] for y in ys for l in two]
     pairs += [[at(h, z, 1, y, l) for l in two] for z in zs for y in ys for h in two]
     return rings, pairs
@@ -223,16 +228,19 @@
     fc, sent = call(first_kernel, [C, out], place, fc.T, both, keep, gram_b)
     for step in range(ITERS):
         got = lax.all_to_all(sent, ALL, 0, 0, axis_index_groups=rings)
-        sums, ring = call(ring_kernel, [((40, 128), F32), ((4 * size_y, 8, 128), F32)], got)
-        ring = lax.all_to_all(ring, ("core", "y", "x_lo"), 0, 0)
+        sums, ring = call(ring_kernel, [((40, 128), F32), ((2 * size_y, 8, 128), F32)], got)
+        ring = lax.all_to_all(ring, ("y", "x_lo"), 0, 0)
         both = lax.all_gather(sums, ALL, axis_index_groups=pairs)
         both = lax.all_gather(both, "core")
         if step < ITERS - 1:
             fa, fb, base, scale, keep, send, gram_b = call(factor_kernel, [A, B, C, TILE] + PRODUCTS, place, both, fa, fb, fc, *weights)
+            send = lax.dynamic_update_slice(send, ring.sum(0), (528, 0))
             both = lax.all_gather(send, "core")
-            fc, sent = call(chip_kernel, [C, out], place, ring, base, scale, both, keep, gram_b)
+            fc, sent = call(chip_kernel, [C, out], place, base, scale, both, keep, gram_b)
         else:
-            fa, fb, fc = call(last_kernel, [A, B, ((8, 32), F32)], place, both, ring, fa, fb, fc)
+            fa, fb, base, scale = call(last_factor_kernel, [A, B, C, TILE], place, both, fa, fb, fc)
+            total = lax.all_gather(ring.sum(0), "core")
+            (fc,) = call(last_c_kernel, [((8, 32), F32)], total, base, scale)
     return (fa, fb, fc.T)
 
 

time: 222 us -> 222 us (level)
  blocking collectives: 159 us -> 177 us
  starting transfers between devices: 41.9 us -> 26.5 us
  waiting for transfers between devices: 3.03 us -> 0.02 us
    all_gather x6, blocking collectives: 16.5 us -> 43.1 us  [shards(): both = lax.all_gather(both, 'core')]
    all_to_all x6, blocking collectives: 101 us -> 82.8 us  [shards(): got = lax.all_to_all(sent, ALL, 0, 0, axis_index_groups=rings)]
    all_to_all x6, starting transfers between devices: 41.9 us -> 26.5 us  [shards(): ring = lax.all_to_all(ring, ('y', 'x_lo'), 0, 0)]
    all_gather x6, blocking collectives: 19.6 us -> 27.6 us  [shards(): both = lax.all_gather(send, 'core')]
    all_gather x0 -> x1, blocking collectives: none -> 3.43 us  [shards(): total = lax.all_gather(ring.sum(0), 'core')]
    all_to_all x6, waiting for transfers between devices: 3.03 us -> 0.02 us  [shards(): ring = lax.all_to_all(ring, ('y', 'x_lo'), 0, 0)]
    pallas_call x19 -> x20, Pallas kernels: 12.4 us -> 12.9 us  [call(): pl.pallas_call(kernel, out_shape=shapes, in_specs=specs, out_specs=[VMEM]...]
  transfers between devices with their start and end apart: 6 -> 6, of which waited for: 1 -> 0; matrix products, arithmetic and copies ran while one was open for 0% -> 0% of each run, Pallas kernels for 2% -> 3%
where the time goes in v8:
time: 222 us; the launch traced here: 221 us
  blocking collectives  177 us (80%)
  starting transfers between devices  26.5 us (12%)
  Pallas kernels  12.9 us (6%)
  local copies, waits for them, and re-layouts  3.4 us (2%)
    all_to_all x6, blocking collectives, shards(): got = lax.all_to_all(sent, ALL, 0, 0, axis_index_groups=rings)  82.8 us
    all_gather x6, blocking collectives, shards(): both = lax.all_gather(both, 'core')  43.1 us
    all_gather x6, blocking collectives, shards(): both = lax.all_gather(send, 'core')  27.6 us
    all_to_all x6, starting transfers between devices, shards(): ring = lax.all_to_all(ring, ('y', 'x_lo'), 0, 0)  26.5 us
    all_gather x6, blocking collectives, shards(): both = lax.all_gather(sums, ALL, axis_index_groups=pairs)  19.9 us
    pallas_call x20, Pallas kernels, call(): pl.pallas_call(kernel, out_shape=shapes, in_specs=specs, out_specs=[VMEM]...  12.9 us
  transfers between devices with their start and end apart: 6, of which 0 were waited for; matrix products, arithmetic and copies ran while one was open for 0% of the time, Pallas kernels for 3%

profile of v8, /device:TPU:1, one launch (start us, length us, event | category | flops | bytes accessed | tf_op | source)
XLA Modules:
  0.0 220.6 jit_solution(10792175918671951350)
XLA Ops:
  0.6 0.0 copy-start
  0.6 1.2 copy-done
  1.9 0.8 copy-done.1
  2.6 0.7 copy-done.3
  3.3 0.9 shard_map.67
  4.2 8.7 %all-gather = f32[1072,128]{1,0:T(8,128)S(1)} all-gather(f32[536,128]{1,0:T(8,128)S(1)} %get-tuple-element.71), channel_id=2, replica_groups=mesh['x_hi'=2,'z'=8,'core'=2,'y'=8,'x_lo'=2] {'core'}, dimensions={0}, use_global_device_ids=true | all-gather | bytes 823296 | tf_op jit(solution)/shard_map/all_gather | solution.py:227
  12.9 0.7 copy-done.5
  13.6 0.3 shard_map.68
  14.0 10.8 %all_to_all.60.got_ref = f32[16,40,128]{2,1,0:T(8,128)S(1)} all-to-all(f32[16,40,128]{2,1,0:T(8,128)S(1)} %get-tuple-element.74), channel_id=1, replica_groups={{0,32,64,96,128,160,192,224,256,288,320,352,384,416,448,480},{2,34,66,9..., dimensions={0} | all-to-all | bytes 655360 | tf_op jit(solution)/shard_map/all_to_all | solution.py:230
  24.7 0.6 shard_map.69
  25.4 4.3 %all-to-all-start.1 = ((f32[16,8,128]{2,1,0:T(8,128)}), f32[16,8,128]{2,1,0:T(8,128)S(1)}, u32[]{:S(2)}, u32[]{:S(2)}) async-start(f32[16,8,128]{2,1,0:T(8,128)} %get-tuple-element.82), calls=%async_computation.1 | async-start | bytes 131072 | tf_op jit(solution)/shard_map/all_to_all | solution.py:232
  29.7 3.3 %all-gather.1 = f32[80,128]{1,0:T(8,128)S(1)} all-gather(f32[40,128]{1,0:T(8,128)S(1)} %get-tuple-element.75), channel_id=3, replica_groups={{0,32},{1,33},{2,34},{3,35},{4,36},{5,37},{6,38},{7,39},{8,40},{9,41},{..., dimensions={0}, use_global_device_ids=true | all-gather | bytes 61440 | tf_op jit(solution)/shard_map/all_gather | solution.py:233
  33.0 13.5 %all-gather.2 = f32[4,40,128]{2,1,0:T(8,128)S(1)} all-gather(f32[2,40,128]{2,1,0:T(8,128)S(1)} %bitcast.46), channel_id=4, replica_groups=mesh['x_hi'=2,'z'=8,'core'=2,'y'=8,'x_lo'=2] {'core'}, dimensions={0}, use_global_device_ids=true | all-gather | bytes 122880 | tf_op jit(solution)/shard_map/all_gather | solution.py:234
  46.5 0.0 copy-done.2
  46.5 0.0 copy-done.4
  46.5 0.9 shard_map.70
  47.4 0.0 all-to-all-done.1
  47.5 3.7 %all_gather.132.both_ref = f32[2,536,128]{2,1,0:T(8,128)S(1)} all-gather(f32[1,536,128]{2,1,0:T(8,128)S(1)} %bitcast_dynamic-update-slice_fusion.4), channel_id=1, replica_groups=mesh['x_hi'=2,'z'=8,'core'=2,'y'=8,'x_lo'=2] {'core'}, dimensions={0}, use_global_device_ids=true | all-gather | bytes 823296 | tf_op jit(solution)/shard_map/all_gather | solution.py:238
  51.2 0.3 shard_map.71
  51.4 14.5 %all_to_all.61.got_ref = f32[16,40,128]{2,1,0:T(8,128)S(1)} all-to-all(f32[16,40,128]{2,1,0:T(8,128)S(1)} %get-tuple-element.85), channel_id=1, replica_groups={{0,32,64,96,128,160,192,224,256,288,320,352,384,416,448,480},{2,34,66,9..., dimensions={0} | all-to-all | bytes 655360 | tf_op jit(solution)/shard_map/all_to_all | solution.py:230
  65.9 0.6 shard_map.72
  66.6 4.4 %all-to-all-start.3 = ((f32[16,8,128]{2,1,0:T(8,128)}), f32[16,8,128]{2,1,0:T(8,128)S(1)}, u32[]{:S(2)}, u32[]{:S(2)}) async-start(f32[16,8,128]{2,1,0:T(8,128)} %get-tuple-element.93), calls=%async_computation.3 | async-start | bytes 131072 | tf_op jit(solution)/shard_map/all_to_all | solution.py:232
  71.0 3.3 %all-gather.3 = f32[80,128]{1,0:T(8,128)S(1)} all-gather(f32[40,128]{1,0:T(8,128)S(1)} %get-tuple-element.86), channel_id=5, replica_groups={{0,32},{1,33},{2,34},{3,35},{4,36},{5,37},{6,38},{7,39},{8,40},{9,41},{..., dimensions={0}, use_global_device_ids=true | all-gather | bytes 61440 | tf_op jit(solution)/shard_map/all_gather | solution.py:233
  74.4 5.9 %all-gather.4 = f32[4,40,128]{2,1,0:T(8,128)S(1)} all-gather(f32[2,40,128]{2,1,0:T(8,128)S(1)} %bitcast.47), channel_id=6, replica_groups=mesh['x_hi'=2,'z'=8,'core'=2,'y'=8,'x_lo'=2] {'core'}, dimensions={0}, use_global_device_ids=true | all-gather | bytes 122880 | tf_op jit(solution)/shard_map/all_gather | solution.py:234
  80.3 0.9 shard_map.73
  81.2 0.0 all-to-all-done.3
  81.3 3.8 %all_gather.139.both_ref = f32[2,536,128]{2,1,0:T(8,128)S(1)} all-gather(f32[1,536,128]{2,1,0:T(8,128)S(1)} %bitcast_dynamic-update-slice_fusion.3), channel_id=1, replica_groups=mesh['x_hi'=2,'z'=8,'core'=2,'y'=8,'x_lo'=2] {'core'}, dimensions={0}, use_global_device_ids=true | all-gather | bytes 823296 | tf_op jit(solution)/shard_map/all_gather | solution.py:238
  85.1 0.3 shard_map.74
  85.3 14.4 %all_to_all.62.got_ref = f32[16,40,128]{2,1,0:T(8,128)S(1)} all-to-all(f32[16,40,128]{2,1,0:T(8,128)S(1)} %get-tuple-element.96), channel_id=1, replica_groups={{0,32,64,96,128,160,192,224,256,288,320,352,384,416,448,480},{2,34,66,9..., dimensions={0} | all-to-all | bytes 655360 | tf_op jit(solution)/shard_map/all_to_all | solution.py:230
  99.7 0.6 shard_map.75
  100.4 4.4 %all-to-all-start.5 = ((f32[16,8,128]{2,1,0:T(8,128)}), f32[16,8,128]{2,1,0:T(8,128)S(1)}, u32[]{:S(2)}, u32[]{:S(2)}) async-start(f32[16,8,128]{2,1,0:T(8,128)} %get-tuple-element.104), calls=%async_computation.5 | async-start | bytes 131072 | tf_op jit(solution)/shard_map/all_to_all | solution.py:232
  104.8 3.3 %all-gather.5 = f32[80,128]{1,0:T(8,128)S(1)} all-gather(f32[40,128]{1,0:T(8,128)S(1)} %get-tuple-element.97), channel_id=7, replica_groups={{0,32},{1,33},{2,34},{3,35},{4,36},{5,37},{6,38},{7,39},{8,40},{9,41},{..., dimensions={0}, use_global_device_ids=true | all-gather | bytes 61440 | tf_op jit(solution)/shard_map/all_gather | solution.py:233
  108.1 5.9 %all-gather.6 = f32[4,40,128]{2,1,0:T(8,128)S(1)} all-gather(f32[2,40,128]{2,1,0:T(8,128)S(1)} %bitcast.48), channel_id=8, replica_groups=mesh['x_hi'=2,'z'=8,'core'=2,'y'=8,'x_lo'=2] {'core'}, dimensions={0}, use_global_device_ids=true | all-gather | bytes 122880 | tf_op jit(solution)/shard_map/all_gather | solution.py:234
  114.0 0.9 shard_map.76
  115.0 0.0 all-to-all-done.5
  115.0 3.8 %all_gather.146.both_ref = f32[2,536,128]{2,1,0:T(8,128)S(1)} all-gather(f32[1,536,128]{2,1,0:T(8,128)S(1)} %bitcast_dynamic-update-slice_fusion.2), channel_id=1, replica_groups=mesh['x_hi'=2,'z'=8,'core'=2,'y'=8,'x_lo'=2] {'core'}, dimensions={0}, use_global_device_ids=true | all-gather | bytes 823296 | tf_op jit(solution)/shard_map/all_gather | solution.py:238
  118.8 0.3 shard_map.77
  119.1 14.4 %all_to_all.63.got_ref = f32[16,40,128]{2,1,0:T(8,128)S(1)} all-to-all(f32[16,40,128]{2,1,0:T(8,128)S(1)} %get-tuple-element.107), channel_id=1, replica_groups={{0,32,64,96,128,160,192,224,256,288,320,352,384,416,448,480},{2,34,66,9..., dimensions={0} | all-to-all | bytes 655360 | tf_op jit(solution)/shard_map/all_to_all | solution.py:230
  133.5 0.6 shard_map.78
  134.1 4.4 %all-to-all-start.7 = ((f32[16,8,128]{2,1,0:T(8,128)}), f32[16,8,128]{2,1,0:T(8,128)S(1)}, u32[]{:S(2)}, u32[]{:S(2)}) async-start(f32[16,8,128]{2,1,0:T(8,128)} %get-tuple-element.115), calls=%async_computation.7 | async-start | bytes 131072 | tf_op jit(solution)/shard_map/all_to_all | solution.py:232
  138.6 3.3 %all-gather.7 = f32[80,128]{1,0:T(8,128)S(1)} all-gather(f32[40,128]{1,0:T(8,128)S(1)} %get-tuple-element.108), channel_id=9, replica_groups={{0,32},{1,33},{2,34},{3,35},{4,36},{5,37},{6,38},{7,39},{8,40},{9,41},{..., dimensions={0}, use_global_device_ids=true | all-gather | bytes 61440 | tf_op jit(solution)/shard_map/all_gather | solution.py:233
  141.9 5.9 %all-gather.8 = f32[4,40,128]{2,1,0:T(8,128)S(1)} all-gather(f32[2,40,128]{2,1,0:T(8,128)S(1)} %bitcast.49), channel_id=10, replica_groups=mesh['x_hi'=2,'z'=8,'core'=2,'y'=8,'x_lo'=2] {'core'}, dimensions={0}, use_global_device_ids=true | all-gather | bytes 122880 | tf_op jit(solution)/shard_map/all_gather | solution.py:234
  147.8 0.9 shard_map.79
  148.8 0.0 all-to-all-done.7
  148.8 3.8 %all_gather.153.both_ref = f32[2,536,128]{2,1,0:T(8,128)S(1)} all-gather(f32[1,536,128]{2,1,0:T(8,128)S(1)} %bitcast_dynamic-update-slice_fusion.1), channel_id=1, replica_groups=mesh['x_hi'=2,'z'=8,'core'=2,'y'=8,'x_lo'=2] {'core'}, dimensions={0}, use_global_device_ids=true | all-gather | bytes 823296 | tf_op jit(solution)/shard_map/all_gather | solution.py:238
  152.6 0.3 shard_map.80
  152.9 14.4 %all_to_all.64.got_ref = f32[16,40,128]{2,1,0:T(8,128)S(1)} all-to-all(f32[16,40,128]{2,1,0:T(8,128)S(1)} %get-tuple-element.118), channel_id=1, replica_groups={{0,32,64,96,128,160,192,224,256,288,320,352,384,416,448,480},{2,34,66,9..., dimensions={0} | all-to-all | bytes 655360 | tf_op jit(solution)/shard_map/all_to_all | solution.py:230
  167.2 0.6 shard_map.81
  167.9 4.4 %all-to-all-start.9 = ((f32[16,8,128]{2,1,0:T(8,128)}), f32[16,8,128]{2,1,0:T(8,128)S(1)}, u32[]{:S(2)}, u32[]{:S(2)}) async-start(f32[16,8,128]{2,1,0:T(8,128)} %get-tuple-element.126), calls=%async_computation.9 | async-start | bytes 131072 | tf_op jit(solution)/shard_map/all_to_all | solution.py:232
  172.3 3.3 %all-gather.9 = f32[80,128]{1,0:T(8,128)S(1)} all-gather(f32[40,128]{1,0:T(8,128)S(1)} %get-tuple-element.119), channel_id=11, replica_groups={{0,32},{1,33},{2,34},{3,35},{4,36},{5,37},{6,38},{7,39},{8,40},{9,41},{..., dimensions={0}, use_global_device_ids=true | all-gather | bytes 61440 | tf_op jit(solution)/shard_map/all_gather | solution.py:233
  175.7 5.9 %all-gather.10 = f32[4,40,128]{2,1,0:T(8,128)S(1)} all-gather(f32[2,40,128]{2,1,0:T(8,128)S(1)} %bitcast.50), channel_id=12, replica_groups=mesh['x_hi'=2,'z'=8,'core'=2,'y'=8,'x_lo'=2] {'core'}, dimensions={0}, use_global_device_ids=true | all-gather | bytes 122880 | tf_op jit(solution)/shard_map/all_gather | solution.py:234
  181.6 0.9 shard_map.82
  182.5 0.0 all-to-all-done.9
  182.6 3.8 %all_gather.160.both_ref = f32[2,536,128]{2,1,0:T(8,128)S(1)} all-gather(f32[1,536,128]{2,1,0:T(8,128)S(1)} %bitcast_dynamic-update-slice_fusion), channel_id=1, replica_groups=mesh['x_hi'=2,'z'=8,'core'=2,'y'=8,'x_lo'=2] {'core'}, dimensions={0}, use_global_device_ids=true | all-gather | bytes 823296 | tf_op jit(solution)/shard_map/all_gather | solution.py:238
  186.4 0.3 shard_map.83
  186.6 14.4 %all_to_all.65.got_ref = f32[16,40,128]{2,1,0:T(8,128)S(1)} all-to-all(f32[16,40,128]{2,1,0:T(8,128)S(1)} %get-tuple-element.129), channel_id=1, replica_groups={{0,32,64,96,128,160,192,224,256,288,320,352,384,416,448,480},{2,34,66,9..., dimensions={0} | all-to-all | bytes 655360 | tf_op jit(solution)/shard_map/all_to_all | solution.py:230
  201.0 0.6 shard_map.84
  201.7 4.4 %all-to-all-start.11 = ((f32[16,8,128]{2,1,0:T(8,128)}), f32[16,8,128]{2,1,0:T(8,128)S(1)}, u32[]{:S(2)}, u32[]{:S(2)}) async-start(f32[16,8,128]{2,1,0:T(8,128)} %get-tuple-element.136), calls=%async_computation.11 | async-start | bytes 131072 | tf_op jit(solution)/shard_map/all_to_all | solution.py:232
  206.1 3.3 %all-gather.11 = f32[80,128]{1,0:T(8,128)S(1)} all-gather(f32[40,128]{1,0:T(8,128)S(1)} %get-tuple-element.130), channel_id=13, replica_groups={{0,32},{1,33},{2,34},{3,35},{4,36},{5,37},{6,38},{7,39},{8,40},{9,41},{..., dimensions={0}, use_global_device_ids=true | all-gather | bytes 61440 | tf_op jit(solution)/shard_map/all_gather | solution.py:233
  209.4 5.9 %all-gather.12 = f32[4,40,128]{2,1,0:T(8,128)S(1)} all-gather(f32[2,40,128]{2,1,0:T(8,128)S(1)} %bitcast.51), channel_id=14, replica_groups=mesh['x_hi'=2,'z'=8,'core'=2,'y'=8,'x_lo'=2] {'core'}, dimensions={0}, use_global_device_ids=true | all-gather | bytes 122880 | tf_op jit(solution)/shard_map/all_gather | solution.py:234
  215.3 1.0 shard_map.85
  216.3 0.0 all-to-all-done.11
  216.4 3.4 %all-gather.13 = f32[16,128]{1,0:T(8,128)S(1)} all-gather(f32[8,128]{1,0:T(8,128)S(1)} %reduce_sum.59), channel_id=15, replica_groups=mesh['x_hi'=2,'z'=8,'core'=2,'y'=8,'x_lo'=2] {'core'}, dimensions={0}, use_global_device_ids=true | all-gather | bytes 12288 | tf_op jit(solution)/shard_map/all_gather | solution.py:242
  219.8 0.8 shard_map.86
  (16 shorter events, 0.1 us)
Async XLA Ops:
  0.6 1.2 copy-start
  1.9 0.8 copy-start.1
  2.6 0.7 copy-start.3
  12.9 0.7 copy-start.5
  25.4 22.1 %all-to-all-start.1 = ((f32[16,8,128]{2,1,0:T(8,128)}), f32[16,8,128]{2,1,0:T(8,128)S(1)}, u32[]{:S(2)}, u32[]{:S(2)}) async-start(f32[16,8,128]{2,1,0:T(8,128)} %get-tuple-element.82), calls=%async_computation.1 | async-start | bytes 131072 | tf_op jit(solution)/shard_map/all_to_all | solution.py:232
  33.0 13.5 %copy-start.2 = (f32[32,256]{1,0:T(8,128)S(1)}, f32[32,256]{1,0:T(8,128)}, u32[]{:S(2)}) copy-start(f32[32,256]{1,0:T(8,128)} %fb_ref.3) | copy-start | bytes 98308
  33.0 13.5 %copy-start.4 = (f32[32,128]{1,0:T(8,128)S(1)}, f32[32,128]{1,0:T(8,128)}, u32[]{:S(2)}) copy-start(f32[32,128]{1,0:T(8,128)} %fa_ref.3) | copy-start | bytes 49156
  66.6 14.6 %all-to-all-start.3 = ((f32[16,8,128]{2,1,0:T(8,128)}), f32[16,8,128]{2,1,0:T(8,128)S(1)}, u32[]{:S(2)}, u32[]{:S(2)}) async-start(f32[16,8,128]{2,1,0:T(8,128)} %get-tuple-element.93), calls=%async_computation.3 | async-start | bytes 131072 | tf_op jit(solution)/shard_map/all_to_all | solution.py:232
  100.4 14.6 %all-to-all-start.5 = ((f32[16,8,128]{2,1,0:T(8,128)}), f32[16,8,128]{2,1,0:T(8,128)S(1)}, u32[]{:S(2)}, u32[]{:S(2)}) async-start(f32[16,8,128]{2,1,0:T(8,128)} %get-tuple-element.104), calls=%async_computation.5 | async-start | bytes 131072 | tf_op jit(solution)/shard_map/all_to_all | solution.py:232
  134.1 14.6 %all-to-all-start.7 = ((f32[16,8,128]{2,1,0:T(8,128)}), f32[16,8,128]{2,1,0:T(8,128)S(1)}, u32[]{:S(2)}, u32[]{:S(2)}) async-start(f32[16,8,128]{2,1,0:T(8,128)} %get-tuple-element.115), calls=%async_computation.7 | async-start | bytes 131072 | tf_op jit(solution)/shard_map/all_to_all | solution.py:232
  167.9 14.6 %all-to-all-start.9 = ((f32[16,8,128]{2,1,0:T(8,128)}), f32[16,8,128]{2,1,0:T(8,128)S(1)}, u32[]{:S(2)}, u32[]{:S(2)}) async-start(f32[16,8,128]{2,1,0:T(8,128)} %get-tuple-element.126), calls=%async_computation.9 | async-start | bytes 131072 | tf_op jit(solution)/shard_map/all_to_all | solution.py:232
  201.7 14.7 %all-to-all-start.11 = ((f32[16,8,128]{2,1,0:T(8,128)}), f32[16,8,128]{2,1,0:T(8,128)S(1)}, u32[]{:S(2)}, u32[]{:S(2)}) async-start(f32[16,8,128]{2,1,0:T(8,128)} %get-tuple-element.136), calls=%async_computation.11 | async-start | bytes 131072 | tf_op jit(solution)/shard_map/all_to_all | solution.py:232

commit v9 on v6

--- a/solution.py
+++ b/solution.py
@@ -109,10 +109,14 @@
     sent_ref[104:112] = part_c
 
 
-def first_kernel(fa_ref, fb_ref, fc_ref, wz_ref, wy_ref, gram_ref, sent_ref):
+def start_kernel(t_ref, fa_ref, fb_ref, fc_ref, wz_ref, wy_ref, nc_ref, gram_ref, sent_ref):
+    square = (lax.broadcasted_iota(jnp.int32, (8, 8), 0) == lax.broadcasted_iota(jnp.int32, (8, 8), 1)).astype(F32)
+    fc = product(fc_ref[...], square, (0, 0))
+    nc_ref[...] = fc
+    prepare(t_ref, wz_ref, wy_ref)
     y, z, gram_a, gram_b, part_c = multiply(fa_ref[...], fb_ref[...], wz_ref, wy_ref)
     gram_ref[...] = gram_b
-    message(fc_ref[...], y, z, gram_a, part_c, sent_ref)
+    message(fc, y, z, gram_a, part_c, sent_ref)
 
 
 def chip_kernel(place_ref, both_ref, gram_ref, out_ref):
@@ -122,12 +126,23 @@
     gram = jnp.where(first, both_ref[0, 96:104] + both_ref[1, 96:104], gram_ref[...])
     part_c = both_ref[0, 104:112] + both_ref[1, 104:112]
     lane = lax.broadcasted_iota(jnp.int32, (8, 128), 1)
-    for h in range(2):
-        tile = jnp.where(lane < 64, pltpu.roll(gram, 64, 1) if h else gram, part_c)
-        for n in range(h, out_ref.shape[0], 2):
-            out_ref[n, 0:16] = low[16 * h : 16 * h + 16]
-            out_ref[n, 16:32] = high[16 * h : 16 * h + 16]
-            out_ref[n, 32:40] = tile
+    size = out_ref.shape[0]
+    tiles = [jnp.where(lane < 64, pltpu.roll(gram, 64, 1) if h else gram, part_c) for h in range(2)]
+
+    def write(slots):
+        for h in range(2):
+            for n in slots[h]:
+                out_ref[n, 0:16] = low[16 * h : 16 * h + 16]
+                out_ref[n, 16:32] = high[16 * h : 16 * h + 16]
+                out_ref[n, 32:40] = tiles[h]
+
+    @pl.when(first)
+    def _():
+        write([range(0, size, 2), range(1, size, 2)])
+
+    @pl.when(jnp.logical_not(first))
+    def _():
+        write([range(size // 2), range(size // 2, size)])
 
 
 def ring_kernel(got_ref, sum_ref, ring_ref):
@@ -159,11 +174,16 @@
     message(fc, y_ref[...], z_ref[...], packs_ref[0], packs_ref[1], sent_ref)
 
 
-def last_kernel(place_ref, both_ref, ring_ref, fa_ref, fb_ref, fc_ref, na_ref, nb_ref, nc_ref):
+def last_factor_kernel(place_ref, both_ref, fa_ref, fb_ref, fc_ref, na_ref, nb_ref, base_ref, scale_ref):
     fa, fb, base, scale = update(place_ref[0], both_ref, fa_ref[...], fb_ref[...], fc_ref[...])
     na_ref[...] = fa
     nb_ref[...] = fb
-    nc_ref[...] = add_mode_c(base, scale, ring_ref)
+    base_ref[...] = base
+    scale_ref[...] = jnp.broadcast_to(scale, (8, 128))
+
+
+def last_c_kernel(ring_ref, base_ref, scale_ref, nc_ref):
+    nc_ref[...] = add_mode_c(base_ref[...], scale_ref[:1, :1], ring_ref).T
 
 
 def call(kernel, outs, *args):
@@ -186,7 +206,7 @@
 
     two, zs, ys = (range(2), range(size_z), range(size_y))
     rings = [[at(h, z, 0, y, l) for h in two for z in zs] for l in two for y in ys]
-    rings += [[at(h, z, 1, y, l) for y in ys for l in two] for h in two for z in zs]
+    rings += [[at(h, z, 1, y, l) for l in two for y in ys] for h in two for z in zs]
     pairs = [[at(h, z, 0, y, l), at(h, z + 1, 0, y, l)] for h in two for z in zs[::2] for y in ys for l in two]
     pairs += [[at(h, z, 1, y, l) for l in two] for z in zs for y in ys for h in two]
     return rings, pairs
@@ -196,8 +216,8 @@
     fa, fb, fc = (factor_a, factor_b, factor_c)
     place = lax.axis_index("core").reshape(1).astype(jnp.int32)
     rings, pairs = groups_of(size_z, size_y)
-    weights = call(prepare, [((256, 2048), BF16), ((2, 256, 1024), BF16)], tensor)
-    gram_b, sent = call(first_kernel, [TILE, SENT], fa, fb, fc, *weights)
+    weights = [((256, 2048), BF16), ((2, 256, 1024), BF16)]
+    *weights, fc, gram_b, sent = call(start_kernel, weights + [C, TILE, SENT], tensor, fa, fb, fc.T)
     for step in range(ITERS):
         both = lax.all_gather(sent, "core")
         (sent,) = call(chip_kernel, [((2 * size_z, 40, 128), F32)], place, both, gram_b)
@@ -210,8 +230,9 @@
             fa, fb, gram_b, *rest = call(factor_kernel, [A, B, TILE, C] + PRODUCTS, place, both, fa, fb, fc, *weights)
             fc, sent = call(send_kernel, [C, SENT], ring, *rest)
         else:
-            fa, fb, fc = call(last_kernel, [A, B, C], place, both, ring, fa, fb, fc)
-    return (fa, fb, fc)
+            fa, fb, base, scale = call(last_factor_kernel, [A, B, C, TILE], place, both, fa, fb, fc)
+            (fc,) = call(last_c_kernel, [((8, 32), F32)], ring, base, scale)
+    return (fa, fb, fc.T)
 
 
 def solution(mesh):

time: 219 us -> 219 us (level)
  starting transfers between devices: 40.5 us -> 52.8 us
  blocking collectives: 148 us -> 136 us
    all_to_all x6, starting transfers between devices: 40.5 us -> 52.8 us  [shards(): ring = lax.all_to_all(ring, ('core', 'y', 'x_lo'), 0, 0)]
    all_to_all x6, blocking collectives: 90.7 us -> 78.4 us  [shards(): got = lax.all_to_all(sent, ALL, 0, 0, axis_index_groups=rings)]
  transfers between devices with their start and end apart: 6 -> 6, of which waited for: 6 -> 6; matrix products, arithmetic and copies ran while one was open for 0% -> 0% of each run, Pallas kernels for 2% -> 3%
where the time goes in v9:
time: 219 us; the launch traced here: 218 us
  blocking collectives  136 us (62%)
  starting transfers between devices  52.8 us (24%)
  Pallas kernels  13.1 us (6%)
  waiting for transfers between devices  12.3 us (6%)
  local copies, waits for them, and re-layouts  3.38 us (2%)
    all_to_all x6, blocking collectives, shards(): got = lax.all_to_all(sent, ALL, 0, 0, axis_index_groups=rings)  78.4 us
    all_to_all x6, starting transfers between devices, shards(): ring = lax.all_to_all(ring, ('core', 'y', 'x_lo'), 0, 0)  52.8 us
    all_gather x6, blocking collectives, shards(): both = lax.all_gather(sums, ALL, axis_index_groups=pairs)  21.6 us
    all_gather x6, blocking collectives, shards(): both = lax.all_gather(sent, 'core')  19.3 us
    all_gather x6, blocking collectives, shards(): both = lax.all_gather(both, 'core')  16.5 us
    pallas_call x25, Pallas kernels, call(): pl.pallas_call(kernel, out_shape=shapes, in_specs=specs, out_specs=[VMEM]...  13.1 us
    all_to_all x6, waiting for transfers between devices, shards(): ring = lax.all_to_all(ring, ('core', 'y', 'x_lo'), 0, 0)  12.3 us
  transfers between devices with their start and end apart: 6, of which 6 were waited for; matrix products, arithmetic and copies ran while one was open for 0% of the time, Pallas kernels for 3%

profile of v9, /device:TPU:1, one launch (start us, length us, event | category | flops | bytes accessed | tf_op | source)
XLA Modules:
  0.0 218.3 jit_solution(798027112909022278)
XLA Ops:
  0.6 0.7 copy-done.5
  1.3 1.2 copy-done
  2.5 0.8 copy-done.1
  3.3 0.7 copy-done.3
  4.0 0.8 shard_map.67
  4.8 8.4 %all-gather = f32[224,128]{1,0:T(8,128)S(1)} all-gather(f32[112,128]{1,0:T(8,128)S(1)} %get-tuple-element.74), channel_id=2, replica_groups=mesh['x_hi'=2,'z'=8,'core'=2,'y'=8,'x_lo'=2] {'core'}, dimensions={0}, use_global_device_ids=true | all-gather | bytes 172032 | tf_op jit(solution)/shard_map/all_gather | solution.py:222
  13.3 0.1 shard_map.68
  13.4 10.8 %all_to_all.60.got_ref = f32[16,40,128]{2,1,0:T(8,128)S(1)} all-to-all(f32[16,40,128]{2,1,0:T(8,128)S(1)} %shard_map.68), channel_id=1, replica_groups={{0,32,64,96,128,160,192,224,256,288,320,352,384,416,448,480},{2,34,66,9..., dimensions={0} | all-to-all | bytes 655360 | tf_op jit(solution)/shard_map/all_to_all | solution.py:224
  24.1 0.7 shard_map.69
  24.8 14.9 %all-to-all-start.1 = ((f32[32,8,128]{2,1,0:T(8,128)}), f32[32,8,128]{2,1,0:T(8,128)S(1)}, u32[]{:S(2)}, u32[]{:S(2)}) async-start(f32[32,8,128]{2,1,0:T(8,128)} %get-tuple-element.76), calls=%async_computation.1 | async-start | bytes 262144 | tf_op jit(solution)/shard_map/all_to_all | solution.py:226
  39.7 3.6 %all-gather.1 = f32[80,128]{1,0:T(8,128)S(1)} all-gather(f32[40,128]{1,0:T(8,128)S(1)} %get-tuple-element.77), channel_id=3, replica_groups={{0,32},{1,33},{2,34},{3,35},{4,36},{5,37},{6,38},{7,39},{8,40},{9,41},{..., dimensions={0}, use_global_device_ids=true | all-gather | bytes 61440 | tf_op jit(solution)/shard_map/all_gather | solution.py:227
  43.3 2.9 %all-gather.2 = f32[4,40,128]{2,1,0:T(8,128)S(1)} all-gather(f32[2,40,128]{2,1,0:T(8,128)S(1)} %bitcast.34), channel_id=4, replica_groups=mesh['x_hi'=2,'z'=8,'core'=2,'y'=8,'x_lo'=2] {'core'}, dimensions={0}, use_global_device_ids=true | all-gather | bytes 122880 | tf_op jit(solution)/shard_map/all_gather | solution.py:228
  46.1 0.9 shard_map.70
  47.1 2.0 all-to-all-done.1.ring_ref
  49.0 0.3 shard_map.71
  49.3 2.2 all-gather.3
  51.5 0.1 shard_map.72
  51.6 13.6 %all_to_all.61.got_ref = f32[16,40,128]{2,1,0:T(8,128)S(1)} all-to-all(f32[16,40,128]{2,1,0:T(8,128)S(1)} %shard_map.72), channel_id=1, replica_groups={{0,32,64,96,128,160,192,224,256,288,320,352,384,416,448,480},{2,34,66,9..., dimensions={0} | all-to-all | bytes 655360 | tf_op jit(solution)/shard_map/all_to_all | solution.py:224
  65.2 0.7 shard_map.73
  65.9 7.6 %all-to-all-start.3 = ((f32[32,8,128]{2,1,0:T(8,128)}), f32[32,8,128]{2,1,0:T(8,128)S(1)}, u32[]{:S(2)}, u32[]{:S(2)}) async-start(f32[32,8,128]{2,1,0:T(8,128)} %get-tuple-element.88), calls=%async_computation.3 | async-start | bytes 262144 | tf_op jit(solution)/shard_map/all_to_all | solution.py:226
  73.5 3.6 %all-gather.4 = f32[80,128]{1,0:T(8,128)S(1)} all-gather(f32[40,128]{1,0:T(8,128)S(1)} %get-tuple-element.89), channel_id=6, replica_groups={{0,32},{1,33},{2,34},{3,35},{4,36},{5,37},{6,38},{7,39},{8,40},{9,41},{..., dimensions={0}, use_global_device_ids=true | all-gather | bytes 61440 | tf_op jit(solution)/shard_map/all_gather | solution.py:227
  77.1 2.7 %all-gather.5 = f32[4,40,128]{2,1,0:T(8,128)S(1)} all-gather(f32[2,40,128]{2,1,0:T(8,128)S(1)} %bitcast.35), channel_id=7, replica_groups=mesh['x_hi'=2,'z'=8,'core'=2,'y'=8,'x_lo'=2] {'core'}, dimensions={0}, use_global_device_ids=true | all-gather | bytes 122880 | tf_op jit(solution)/shard_map/all_gather | solution.py:228
  79.8 0.9 shard_map.74
  80.7 2.1 all-to-all-done.3.ring_ref
  82.8 0.3 shard_map.75
  83.1 2.2 all-gather.6
  85.3 0.1 shard_map.76
  85.4 13.5 %all_to_all.62.got_ref = f32[16,40,128]{2,1,0:T(8,128)S(1)} all-to-all(f32[16,40,128]{2,1,0:T(8,128)S(1)} %shard_map.76), channel_id=1, replica_groups={{0,32,64,96,128,160,192,224,256,288,320,352,384,416,448,480},{2,34,66,9..., dimensions={0} | all-to-all | bytes 655360 | tf_op jit(solution)/shard_map/all_to_all | solution.py:224
  98.9 0.7 shard_map.77
  99.5 7.6 %all-to-all-start.5 = ((f32[32,8,128]{2,1,0:T(8,128)}), f32[32,8,128]{2,1,0:T(8,128)S(1)}, u32[]{:S(2)}, u32[]{:S(2)}) async-start(f32[32,8,128]{2,1,0:T(8,128)} %get-tuple-element.100), calls=%async_computation.5 | async-start | bytes 262144 | tf_op jit(solution)/shard_map/all_to_all | solution.py:226
  107.1 3.6 %all-gather.7 = f32[80,128]{1,0:T(8,128)S(1)} all-gather(f32[40,128]{1,0:T(8,128)S(1)} %get-tuple-element.101), channel_id=9, replica_groups={{0,32},{1,33},{2,34},{3,35},{4,36},{5,37},{6,38},{7,39},{8,40},{9,41},{..., dimensions={0}, use_global_device_ids=true | all-gather | bytes 61440 | tf_op jit(solution)/shard_map/all_gather | solution.py:227
  110.7 2.7 %all-gather.8 = f32[4,40,128]{2,1,0:T(8,128)S(1)} all-gather(f32[2,40,128]{2,1,0:T(8,128)S(1)} %bitcast.36), channel_id=10, replica_groups=mesh['x_hi'=2,'z'=8,'core'=2,'y'=8,'x_lo'=2] {'core'}, dimensions={0}, use_global_device_ids=true | all-gather | bytes 122880 | tf_op jit(solution)/shard_map/all_gather | solution.py:228
  113.5 0.9 shard_map.78
  114.4 2.1 all-to-all-done.5.ring_ref
  116.5 0.3 shard_map.79
  116.8 2.2 all-gather.9
  118.9 0.1 shard_map.80
  119.0 13.5 %all_to_all.63.got_ref = f32[16,40,128]{2,1,0:T(8,128)S(1)} all-to-all(f32[16,40,128]{2,1,0:T(8,128)S(1)} %shard_map.80), channel_id=1, replica_groups={{0,32,64,96,128,160,192,224,256,288,320,352,384,416,448,480},{2,34,66,9..., dimensions={0} | all-to-all | bytes 655360 | tf_op jit(solution)/shard_map/all_to_all | solution.py:224
  132.5 0.7 shard_map.81
  133.2 7.6 %all-to-all-start.7 = ((f32[32,8,128]{2,1,0:T(8,128)}), f32[32,8,128]{2,1,0:T(8,128)S(1)}, u32[]{:S(2)}, u32[]{:S(2)}) async-start(f32[32,8,128]{2,1,0:T(8,128)} %get-tuple-element.112), calls=%async_computation.7 | async-start | bytes 262144 | tf_op jit(solution)/shard_map/all_to_all | solution.py:226
  140.8 3.6 %all-gather.10 = f32[80,128]{1,0:T(8,128)S(1)} all-gather(f32[40,128]{1,0:T(8,128)S(1)} %get-tuple-element.113), channel_id=12, replica_groups={{0,32},{1,33},{2,34},{3,35},{4,36},{5,37},{6,38},{7,39},{8,40},{9,41},{..., dimensions={0}, use_global_device_ids=true | all-gather | bytes 61440 | tf_op jit(solution)/shard_map/all_gather | solution.py:227
  144.4 2.7 %all-gather.11 = f32[4,40,128]{2,1,0:T(8,128)S(1)} all-gather(f32[2,40,128]{2,1,0:T(8,128)S(1)} %bitcast.37), channel_id=13, replica_groups=mesh['x_hi'=2,'z'=8,'core'=2,'y'=8,'x_lo'=2] {'core'}, dimensions={0}, use_global_device_ids=true | all-gather | bytes 122880 | tf_op jit(solution)/shard_map/all_gather | solution.py:228
  147.1 0.9 shard_map.82
  148.1 2.1 all-to-all-done.7.ring_ref
  150.1 0.3 shard_map.83
  150.4 2.2 all-gather.12
  152.6 0.1 shard_map.84
  152.7 13.5 %all_to_all.64.got_ref = f32[16,40,128]{2,1,0:T(8,128)S(1)} all-to-all(f32[16,40,128]{2,1,0:T(8,128)S(1)} %shard_map.84), channel_id=1, replica_groups={{0,32,64,96,128,160,192,224,256,288,320,352,384,416,448,480},{2,34,66,9..., dimensions={0} | all-to-all | bytes 655360 | tf_op jit(solution)/shard_map/all_to_all | solution.py:224
  166.2 0.7 shard_map.85
  166.9 7.6 %all-to-all-start.9 = ((f32[32,8,128]{2,1,0:T(8,128)}), f32[32,8,128]{2,1,0:T(8,128)S(1)}, u32[]{:S(2)}, u32[]{:S(2)}) async-start(f32[32,8,128]{2,1,0:T(8,128)} %get-tuple-element.124), calls=%async_computation.9 | async-start | bytes 262144 | tf_op jit(solution)/shard_map/all_to_all | solution.py:226
  174.4 3.6 %all-gather.13 = f32[80,128]{1,0:T(8,128)S(1)} all-gather(f32[40,128]{1,0:T(8,128)S(1)} %get-tuple-element.125), channel_id=15, replica_groups={{0,32},{1,33},{2,34},{3,35},{4,36},{5,37},{6,38},{7,39},{8,40},{9,41},{..., dimensions={0}, use_global_device_ids=true | all-gather | bytes 61440 | tf_op jit(solution)/shard_map/all_gather | solution.py:227
  178.1 2.7 %all-gather.14 = f32[4,40,128]{2,1,0:T(8,128)S(1)} all-gather(f32[2,40,128]{2,1,0:T(8,128)S(1)} %bitcast.38), channel_id=16, replica_groups=mesh['x_hi'=2,'z'=8,'core'=2,'y'=8,'x_lo'=2] {'core'}, dimensions={0}, use_global_device_ids=true | all-gather | bytes 122880 | tf_op jit(solution)/shard_map/all_gather | solution.py:228
  180.8 0.9 shard_map.86
  181.7 2.1 all-to-all-done.9.ring_ref
  183.8 0.3 shard_map.87
  184.1 2.2 all-gather.15
  186.4 13.5 %all_to_all.65.got_ref = f32[16,40,128]{2,1,0:T(8,128)S(1)} all-to-all(f32[16,40,128]{2,1,0:T(8,128)S(1)} %shard_map.88), channel_id=1, replica_groups={{0,32,64,96,128,160,192,224,256,288,320,352,384,416,448,480},{2,34,66,9..., dimensions={0} | all-to-all | bytes 655360 | tf_op jit(solution)/shard_map/all_to_all | solution.py:224
  199.8 0.7 shard_map.89
  200.5 7.6 %all-to-all-start.11 = ((f32[32,8,128]{2,1,0:T(8,128)}), f32[32,8,128]{2,1,0:T(8,128)S(1)}, u32[]{:S(2)}, u32[]{:S(2)}) async-start(f32[32,8,128]{2,1,0:T(8,128)} %get-tuple-element.142), calls=%async_computation.11 | async-start | bytes 262144 | tf_op jit(solution)/shard_map/all_to_all | solution.py:226
  208.1 3.6 %all-gather.16 = f32[80,128]{1,0:T(8,128)S(1)} all-gather(f32[40,128]{1,0:T(8,128)S(1)} %get-tuple-element.136), channel_id=18, replica_groups={{0,32},{1,33},{2,34},{3,35},{4,36},{5,37},{6,38},{7,39},{8,40},{9,41},{..., dimensions={0}, use_global_device_ids=true | all-gather | bytes 61440 | tf_op jit(solution)/shard_map/all_gather | solution.py:227
  211.7 2.7 %all-gather.17 = f32[4,40,128]{2,1,0:T(8,128)S(1)} all-gather(f32[2,40,128]{2,1,0:T(8,128)S(1)} %bitcast.39), channel_id=19, replica_groups=mesh['x_hi'=2,'z'=8,'core'=2,'y'=8,'x_lo'=2] {'core'}, dimensions={0}, use_global_device_ids=true | all-gather | bytes 122880 | tf_op jit(solution)/shard_map/all_gather | solution.py:228
  214.4 1.0 shard_map.90
  215.4 2.0 all-to-all-done.11.ring_ref
  217.5 0.8 shard_map.91
  (9 shorter events, 0.1 us)
Async XLA Ops:
  0.6 0.7 copy-start.5
  1.3 1.2 copy-start
  2.5 0.8 copy-start.1
  3.3 0.7 copy-start.3
  24.8 24.2 %all-to-all-start.1 = ((f32[32,8,128]{2,1,0:T(8,128)}), f32[32,8,128]{2,1,0:T(8,128)S(1)}, u32[]{:S(2)}, u32[]{:S(2)}) async-start(f32[32,8,128]{2,1,0:T(8,128)} %get-tuple-element.76), calls=%async_computation.1 | async-start | bytes 262144 | tf_op jit(solution)/shard_map/all_to_all | solution.py:226
  43.3 2.9 %copy-start.2 = (f32[32,256]{1,0:T(8,128)S(1)}, f32[32,256]{1,0:T(8,128)}, u32[]{:S(2)}) copy-start(f32[32,256]{1,0:T(8,128)} %fb_ref.3) | copy-start | bytes 98308
  43.3 2.9 %copy-start.4 = (f32[32,128]{1,0:T(8,128)S(1)}, f32[32,128]{1,0:T(8,128)}, u32[]{:S(2)}) copy-start(f32[32,128]{1,0:T(8,128)} %fa_ref.3) | copy-start | bytes 49156
  65.9 17.0 %all-to-all-start.3 = ((f32[32,8,128]{2,1,0:T(8,128)}), f32[32,8,128]{2,1,0:T(8,128)S(1)}, u32[]{:S(2)}, u32[]{:S(2)}) async-start(f32[32,8,128]{2,1,0:T(8,128)} %get-tuple-element.88), calls=%async_computation.3 | async-start | bytes 262144 | tf_op jit(solution)/shard_map/all_to_all | solution.py:226
  99.5 17.0 %all-to-all-start.5 = ((f32[32,8,128]{2,1,0:T(8,128)}), f32[32,8,128]{2,1,0:T(8,128)S(1)}, u32[]{:S(2)}, u32[]{:S(2)}) async-start(f32[32,8,128]{2,1,0:T(8,128)} %get-tuple-element.100), calls=%async_computation.5 | async-start | bytes 262144 | tf_op jit(solution)/shard_map/all_to_all | solution.py:226
  133.2 17.0 %all-to-all-start.7 = ((f32[32,8,128]{2,1,0:T(8,128)}), f32[32,8,128]{2,1,0:T(8,128)S(1)}, u32[]{:S(2)}, u32[]{:S(2)}) async-start(f32[32,8,128]{2,1,0:T(8,128)} %get-tuple-element.112), calls=%async_computation.7 | async-start | bytes 262144 | tf_op jit(solution)/shard_map/all_to_all | solution.py:226
  166.9 17.0 %all-to-all-start.9 = ((f32[32,8,128]{2,1,0:T(8,128)}), f32[32,8,128]{2,1,0:T(8,128)S(1)}, u32[]{:S(2)}, u32[]{:S(2)}) async-start(f32[32,8,128]{2,1,0:T(8,128)} %get-tuple-element.124), calls=%async_computation.9 | async-start | bytes 262144 | tf_op jit(solution)/shard_map/all_to_all | solution.py:226
  200.5 17.0 %all-to-all-start.11 = ((f32[32,8,128]{2,1,0:T(8,128)}), f32[32,8,128]{2,1,0:T(8,128)S(1)}, u32[]{:S(2)}, u32[]{:S(2)}) async-start(f32[32,8,128]{2,1,0:T(8,128)} %get-tuple-element.142), calls=%async_computation.11 | async-start | bytes 262144 | tf_op jit(solution)/shard_map/all_to_all | solution.py:226

commit v10 on v9

--- a/solution.py
+++ b/solution.py
@@ -109,11 +109,10 @@
     sent_ref[104:112] = part_c
 
 
-def start_kernel(t_ref, fa_ref, fb_ref, fc_ref, wz_ref, wy_ref, nc_ref, gram_ref, sent_ref):
+def start_kernel(fa_ref, fb_ref, fc_ref, wz_ref, wy_ref, nc_ref, gram_ref, sent_ref):
     square = (lax.broadcasted_iota(jnp.int32, (8, 8), 0) == lax.broadcasted_iota(jnp.int32, (8, 8), 1)).astype(F32)
     fc = product(fc_ref[...], square, (0, 0))
     nc_ref[...] = fc
-    prepare(t_ref, wz_ref, wy_ref)
     y, z, gram_a, gram_b, part_c = multiply(fa_ref[...], fb_ref[...], wz_ref, wy_ref)
     gram_ref[...] = gram_b
     message(fc, y, z, gram_a, part_c, sent_ref)
@@ -216,8 +215,8 @@
     fa, fb, fc = (factor_a, factor_b, factor_c)
     place = lax.axis_index("core").reshape(1).astype(jnp.int32)
     rings, pairs = groups_of(size_z, size_y)
-    weights = [((256, 2048), BF16), ((2, 256, 1024), BF16)]
-    *weights, fc, gram_b, sent = call(start_kernel, weights + [C, TILE, SENT], tensor, fa, fb, fc.T)
+    weights = call(prepare, [((256, 2048), BF16), ((2, 256, 1024), BF16)], tensor)
+    fc, gram_b, sent = call(start_kernel, [C, TILE, SENT], fa, fb, fc.T, *weights)
     for step in range(ITERS):
         both = lax.all_gather(sent, "core")
         (sent,) = call(chip_kernel, [((2 * size_z, 40, 128), F32)], place, both, gram_b)

time: 219 us -> 218 us (level)
    pallas_call x25 -> x26, Pallas kernels: 13.1 us -> 13.6 us  [call(): pl.pallas_call(kernel, out_shape=shapes, in_specs=specs, out_specs=[VMEM]...]
where the time goes in v10:
time: 218 us; the launch traced here: 217 us
  blocking collectives  136 us (62%)
  starting transfers between devices  52.8 us (24%)
  Pallas kernels  13.6 us (6%)
  waiting for transfers between devices  12.5 us (6%)
    all_to_all x6, blocking collectives, shards(): got = lax.all_to_all(sent, ALL, 0, 0, axis_index_groups=rings)  78.2 us
    all_to_all x6, starting transfers between devices, shards(): ring = lax.all_to_all(ring, ('core', 'y', 'x_lo'), 0, 0)  52.8 us
    all_gather x6, blocking collectives, shards(): both = lax.all_gather(sums, ALL, axis_index_groups=pairs)  21.6 us
    all_gather x6, blocking collectives, shards(): both = lax.all_gather(sent, 'core')  19.3 us
    all_gather x6, blocking collectives, shards(): both = lax.all_gather(both, 'core')  16.4 us
    pallas_call x26, Pallas kernels, call(): pl.pallas_call(kernel, out_shape=shapes, in_specs=specs, out_specs=[VMEM]...  13.6 us
    all_to_all x6, waiting for transfers between devices, shards(): ring = lax.all_to_all(ring, ('core', 'y', 'x_lo'), 0, 0)  12.5 us
  transfers between devices with their start and end apart: 6, of which 6 were waited for; matrix products, arithmetic and copies ran while one was open for 0% of the time, Pallas kernels for 3%

profile of v10, /device:TPU:1, one launch (start us, length us, event | category | flops | bytes accessed | tf_op | source)
XLA Modules:
  0.0 217.1 jit_solution(14558656155779607661)
XLA Ops:
  0.6 1.2 copy-done
  1.9 0.6 shard_map.67
  2.4 0.2 copy-done.1
  2.6 0.5 copy-done.3
  3.1 0.6 shard_map.68
  3.8 8.4 %all-gather = f32[224,128]{1,0:T(8,128)S(1)} all-gather(f32[112,128]{1,0:T(8,128)S(1)} %get-tuple-element.76), channel_id=2, replica_groups=mesh['x_hi'=2,'z'=8,'core'=2,'y'=8,'x_lo'=2] {'core'}, dimensions={0}, use_global_device_ids=true | all-gather | bytes 172032 | tf_op jit(solution)/shard_map/all_gather | solution.py:221
  12.2 0.1 shard_map.69
  12.3 10.8 %all_to_all.60.got_ref = f32[16,40,128]{2,1,0:T(8,128)S(1)} all-to-all(f32[16,40,128]{2,1,0:T(8,128)S(1)} %shard_map.69), channel_id=1, replica_groups={{0,32,64,96,128,160,192,224,256,288,320,352,384,416,448,480},{2,34,66,9..., dimensions={0} | all-to-all | bytes 655360 | tf_op jit(solution)/shard_map/all_to_all | solution.py:223
  23.1 0.7 shard_map.70
  23.7 14.8 %all-to-all-start.1 = ((f32[32,8,128]{2,1,0:T(8,128)}), f32[32,8,128]{2,1,0:T(8,128)S(1)}, u32[]{:S(2)}, u32[]{:S(2)}) async-start(f32[32,8,128]{2,1,0:T(8,128)} %get-tuple-element.78), calls=%async_computation.1 | async-start | bytes 262144 | tf_op jit(solution)/shard_map/all_to_all | solution.py:225
  38.6 3.6 %all-gather.1 = f32[80,128]{1,0:T(8,128)S(1)} all-gather(f32[40,128]{1,0:T(8,128)S(1)} %get-tuple-element.79), channel_id=3, replica_groups={{0,32},{1,33},{2,34},{3,35},{4,36},{5,37},{6,38},{7,39},{8,40},{9,41},{..., dimensions={0}, use_global_device_ids=true | all-gather | bytes 61440 | tf_op jit(solution)/shard_map/all_gather | solution.py:226
  42.2 2.7 %all-gather.2 = f32[4,40,128]{2,1,0:T(8,128)S(1)} all-gather(f32[2,40,128]{2,1,0:T(8,128)S(1)} %bitcast.34), channel_id=4, replica_groups=mesh['x_hi'=2,'z'=8,'core'=2,'y'=8,'x_lo'=2] {'core'}, dimensions={0}, use_global_device_ids=true | all-gather | bytes 122880 | tf_op jit(solution)/shard_map/all_gather | solution.py:227
  44.9 0.9 shard_map.71
  45.9 2.1 all-to-all-done.1.ring_ref
  48.0 0.3 shard_map.72
  48.2 2.2 %all-gather.3 = f32[224,128]{1,0:T(8,128)S(1)} all-gather(f32[112,128]{1,0:T(8,128)S(1)} %get-tuple-element.86), channel_id=5, replica_groups=mesh['x_hi'=2,'z'=8,'core'=2,'y'=8,'x_lo'=2] {'core'}, dimensions={0}, use_global_device_ids=true | all-gather | bytes 172032 | tf_op jit(solution)/shard_map/all_gather | solution.py:221
  50.4 0.1 shard_map.73
  50.5 13.5 %all_to_all.61.got_ref = f32[16,40,128]{2,1,0:T(8,128)S(1)} all-to-all(f32[16,40,128]{2,1,0:T(8,128)S(1)} %shard_map.73), channel_id=1, replica_groups={{0,32,64,96,128,160,192,224,256,288,320,352,384,416,448,480},{2,34,66,9..., dimensions={0} | all-to-all | bytes 655360 | tf_op jit(solution)/shard_map/all_to_all | solution.py:223
  64.0 0.7 shard_map.74
  64.7 7.6 %all-to-all-start.3 = ((f32[32,8,128]{2,1,0:T(8,128)}), f32[32,8,128]{2,1,0:T(8,128)S(1)}, u32[]{:S(2)}, u32[]{:S(2)}) async-start(f32[32,8,128]{2,1,0:T(8,128)} %get-tuple-element.88), calls=%async_computation.3 | async-start | bytes 262144 | tf_op jit(solution)/shard_map/all_to_all | solution.py:225
  72.3 3.6 %all-gather.4 = f32[80,128]{1,0:T(8,128)S(1)} all-gather(f32[40,128]{1,0:T(8,128)S(1)} %get-tuple-element.89), channel_id=6, replica_groups={{0,32},{1,33},{2,34},{3,35},{4,36},{5,37},{6,38},{7,39},{8,40},{9,41},{..., dimensions={0}, use_global_device_ids=true | all-gather | bytes 61440 | tf_op jit(solution)/shard_map/all_gather | solution.py:226
  75.9 2.7 %all-gather.5 = f32[4,40,128]{2,1,0:T(8,128)S(1)} all-gather(f32[2,40,128]{2,1,0:T(8,128)S(1)} %bitcast.35), channel_id=7, replica_groups=mesh['x_hi'=2,'z'=8,'core'=2,'y'=8,'x_lo'=2] {'core'}, dimensions={0}, use_global_device_ids=true | all-gather | bytes 122880 | tf_op jit(solution)/shard_map/all_gather | solution.py:227
  78.6 0.9 shard_map.75
  79.5 2.1 all-to-all-done.3.ring_ref
  81.6 0.3 shard_map.76
  81.9 2.2 %all-gather.6 = f32[224,128]{1,0:T(8,128)S(1)} all-gather(f32[112,128]{1,0:T(8,128)S(1)} %get-tuple-element.98), channel_id=8, replica_groups=mesh['x_hi'=2,'z'=8,'core'=2,'y'=8,'x_lo'=2] {'core'}, dimensions={0}, use_global_device_ids=true | all-gather | bytes 172032 | tf_op jit(solution)/shard_map/all_gather | solution.py:221
  84.1 0.1 shard_map.77
  84.2 13.5 %all_to_all.62.got_ref = f32[16,40,128]{2,1,0:T(8,128)S(1)} all-to-all(f32[16,40,128]{2,1,0:T(8,128)S(1)} %shard_map.77), channel_id=1, replica_groups={{0,32,64,96,128,160,192,224,256,288,320,352,384,416,448,480},{2,34,66,9..., dimensions={0} | all-to-all | bytes 655360 | tf_op jit(solution)/shard_map/all_to_all | solution.py:223
  97.7 0.7 shard_map.78
  98.3 7.6 %all-to-all-start.5 = ((f32[32,8,128]{2,1,0:T(8,128)}), f32[32,8,128]{2,1,0:T(8,128)S(1)}, u32[]{:S(2)}, u32[]{:S(2)}) async-start(f32[32,8,128]{2,1,0:T(8,128)} %get-tuple-element.100), calls=%async_computation.5 | async-start | bytes 262144 | tf_op jit(solution)/shard_map/all_to_all | solution.py:225
  105.9 3.6 %all-gather.7 = f32[80,128]{1,0:T(8,128)S(1)} all-gather(f32[40,128]{1,0:T(8,128)S(1)} %get-tuple-element.101), channel_id=9, replica_groups={{0,32},{1,33},{2,34},{3,35},{4,36},{5,37},{6,38},{7,39},{8,40},{9,41},{..., dimensions={0}, use_global_device_ids=true | all-gather | bytes 61440 | tf_op jit(solution)/shard_map/all_gather | solution.py:226
  109.5 2.7 %all-gather.8 = f32[4,40,128]{2,1,0:T(8,128)S(1)} all-gather(f32[2,40,128]{2,1,0:T(8,128)S(1)} %bitcast.36), channel_id=10, replica_groups=mesh['x_hi'=2,'z'=8,'core'=2,'y'=8,'x_lo'=2] {'core'}, dimensions={0}, use_global_device_ids=true | all-gather | bytes 122880 | tf_op jit(solution)/shard_map/all_gather | solution.py:227
  112.3 0.9 shard_map.79
  113.2 2.1 all-to-all-done.5.ring_ref
  115.3 0.3 shard_map.80
  115.6 2.2 %all-gather.9 = f32[224,128]{1,0:T(8,128)S(1)} all-gather(f32[112,128]{1,0:T(8,128)S(1)} %get-tuple-element.110), channel_id=11, replica_groups=mesh['x_hi'=2,'z'=8,'core'=2,'y'=8,'x_lo'=2] {'core'}, dimensions={0}, use_global_device_ids=true | all-gather | bytes 172032 | tf_op jit(solution)/shard_map/all_gather | solution.py:221
  117.7 0.1 shard_map.81
  117.8 13.5 %all_to_all.63.got_ref = f32[16,40,128]{2,1,0:T(8,128)S(1)} all-to-all(f32[16,40,128]{2,1,0:T(8,128)S(1)} %shard_map.81), channel_id=1, replica_groups={{0,32,64,96,128,160,192,224,256,288,320,352,384,416,448,480},{2,34,66,9..., dimensions={0} | all-to-all | bytes 655360 | tf_op jit(solution)/shard_map/all_to_all | solution.py:223
  131.3 0.7 shard_map.82
  132.0 7.6 %all-to-all-start.7 = ((f32[32,8,128]{2,1,0:T(8,128)}), f32[32,8,128]{2,1,0:T(8,128)S(1)}, u32[]{:S(2)}, u32[]{:S(2)}) async-start(f32[32,8,128]{2,1,0:T(8,128)} %get-tuple-element.112), calls=%async_computation.7 | async-start | bytes 262144 | tf_op jit(solution)/shard_map/all_to_all | solution.py:225
  139.6 3.6 %all-gather.10 = f32[80,128]{1,0:T(8,128)S(1)} all-gather(f32[40,128]{1,0:T(8,128)S(1)} %get-tuple-element.113), channel_id=12, replica_groups={{0,32},{1,33},{2,34},{3,35},{4,36},{5,37},{6,38},{7,39},{8,40},{9,41},{..., dimensions={0}, use_global_device_ids=true | all-gather | bytes 61440 | tf_op jit(solution)/shard_map/all_gather | solution.py:226
  143.2 2.7 %all-gather.11 = f32[4,40,128]{2,1,0:T(8,128)S(1)} all-gather(f32[2,40,128]{2,1,0:T(8,128)S(1)} %bitcast.37), channel_id=13, replica_groups=mesh['x_hi'=2,'z'=8,'core'=2,'y'=8,'x_lo'=2] {'core'}, dimensions={0}, use_global_device_ids=true | all-gather | bytes 122880 | tf_op jit(solution)/shard_map/all_gather | solution.py:227
  145.9 0.9 shard_map.83
  146.9 2.1 all-to-all-done.7.ring_ref
  149.0 0.3 shard_map.84
  149.2 2.2 %all-gather.12 = f32[224,128]{1,0:T(8,128)S(1)} all-gather(f32[112,128]{1,0:T(8,128)S(1)} %get-tuple-element.122), channel_id=14, replica_groups=mesh['x_hi'=2,'z'=8,'core'=2,'y'=8,'x_lo'=2] {'core'}, dimensions={0}, use_global_device_ids=true | all-gather | bytes 172032 | tf_op jit(solution)/shard_map/all_gather | solution.py:221
  151.5 13.5 %all_to_all.64.got_ref = f32[16,40,128]{2,1,0:T(8,128)S(1)} all-to-all(f32[16,40,128]{2,1,0:T(8,128)S(1)} %shard_map.85), channel_id=1, replica_groups={{0,32,64,96,128,160,192,224,256,288,320,352,384,416,448,480},{2,34,66,9..., dimensions={0} | all-to-all | bytes 655360 | tf_op jit(solution)/shard_map/all_to_all | solution.py:223
  165.0 0.7 shard_map.86
  165.7 7.6 %all-to-all-start.9 = ((f32[32,8,128]{2,1,0:T(8,128)}), f32[32,8,128]{2,1,0:T(8,128)S(1)}, u32[]{:S(2)}, u32[]{:S(2)}) async-start(f32[32,8,128]{2,1,0:T(8,128)} %get-tuple-element.124), calls=%async_computation.9 | async-start | bytes 262144 | tf_op jit(solution)/shard_map/all_to_all | solution.py:225
  173.3 3.6 %all-gather.13 = f32[80,128]{1,0:T(8,128)S(1)} all-gather(f32[40,128]{1,0:T(8,128)S(1)} %get-tuple-element.125), channel_id=15, replica_groups={{0,32},{1,33},{2,34},{3,35},{4,36},{5,37},{6,38},{7,39},{8,40},{9,41},{..., dimensions={0}, use_global_device_ids=true | all-gather | bytes 61440 | tf_op jit(solution)/shard_map/all_gather | solution.py:226
  176.9 2.7 %all-gather.14 = f32[4,40,128]{2,1,0:T(8,128)S(1)} all-gather(f32[2,40,128]{2,1,0:T(8,128)S(1)} %bitcast.38), channel_id=16, replica_groups=mesh['x_hi'=2,'z'=8,'core'=2,'y'=8,'x_lo'=2] {'core'}, dimensions={0}, use_global_device_ids=true | all-gather | bytes 122880 | tf_op jit(solution)/shard_map/all_gather | solution.py:227
  179.6 0.9 shard_map.87
  180.5 2.1 all-to-all-done.9.ring_ref
  182.6 0.3 shard_map.88
  182.9 2.2 %all-gather.15 = f32[224,128]{1,0:T(8,128)S(1)} all-gather(f32[112,128]{1,0:T(8,128)S(1)} %get-tuple-element.134), channel_id=17, replica_groups=mesh['x_hi'=2,'z'=8,'core'=2,'y'=8,'x_lo'=2] {'core'}, dimensions={0}, use_global_device_ids=true | all-gather | bytes 172032 | tf_op jit(solution)/shard_map/all_gather | solution.py:221
  185.1 0.1 shard_map.89
  185.2 13.5 %all_to_all.65.got_ref = f32[16,40,128]{2,1,0:T(8,128)S(1)} all-to-all(f32[16,40,128]{2,1,0:T(8,128)S(1)} %shard_map.89), channel_id=1, replica_groups={{0,32,64,96,128,160,192,224,256,288,320,352,384,416,448,480},{2,34,66,9..., dimensions={0} | all-to-all | bytes 655360 | tf_op jit(solution)/shard_map/all_to_all | solution.py:223
  198.7 0.7 shard_map.90
  199.3 7.6 %all-to-all-start.11 = ((f32[32,8,128]{2,1,0:T(8,128)}), f32[32,8,128]{2,1,0:T(8,128)S(1)}, u32[]{:S(2)}, u32[]{:S(2)}) async-start(f32[32,8,128]{2,1,0:T(8,128)} %get-tuple-element.142), calls=%async_computation.11 | async-start | bytes 262144 | tf_op jit(solution)/shard_map/all_to_all | solution.py:225
  206.9 3.6 %all-gather.16 = f32[80,128]{1,0:T(8,128)S(1)} all-gather(f32[40,128]{1,0:T(8,128)S(1)} %get-tuple-element.136), channel_id=18, replica_groups={{0,32},{1,33},{2,34},{3,35},{4,36},{5,37},{6,38},{7,39},{8,40},{9,41},{..., dimensions={0}, use_global_device_ids=true | all-gather | bytes 61440 | tf_op jit(solution)/shard_map/all_gather | solution.py:226
  210.5 2.7 %all-gather.17 = f32[4,40,128]{2,1,0:T(8,128)S(1)} all-gather(f32[2,40,128]{2,1,0:T(8,128)S(1)} %bitcast.39), channel_id=19, replica_groups=mesh['x_hi'=2,'z'=8,'core'=2,'y'=8,'x_lo'=2] {'core'}, dimensions={0}, use_global_device_ids=true | all-gather | bytes 122880 | tf_op jit(solution)/shard_map/all_gather | solution.py:227
  213.3 1.0 shard_map.91
  214.3 2.0 all-to-all-done.11.ring_ref
  216.3 0.8 shard_map.92
  (6 shorter events, 0.1 us)
Async XLA Ops:
  0.6 1.2 copy-start
  1.9 0.8 copy-start.1
  1.9 0.8 copy-start.2
  2.4 0.7 copy-start.3
  23.7 24.2 %all-to-all-start.1 = ((f32[32,8,128]{2,1,0:T(8,128)}), f32[32,8,128]{2,1,0:T(8,128)S(1)}, u32[]{:S(2)}, u32[]{:S(2)}) async-start(f32[32,8,128]{2,1,0:T(8,128)} %get-tuple-element.78), calls=%async_computation.1 | async-start | bytes 262144 | tf_op jit(solution)/shard_map/all_to_all | solution.py:225
  64.7 17.0 %all-to-all-start.3 = ((f32[32,8,128]{2,1,0:T(8,128)}), f32[32,8,128]{2,1,0:T(8,128)S(1)}, u32[]{:S(2)}, u32[]{:S(2)}) async-start(f32[32,8,128]{2,1,0:T(8,128)} %get-tuple-element.88), calls=%async_computation.3 | async-start | bytes 262144 | tf_op jit(solution)/shard_map/all_to_all | solution.py:225
  98.3 17.0 %all-to-all-start.5 = ((f32[32,8,128]{2,1,0:T(8,128)}), f32[32,8,128]{2,1,0:T(8,128)S(1)}, u32[]{:S(2)}, u32[]{:S(2)}) async-start(f32[32,8,128]{2,1,0:T(8,128)} %get-tuple-element.100), calls=%async_computation.5 | async-start | bytes 262144 | tf_op jit(solution)/shard_map/all_to_all | solution.py:225
  132.0 17.0 %all-to-all-start.7 = ((f32[32,8,128]{2,1,0:T(8,128)}), f32[32,8,128]{2,1,0:T(8,128)S(1)}, u32[]{:S(2)}, u32[]{:S(2)}) async-start(f32[32,8,128]{2,1,0:T(8,128)} %get-tuple-element.112), calls=%async_computation.7 | async-start | bytes 262144 | tf_op jit(solution)/shard_map/all_to_all | solution.py:225
  165.7 17.0 %all-to-all-start.9 = ((f32[32,8,128]{2,1,0:T(8,128)}), f32[32,8,128]{2,1,0:T(8,128)S(1)}, u32[]{:S(2)}, u32[]{:S(2)}) async-start(f32[32,8,128]{2,1,0:T(8,128)} %get-tuple-element.124), calls=%async_computation.9 | async-start | bytes 262144 | tf_op jit(solution)/shard_map/all_to_all | solution.py:225
  199.3 17.0 %all-to-all-start.11 = ((f32[32,8,128]{2,1,0:T(8,128)}), f32[32,8,128]{2,1,0:T(8,128)S(1)}, u32[]{:S(2)}, u32[]{:S(2)}) async-start(f32[32,8,128]{2,1,0:T(8,128)} %get-tuple-element.142), calls=%async_computation.11 | async-start | bytes 262144 | tf_op jit(solution)/shard_map/all_to_all | solution.py:225

commit v11 on v10

--- a/solution.py
+++ b/solution.py
@@ -128,20 +128,11 @@
     size = out_ref.shape[0]
     tiles = [jnp.where(lane < 64, pltpu.roll(gram, 64, 1) if h else gram, part_c) for h in range(2)]
 
-    def write(slots):
-        for h in range(2):
-            for n in slots[h]:
-                out_ref[n, 0:16] = low[16 * h : 16 * h + 16]
-                out_ref[n, 16:32] = high[16 * h : 16 * h + 16]
-                out_ref[n, 32:40] = tiles[h]
-
-    @pl.when(first)
-    def _():
-        write([range(0, size, 2), range(1, size, 2)])
-
-    @pl.when(jnp.logical_not(first))
-    def _():
-        write([range(size // 2), range(size // 2, size)])
+    for h in range(2):
+        for n in range(h * size // 2, (h + 1) * size // 2):
+            out_ref[n, 0:16] = low[16 * h : 16 * h + 16]
+            out_ref[n, 16:32] = high[16 * h : 16 * h + 16]
+            out_ref[n, 32:40] = tiles[h]
 
 
 def ring_kernel(got_ref, sum_ref, ring_ref):
@@ -204,7 +195,7 @@
         return (((x_hi * size_z + z) * 2 + core) * size_y + y) * 2 + x_lo
 
     two, zs, ys = (range(2), range(size_z), range(size_y))
-    rings = [[at(h, z, 0, y, l) for h in two for z in zs] for l in two for y in ys]
+    rings = [[at(h, z, 0, y, l) for p in two for h in two for z in zs[p::2]] for l in two for y in ys]
     rings += [[at(h, z, 1, y, l) for l in two for y in ys] for h in two for z in zs]
     pairs = [[at(h, z, 0, y, l), at(h, z + 1, 0, y, l)] for h in two for z in zs[::2] for y in ys for l in two]
     pairs += [[at(h, z, 1, y, l) for l in two] for z in zs for y in ys for h in two]

time: 218 us -> 218 us (level)
  blocking collectives: 136 us -> 139 us
where the time goes in v11:
time: 218 us; the launch traced here: 217 us
  blocking collectives  139 us (64%)
  starting transfers between devices  51.5 us (24%)
  Pallas kernels  13.5 us (6%)
  waiting for transfers between devices  10.5 us (5%)
    all_to_all x6, blocking collectives, shards(): got = lax.all_to_all(sent, ALL, 0, 0, axis_index_groups=rings)  79.8 us
    all_to_all x6, starting transfers between devices, shards(): ring = lax.all_to_all(ring, ('core', 'y', 'x_lo'), 0, 0)  51.5 us
    all_gather x6, blocking collectives, shards(): both = lax.all_gather(sums, ALL, axis_index_groups=pairs)  21.6 us
    all_gather x6, blocking collectives, shards(): both = lax.all_gather(sent, 'core')  19.3 us
    all_gather x6, blocking collectives, shards(): both = lax.all_gather(both, 'core')  18.3 us
    pallas_call x26, Pallas kernels, call(): pl.pallas_call(kernel, out_shape=shapes, in_specs=specs, out_specs=[VMEM]...  13.5 us
    all_to_all x6, waiting for transfers between devices, shards(): ring = lax.all_to_all(ring, ('core', 'y', 'x_lo'), 0, 0)  10.5 us
  transfers between devices with their start and end apart: 6, of which 6 were waited for; matrix products, arithmetic and copies ran while one was open for 0% of the time, Pallas kernels for 3%

profile of v11, /device:TPU:1, one launch (start us, length us, event | category | flops | bytes accessed | tf_op | source)
XLA Modules:
  0.0 217.3 jit_solution(4530319352502932008)
XLA Ops:
  0.6 1.2 copy-done
  1.9 0.6 shard_map.67
  2.4 0.2 copy-done.1
  2.6 0.5 copy-done.3
  3.1 0.6 shard_map.68
  3.8 8.4 %all-gather = f32[224,128]{1,0:T(8,128)S(1)} all-gather(f32[112,128]{1,0:T(8,128)S(1)} %get-tuple-element.76), channel_id=2, replica_groups=mesh['x_hi'=2,'z'=8,'core'=2,'y'=8,'x_lo'=2] {'core'}, dimensions={0}, use_global_device_ids=true | all-gather | bytes 172032 | tf_op jit(solution)/shard_map/all_gather | solution.py:212
  12.2 0.1 shard_map.69
  12.3 10.8 %all_to_all.60.got_ref = f32[16,40,128]{2,1,0:T(8,128)S(1)} all-to-all(f32[16,40,128]{2,1,0:T(8,128)S(1)} %shard_map.69), channel_id=1, replica_groups={{0,64,128,192,256,320,384,448,32,96,160,224,288,352,416,480},{2,66,130,..., dimensions={0} | all-to-all | bytes 655360 | tf_op jit(solution)/shard_map/all_to_all | solution.py:214
  23.0 0.7 shard_map.70
  23.7 15.0 %all-to-all-start.1 = ((f32[32,8,128]{2,1,0:T(8,128)}), f32[32,8,128]{2,1,0:T(8,128)S(1)}, u32[]{:S(2)}, u32[]{:S(2)}) async-start(f32[32,8,128]{2,1,0:T(8,128)} %get-tuple-element.78), calls=%async_computation.1 | async-start | bytes 262144 | tf_op jit(solution)/shard_map/all_to_all | solution.py:216
  38.7 3.6 %all-gather.1 = f32[80,128]{1,0:T(8,128)S(1)} all-gather(f32[40,128]{1,0:T(8,128)S(1)} %get-tuple-element.79), channel_id=3, replica_groups={{0,32},{1,33},{2,34},{3,35},{4,36},{5,37},{6,38},{7,39},{8,40},{9,41},{..., dimensions={0}, use_global_device_ids=true | all-gather | bytes 61440 | tf_op jit(solution)/shard_map/all_gather | solution.py:217
  42.3 3.1 %all-gather.2 = f32[4,40,128]{2,1,0:T(8,128)S(1)} all-gather(f32[2,40,128]{2,1,0:T(8,128)S(1)} %bitcast.34), channel_id=4, replica_groups=mesh['x_hi'=2,'z'=8,'core'=2,'y'=8,'x_lo'=2] {'core'}, dimensions={0}, use_global_device_ids=true | all-gather | bytes 122880 | tf_op jit(solution)/shard_map/all_gather | solution.py:218
  45.4 0.9 shard_map.71
  46.4 1.7 all-to-all-done.1.ring_ref
  48.1 0.3 shard_map.72
  48.4 2.2 %all-gather.3 = f32[224,128]{1,0:T(8,128)S(1)} all-gather(f32[112,128]{1,0:T(8,128)S(1)} %get-tuple-element.86), channel_id=5, replica_groups=mesh['x_hi'=2,'z'=8,'core'=2,'y'=8,'x_lo'=2] {'core'}, dimensions={0}, use_global_device_ids=true | all-gather | bytes 172032 | tf_op jit(solution)/shard_map/all_gather | solution.py:212
  50.5 0.1 shard_map.73
  50.6 13.8 %all_to_all.61.got_ref = f32[16,40,128]{2,1,0:T(8,128)S(1)} all-to-all(f32[16,40,128]{2,1,0:T(8,128)S(1)} %shard_map.73), channel_id=1, replica_groups={{0,64,128,192,256,320,384,448,32,96,160,224,288,352,416,480},{2,66,130,..., dimensions={0} | all-to-all | bytes 655360 | tf_op jit(solution)/shard_map/all_to_all | solution.py:214
  64.5 0.7 shard_map.74
  65.1 7.3 %all-to-all-start.3 = ((f32[32,8,128]{2,1,0:T(8,128)}), f32[32,8,128]{2,1,0:T(8,128)S(1)}, u32[]{:S(2)}, u32[]{:S(2)}) async-start(f32[32,8,128]{2,1,0:T(8,128)} %get-tuple-element.88), calls=%async_computation.3 | async-start | bytes 262144 | tf_op jit(solution)/shard_map/all_to_all | solution.py:216
  72.4 3.6 %all-gather.4 = f32[80,128]{1,0:T(8,128)S(1)} all-gather(f32[40,128]{1,0:T(8,128)S(1)} %get-tuple-element.89), channel_id=6, replica_groups={{0,32},{1,33},{2,34},{3,35},{4,36},{5,37},{6,38},{7,39},{8,40},{9,41},{..., dimensions={0}, use_global_device_ids=true | all-gather | bytes 61440 | tf_op jit(solution)/shard_map/all_gather | solution.py:217
  76.0 3.1 %all-gather.5 = f32[4,40,128]{2,1,0:T(8,128)S(1)} all-gather(f32[2,40,128]{2,1,0:T(8,128)S(1)} %bitcast.35), channel_id=7, replica_groups=mesh['x_hi'=2,'z'=8,'core'=2,'y'=8,'x_lo'=2] {'core'}, dimensions={0}, use_global_device_ids=true | all-gather | bytes 122880 | tf_op jit(solution)/shard_map/all_gather | solution.py:218
  79.1 0.9 shard_map.75
  80.0 1.8 all-to-all-done.3.ring_ref
  81.8 0.3 shard_map.76
  82.1 2.2 %all-gather.6 = f32[224,128]{1,0:T(8,128)S(1)} all-gather(f32[112,128]{1,0:T(8,128)S(1)} %get-tuple-element.98), channel_id=8, replica_groups=mesh['x_hi'=2,'z'=8,'core'=2,'y'=8,'x_lo'=2] {'core'}, dimensions={0}, use_global_device_ids=true | all-gather | bytes 172032 | tf_op jit(solution)/shard_map/all_gather | solution.py:212
  84.2 0.1 shard_map.77
  84.3 13.8 %all_to_all.62.got_ref = f32[16,40,128]{2,1,0:T(8,128)S(1)} all-to-all(f32[16,40,128]{2,1,0:T(8,128)S(1)} %shard_map.77), channel_id=1, replica_groups={{0,64,128,192,256,320,384,448,32,96,160,224,288,352,416,480},{2,66,130,..., dimensions={0} | all-to-all | bytes 655360 | tf_op jit(solution)/shard_map/all_to_all | solution.py:214
  98.1 0.7 shard_map.78
  98.8 7.3 %all-to-all-start.5 = ((f32[32,8,128]{2,1,0:T(8,128)}), f32[32,8,128]{2,1,0:T(8,128)S(1)}, u32[]{:S(2)}, u32[]{:S(2)}) async-start(f32[32,8,128]{2,1,0:T(8,128)} %get-tuple-element.100), calls=%async_computation.5 | async-start | bytes 262144 | tf_op jit(solution)/shard_map/all_to_all | solution.py:216
  106.1 3.6 %all-gather.7 = f32[80,128]{1,0:T(8,128)S(1)} all-gather(f32[40,128]{1,0:T(8,128)S(1)} %get-tuple-element.101), channel_id=9, replica_groups={{0,32},{1,33},{2,34},{3,35},{4,36},{5,37},{6,38},{7,39},{8,40},{9,41},{..., dimensions={0}, use_global_device_ids=true | all-gather | bytes 61440 | tf_op jit(solution)/shard_map/all_gather | solution.py:217
  109.7 3.1 %all-gather.8 = f32[4,40,128]{2,1,0:T(8,128)S(1)} all-gather(f32[2,40,128]{2,1,0:T(8,128)S(1)} %bitcast.36), channel_id=10, replica_groups=mesh['x_hi'=2,'z'=8,'core'=2,'y'=8,'x_lo'=2] {'core'}, dimensions={0}, use_global_device_ids=true | all-gather | bytes 122880 | tf_op jit(solution)/shard_map/all_gather | solution.py:218
  112.8 0.9 shard_map.79
  113.7 1.8 all-to-all-done.5.ring_ref
  115.5 0.3 shard_map.80
  115.7 2.2 %all-gather.9 = f32[224,128]{1,0:T(8,128)S(1)} all-gather(f32[112,128]{1,0:T(8,128)S(1)} %get-tuple-element.110), channel_id=11, replica_groups=mesh['x_hi'=2,'z'=8,'core'=2,'y'=8,'x_lo'=2] {'core'}, dimensions={0}, use_global_device_ids=true | all-gather | bytes 172032 | tf_op jit(solution)/shard_map/all_gather | solution.py:212
  117.9 0.1 shard_map.81
  118.0 13.8 %all_to_all.63.got_ref = f32[16,40,128]{2,1,0:T(8,128)S(1)} all-to-all(f32[16,40,128]{2,1,0:T(8,128)S(1)} %shard_map.81), channel_id=1, replica_groups={{0,64,128,192,256,320,384,448,32,96,160,224,288,352,416,480},{2,66,130,..., dimensions={0} | all-to-all | bytes 655360 | tf_op jit(solution)/shard_map/all_to_all | solution.py:214
  131.8 0.7 shard_map.82
  132.5 7.3 %all-to-all-start.7 = ((f32[32,8,128]{2,1,0:T(8,128)}), f32[32,8,128]{2,1,0:T(8,128)S(1)}, u32[]{:S(2)}, u32[]{:S(2)}) async-start(f32[32,8,128]{2,1,0:T(8,128)} %get-tuple-element.112), calls=%async_computation.7 | async-start | bytes 262144 | tf_op jit(solution)/shard_map/all_to_all | solution.py:216
  139.8 3.6 %all-gather.10 = f32[80,128]{1,0:T(8,128)S(1)} all-gather(f32[40,128]{1,0:T(8,128)S(1)} %get-tuple-element.113), channel_id=12, replica_groups={{0,32},{1,33},{2,34},{3,35},{4,36},{5,37},{6,38},{7,39},{8,40},{9,41},{..., dimensions={0}, use_global_device_ids=true | all-gather | bytes 61440 | tf_op jit(solution)/shard_map/all_gather | solution.py:217
  143.4 3.1 %all-gather.11 = f32[4,40,128]{2,1,0:T(8,128)S(1)} all-gather(f32[2,40,128]{2,1,0:T(8,128)S(1)} %bitcast.37), channel_id=13, replica_groups=mesh['x_hi'=2,'z'=8,'core'=2,'y'=8,'x_lo'=2] {'core'}, dimensions={0}, use_global_device_ids=true | all-gather | bytes 122880 | tf_op jit(solution)/shard_map/all_gather | solution.py:218
  146.4 0.9 shard_map.83
  147.3 1.8 all-to-all-done.7.ring_ref
  149.1 0.3 shard_map.84
  149.4 2.2 %all-gather.12 = f32[224,128]{1,0:T(8,128)S(1)} all-gather(f32[112,128]{1,0:T(8,128)S(1)} %get-tuple-element.122), channel_id=14, replica_groups=mesh['x_hi'=2,'z'=8,'core'=2,'y'=8,'x_lo'=2] {'core'}, dimensions={0}, use_global_device_ids=true | all-gather | bytes 172032 | tf_op jit(solution)/shard_map/all_gather | solution.py:212
  151.6 0.1 shard_map.85
  151.7 13.8 %all_to_all.64.got_ref = f32[16,40,128]{2,1,0:T(8,128)S(1)} all-to-all(f32[16,40,128]{2,1,0:T(8,128)S(1)} %shard_map.85), channel_id=1, replica_groups={{0,64,128,192,256,320,384,448,32,96,160,224,288,352,416,480},{2,66,130,..., dimensions={0} | all-to-all | bytes 655360 | tf_op jit(solution)/shard_map/all_to_all | solution.py:214
  165.5 0.7 shard_map.86
  166.1 7.3 %all-to-all-start.9 = ((f32[32,8,128]{2,1,0:T(8,128)}), f32[32,8,128]{2,1,0:T(8,128)S(1)}, u32[]{:S(2)}, u32[]{:S(2)}) async-start(f32[32,8,128]{2,1,0:T(8,128)} %get-tuple-element.124), calls=%async_computation.9 | async-start | bytes 262144 | tf_op jit(solution)/shard_map/all_to_all | solution.py:216
  173.4 3.6 %all-gather.13 = f32[80,128]{1,0:T(8,128)S(1)} all-gather(f32[40,128]{1,0:T(8,128)S(1)} %get-tuple-element.125), channel_id=15, replica_groups={{0,32},{1,33},{2,34},{3,35},{4,36},{5,37},{6,38},{7,39},{8,40},{9,41},{..., dimensions={0}, use_global_device_ids=true | all-gather | bytes 61440 | tf_op jit(solution)/shard_map/all_gather | solution.py:217
  177.0 3.0 %all-gather.14 = f32[4,40,128]{2,1,0:T(8,128)S(1)} all-gather(f32[2,40,128]{2,1,0:T(8,128)S(1)} %bitcast.38), channel_id=16, replica_groups=mesh['x_hi'=2,'z'=8,'core'=2,'y'=8,'x_lo'=2] {'core'}, dimensions={0}, use_global_device_ids=true | all-gather | bytes 122880 | tf_op jit(solution)/shard_map/all_gather | solution.py:218
  180.1 0.9 shard_map.87
  181.0 1.8 all-to-all-done.9.ring_ref
  182.8 0.3 shard_map.88
  183.1 2.2 %all-gather.15 = f32[224,128]{1,0:T(8,128)S(1)} all-gather(f32[112,128]{1,0:T(8,128)S(1)} %get-tuple-element.134), channel_id=17, replica_groups=mesh['x_hi'=2,'z'=8,'core'=2,'y'=8,'x_lo'=2] {'core'}, dimensions={0}, use_global_device_ids=true | all-gather | bytes 172032 | tf_op jit(solution)/shard_map/all_gather | solution.py:212
  185.3 13.8 %all_to_all.65.got_ref = f32[16,40,128]{2,1,0:T(8,128)S(1)} all-to-all(f32[16,40,128]{2,1,0:T(8,128)S(1)} %shard_map.89), channel_id=1, replica_groups={{0,64,128,192,256,320,384,448,32,96,160,224,288,352,416,480},{2,66,130,..., dimensions={0} | all-to-all | bytes 655360 | tf_op jit(solution)/shard_map/all_to_all | solution.py:214
  199.1 0.7 shard_map.90
  199.8 7.3 %all-to-all-start.11 = ((f32[32,8,128]{2,1,0:T(8,128)}), f32[32,8,128]{2,1,0:T(8,128)S(1)}, u32[]{:S(2)}, u32[]{:S(2)}) async-start(f32[32,8,128]{2,1,0:T(8,128)} %get-tuple-element.142), calls=%async_computation.11 | async-start | bytes 262144 | tf_op jit(solution)/shard_map/all_to_all | solution.py:216
  207.1 3.6 %all-gather.16 = f32[80,128]{1,0:T(8,128)S(1)} all-gather(f32[40,128]{1,0:T(8,128)S(1)} %get-tuple-element.136), channel_id=18, replica_groups={{0,32},{1,33},{2,34},{3,35},{4,36},{5,37},{6,38},{7,39},{8,40},{9,41},{..., dimensions={0}, use_global_device_ids=true | all-gather | bytes 61440 | tf_op jit(solution)/shard_map/all_gather | solution.py:217
  210.7 3.0 %all-gather.17 = f32[4,40,128]{2,1,0:T(8,128)S(1)} all-gather(f32[2,40,128]{2,1,0:T(8,128)S(1)} %bitcast.39), channel_id=19, replica_groups=mesh['x_hi'=2,'z'=8,'core'=2,'y'=8,'x_lo'=2] {'core'}, dimensions={0}, use_global_device_ids=true | all-gather | bytes 122880 | tf_op jit(solution)/shard_map/all_gather | solution.py:218
  213.8 1.0 shard_map.91
  214.8 1.7 all-to-all-done.11.ring_ref
  216.5 0.8 shard_map.92
  (6 shorter events, 0.1 us)
Async XLA Ops:
  0.6 1.2 copy-start
  1.9 0.8 copy-start.1
  1.9 0.8 copy-start.2
  2.4 0.7 copy-start.3
  23.7 24.4 %all-to-all-start.1 = ((f32[32,8,128]{2,1,0:T(8,128)}), f32[32,8,128]{2,1,0:T(8,128)S(1)}, u32[]{:S(2)}, u32[]{:S(2)}) async-start(f32[32,8,128]{2,1,0:T(8,128)} %get-tuple-element.78), calls=%async_computation.1 | async-start | bytes 262144 | tf_op jit(solution)/shard_map/all_to_all | solution.py:216
  65.1 16.7 %all-to-all-start.3 = ((f32[32,8,128]{2,1,0:T(8,128)}), f32[32,8,128]{2,1,0:T(8,128)S(1)}, u32[]{:S(2)}, u32[]{:S(2)}) async-start(f32[32,8,128]{2,1,0:T(8,128)} %get-tuple-element.88), calls=%async_computation.3 | async-start | bytes 262144 | tf_op jit(solution)/shard_map/all_to_all | solution.py:216
  98.8 16.7 %all-to-all-start.5 = ((f32[32,8,128]{2,1,0:T(8,128)}), f32[32,8,128]{2,1,0:T(8,128)S(1)}, u32[]{:S(2)}, u32[]{:S(2)}) async-start(f32[32,8,128]{2,1,0:T(8,128)} %get-tuple-element.100), calls=%async_computation.5 | async-start | bytes 262144 | tf_op jit(solution)/shard_map/all_to_all | solution.py:216
  132.5 16.7 %all-to-all-start.7 = ((f32[32,8,128]{2,1,0:T(8,128)}), f32[32,8,128]{2,1,0:T(8,128)S(1)}, u32[]{:S(2)}, u32[]{:S(2)}) async-start(f32[32,8,128]{2,1,0:T(8,128)} %get-tuple-element.112), calls=%async_computation.7 | async-start | bytes 262144 | tf_op jit(solution)/shard_map/all_to_all | solution.py:216
  166.1 16.7 %all-to-all-start.9 = ((f32[32,8,128]{2,1,0:T(8,128)}), f32[32,8,128]{2,1,0:T(8,128)S(1)}, u32[]{:S(2)}, u32[]{:S(2)}) async-start(f32[32,8,128]{2,1,0:T(8,128)} %get-tuple-element.124), calls=%async_computation.9 | async-start | bytes 262144 | tf_op jit(solution)/shard_map/all_to_all | solution.py:216
  199.8 16.7 %all-to-all-start.11 = ((f32[32,8,128]{2,1,0:T(8,128)}), f32[32,8,128]{2,1,0:T(8,128)S(1)}, u32[]{:S(2)}, u32[]{:S(2)}) async-start(f32[32,8,128]{2,1,0:T(8,128)} %get-tuple-element.142), calls=%async_computation.11 | async-start | bytes 262144 | tf_op jit(solution)/shard_map/all_to_all | solution.py:216
